TPU v7x, 128 devices: a whole 4x4x4 slice. The times are simulated.
128 devices in a mesh: dp: 64 (over z, y, x_lo, core), mp: 2 (over x_hi).
Axes of the slice: x: 4 (x_hi: 2, x_lo: 2; x = x_hi * 2 + x_lo), y: 4, z: 4, core: 2. Of those that a mesh axis runs over, the one named last changes fastest.
Arguments:
- grad_parts: bfloat16 [64, 1, 7168, 1024], P('dp', None, 'mp'), may hold values from -850.5 to 850.5
- master: float32 [1, 2, 3584, 1024], P(None, 'mp', 'dp'), may hold values from -3 to 3
- momentum: float32 [1, 2, 3584, 1024], P(None, 'mp', 'dp'), may hold values from -1.5 to 1.5
Outputs:
- new_weights: bfloat16 [1, 7168, 1024], P(None, 'mp')
- new_momentum: float32 [1, 2, 3584, 1024], P(None, 'mp', 'dp')
- new_master: float32 [1, 2, 3584, 1024], P(None, 'mp', 'dp')
- update: float32 [1, 2, 3584, 1024], P(None, 'mp', 'dp')
All inputs are finite; a program needn't handle non-finite values.
Results may differ from a plain program's by a relative error of at most 0.001.
Values may be sent and summed in bfloat16 or wider, within the bound.
No kernel may reach another device: no remote copies, remote signals or barrier semaphores. Data moves between devices by JAX's collectives and lax.ppermute only.
A program may use at most 128 MiB of HBM per device.

v0:
```python
import jax
import jax.numpy as jnp
from jax import lax
from jax.sharding import PartitionSpec as P

D = 7168
H = 1024
ITERS = 3


beta_rate = 0.95
learn_rate = 0.02
decay_rate = 0.1
small_eps = 1e-07
coef_first = 3.4445
coef_second = -4.775
coef_third = 2.0315


def local_gram(scaled):
    return jnp.einsum("erh,erk->ehk", scaled, scaled, precision=lax.Precision.HIGHEST)


def summed_gram(scaled):
    partial_gram = local_gram(scaled)
    return lax.psum(partial_gram, ("dp", "mp"))


def newton_step(scaled, gram):
    square = jnp.einsum("ehk,ekl->ehl", gram, gram, precision=lax.Precision.HIGHEST)
    mixed = coef_second * gram + coef_third * square
    return coef_first * scaled + jnp.einsum(
        "erh,ehk->erk", scaled, mixed, precision=lax.Precision.HIGHEST
    )


def shards(grad_parts, master, momentum):
    local_terms = grad_parts[0].astype(jnp.float32)
    summed_grad = lax.psum_scatter(local_terms, "dp", scatter_dimension=1, tiled=True)
    expert_count = summed_grad.shape[0]
    row_count = summed_grad.shape[1]
    unit_count = summed_grad.shape[2]
    old_master = master.reshape(expert_count, row_count, unit_count)
    old_momentum = momentum.reshape(expert_count, row_count, unit_count)
    new_momentum = beta_rate * old_momentum + summed_grad
    direction = summed_grad + beta_rate * new_momentum
    squares = lax.psum(jnp.sum(direction * direction, axis=(1, 2)), ("dp", "mp"))
    scaled = direction / (jnp.sqrt(squares) + small_eps)[:, None, None]
    gram = summed_gram(scaled)
    for step in range(ITERS):
        scaled = newton_step(scaled, gram)
        if step + 1 < ITERS:
            gram = summed_gram(scaled)
    factor = 0.2 * max(D, H) ** 0.5
    update = factor * scaled
    new_master = old_master * (1.0 - learn_rate * decay_rate) - learn_rate * update
    weight_rows = new_master.astype(jnp.bfloat16)
    new_weights = lax.all_gather(weight_rows, "dp", axis=1, tiled=True)
    return (
        new_weights,
        new_momentum.reshape(momentum.shape),
        new_master.reshape(master.shape),
        update.reshape(master.shape),
    )


def solution(mesh):
    placed = (P("dp", None, "mp", None), P(None, "mp", "dp", None), P(None, "mp", "dp", None))
    return jax.shard_map(
        shards,
        mesh=mesh,
        in_specs=placed,
        out_specs=(
            P(None, "mp", None),
            P(None, "mp", "dp", None),
            P(None, "mp", "dp", None),
            P(None, "mp", "dp", None),
        ),
        check_vma=False,
    )
```

profile of v0, /device:TPU:1, one launch (start us, length us, event | category | flops | bytes accessed | tf_op | source)
XLA Modules:
  0.0 1054.6 jit_solution(5955550946987885013)
XLA Ops:
  7.2 0.0 reduce-scatter.2.cloned.1.call-start
  7.2 10.1 bitcast_convert_fusion
  17.4 0.0 copy-start.3
  17.4 0.0 reduce-scatter.2.cloned.1.call-update
  17.4 0.0 all-reduce.4.cloned.1.call-start
  17.4 309.7 %reduce-scatter.2.cloned.1.call-done = f32[1,56,1024]{2,1,0:T(8,128)} async-done(((f32[1,3584,1024]{2,1,0:T(8,128)}), f32[1,56,1024]{2,1,0:T(8,128)}) %reduce-scatter.2.cloned.1.call-update) | async-done | bytes 229392 | tf_op jit(solution)/shard_map/reduce_scatter | solution.py:39
  327.1 0.0 copy-done.3
  327.1 2.3 fusion.48
  329.4 66.9 %psum.28 = f32[1]{0:T(128)} all-reduce(f32[1]{0:T(128)} %bitcast.3), channel_id=1, replica_groups=mesh['dp'=64,'mp'=2] {'dp','mp'}, use_global_device_ids=true, to_apply=%region_2.0 | all-reduce | flops 1 | bytes 8 | tf_op jit(solution)/shard_map/psum | solution.py:47
  397.0 6.5 convolution_bitcast_fusion.2
  403.5 0.0 all-reduce.4.cloned.1.call-update
  403.6 0.0 copy-start.4
  403.6 0.2 all-reduce.6.cloned.1.call-start
  403.8 150.6 %all-reduce.4.cloned.1.call-done = f32[1,1024,1024]{2,1,0:T(8,128)} async-done(((f32[1,1024,1024]{2,1,0:T(8,128)}), f32[1,1024,1024]{2,1,0:T(8,128)}) %all-reduce.4.cloned.1.call-update) | async-done | bytes 4194320 | tf_op jit(solution)/shard_map/psum | solution.py:26
  554.4 0.0 copy-start
  554.4 17.3 %fusion.10 = f32[1024,1024]{1,0:T(8,128)S(1)} fusion(f32[1,1024,1024]{2,1,0:T(8,128)} %all-reduce.4.cloned.1.call-done), kind=kOutput, calls=%fused_computation.14 | convolution fusion | flops 12884901888 | bytes 8388608 | tf_op jit(solution)/shard_map/ehk,ekl->ehl/dot_general | solution.py:30
  571.7 0.0 copy-done.4
  571.7 0.0 copy-done
  571.7 3.1 fusion.39
  574.9 5.0 convolution_bitcast_fusion.1
  579.9 0.0 all-reduce.6.cloned.1.call-update
  579.9 0.3 all-reduce.8.cloned.1.call-start
  580.2 152.4 %all-reduce.6.cloned.1.call-done = f32[1,1024,1024]{2,1,0:T(8,128)} async-done(((f32[1,1024,1024]{2,1,0:T(8,128)}), f32[1,1024,1024]{2,1,0:T(8,128)}) %all-reduce.6.cloned.1.call-update) | async-done | bytes 4194320 | tf_op jit(solution)/shard_map/psum | solution.py:26
  732.6 0.0 copy-start.2
  732.6 17.3 %fusion.6 = f32[1024,1024]{1,0:T(8,128)S(1)} fusion(f32[1,1024,1024]{2,1,0:T(8,128)} %all-reduce.6.cloned.1.call-done), kind=kOutput, calls=%fused_computation.9 | convolution fusion | flops 12884901888 | bytes 8388608 | tf_op jit(solution)/shard_map/ehk,ekl->ehl/dot_general | solution.py:30
  749.9 0.0 copy-done.2
  749.9 3.1 fusion.36
  753.0 5.0 convolution_bitcast_fusion
  758.0 0.0 all-reduce.8.cloned.1.call-update
  758.0 0.0 copy-start.5
  758.1 0.3 all-gather.2.cloned.1.call-start
  758.4 152.4 %all-reduce.8.cloned.1.call-done = f32[1,1024,1024]{2,1,0:T(8,128)} async-done(((f32[1,1024,1024]{2,1,0:T(8,128)}), f32[1,1024,1024]{2,1,0:T(8,128)}) %all-reduce.8.cloned.1.call-update) | async-done | bytes 4194320 | tf_op jit(solution)/shard_map/psum | solution.py:26
  910.8 0.0 copy-start.1
  910.8 17.3 %fusion.2 = f32[1024,1024]{1,0:T(8,128)S(1)} fusion(f32[1,1024,1024]{2,1,0:T(8,128)} %all-reduce.8.cloned.1.call-done), kind=kOutput, calls=%fused_computation.4 | convolution fusion | flops 12884901888 | bytes 8388608 | tf_op jit(solution)/shard_map/ehk,ekl->ehl/dot_general | solution.py:30
  928.1 0.0 copy-done.5
  928.1 0.0 copy-done.1
  928.1 3.9 fusion.49
  932.0 0.0 all-gather.2.cloned.1.call-update
  932.0 109.1 %all-gather.2.cloned.1.call-done = bf16[1,3584,1024]{2,1,0:T(8,128)(2,1)} async-done(((bf16[1,56,1024]{2,1,0:T(8,128)(2,1)}), bf16[1,3584,1024]{2,1,0:T(8,128)(2,1)}) %all-gather.2.cloned.1.call-update) | async-done | bytes 7340048 | tf_op jit(solution)/shard_map/all_gather | solution.py:58
  1041.1 7.0 copy.11
Async XLA Ops:
  7.2 320.0 %reduce-scatter.2.cloned.1.call-start = ((), (), s32[]{:S(2)}) async-start(), calls=%async_computation.1 | async-start | bytes 14909440 | tf_op jit(solution)/shard_map/reduce_scatter | solution.py:39
  17.4 309.8 %copy-start.3 = (f32[1,1,56,1024]{3,2,1,0:T(8,128)S(1)}, f32[1,1,56,1024]{3,2,1,0:T(8,128)}, u32[]{:S(2)}) copy-start(f32[1,1,56,1024]{3,2,1,0:T(8,128)} %param.5) | copy-start | bytes 688132
  17.4 537.0 %all-reduce.4.cloned.1.call-start = ((), (), s32[]{:S(2)}) async-start(), calls=%async_computation.2 | async-start | bytes 8388608 | tf_op jit(solution)/shard_map/psum | solution.py:26
  403.6 168.2 %copy-start.4 = (f32[1,56,1024]{2,1,0:T(8,128)S(1)}, f32[1,56,1024]{2,1,0:T(8,128)}, u32[]{:S(2)}) copy-start(f32[1,56,1024]{2,1,0:T(8,128)} %reduce-scatter.2.cloned.1.call-done) | copy-start | bytes 688132
  403.6 329.0 %all-reduce.6.cloned.1.call-start = ((), (), s32[]{:S(2)}) async-start(), calls=%async_computation.3 | async-start | bytes 8388608 | tf_op jit(solution)/shard_map/psum | solution.py:26
  554.4 17.3 %copy-start = (f32[1,1024,1024]{2,1,0:T(8,128)S(1)}, f32[1,1024,1024]{2,1,0:T(8,128)}, u32[]{:S(2)}) copy-start(f32[1,1024,1024]{2,1,0:T(8,128)} %all-reduce.4.cloned.1.call-done) | copy-start | bytes 12582916
  579.9 330.9 %all-reduce.8.cloned.1.call-start = ((), (), s32[]{:S(2)}) async-start(), calls=%async_computation.4 | async-start | bytes 8388608 | tf_op jit(solution)/shard_map/psum | solution.py:26
  732.6 17.3 %copy-start.2 = (f32[1,1024,1024]{2,1,0:T(8,128)S(1)}, f32[1,1024,1024]{2,1,0:T(8,128)}, u32[]{:S(2)}) copy-start(f32[1,1024,1024]{2,1,0:T(8,128)} %all-reduce.6.cloned.1.call-done) | copy-start | bytes 12582916
  758.0 170.0 %copy-start.5 = (f32[1,1,56,1024]{3,2,1,0:T(8,128)S(1)}, f32[1,1,56,1024]{3,2,1,0:T(8,128)}, u32[]{:S(2)}) copy-start(f32[1,1,56,1024]{3,2,1,0:T(8,128)} %param.4) | copy-start | bytes 688132
  758.1 283.0 %all-gather.2.cloned.1.call-start = ((), (), s32[]{:S(2)}) async-start(), calls=%async_computation.5 | async-start | bytes 7454720 | tf_op jit(solution)/shard_map/all_gather | solution.py:58
  910.8 17.3 %copy-start.1 = (f32[1,1024,1024]{2,1,0:T(8,128)S(1)}, f32[1,1024,1024]{2,1,0:T(8,128)}, u32[]{:S(2)}) copy-start(f32[1,1024,1024]{2,1,0:T(8,128)} %all-reduce.8.cloned.1.call-done) | copy-start | bytes 12582916
Sparse Core Ops, SparseCore 0:
  17.5 309.5 reduce-scatter.1
  403.7 150.6 all-reduce.3
  580.0 152.5 all-reduce.5
  758.2 152.5 all-reduce.7
  932.1 108.8 all-gather.1
where the time goes:
time: 1050 us
  waiting for transfers between devices  874 us (83%)
  matrix products  78.6 us (7%)
  blocking collectives  66.9 us (6%)
  between operations  14.6 us (1%)
  other arithmetic  12.4 us (1%)
    psum x3, waiting for transfers between devices, summed_gram(): return lax.psum(partial_gram, ('dp', 'mp'))  455 us
    reduce_scatter x1, waiting for transfers between devices, shards(): lax.psum_scatter(local_terms, 'dp', scatter_dimension=1, tiled=True)  310 us
    all_gather x1, waiting for transfers between devices, shards(): new_weights = lax.all_gather(weight_rows, 'dp', axis=1, tiled=True)  109 us
    psum x1, blocking collectives, shards(): lax.psum(jnp.sum(direction * direction, axis=(1, 2)), ('dp', 'mp'))  66.9 us
    dot_general x3, matrix products, newton_step(): jnp.einsum('ehk,ekl->ehl', gram, gram, precision=lax.Precision.HIGHEST)  51.9 us
  transfers between devices with their start and end apart: 5, of which 5 were waited for; matrix products, arithmetic and copies ran while one was open for 0% of the time, Pallas kernels for 0%

commit v1 on v0

v1 whole, which is shorter than its diff:
```python
import jax
import jax.numpy as jnp
import numpy as np
from jax import lax
from jax.experimental import pallas as pl
from jax.experimental.pallas import tpu as pltpu
from jax.sharding import Mesh, PartitionSpec as P

D = 7168
H = 1024
ITERS = 3
N_DP = 64
ROWS = 56
BLOCK = 256
UPPER = [(i, j) for i in range(H // BLOCK) for j in range(i, H // BLOCK)]
PACKED = len(UPPER) * BLOCK * BLOCK // 128

beta_rate = 0.95
learn_rate = 0.02
decay_rate = 0.1
small_eps = 1e-07
coef_first = 3.4445
coef_second = -4.775
coef_third = 2.0315

f32 = jnp.float32
bf16 = jnp.bfloat16
CHIPS = ("z", "y", "xl", "xh")
DP = ("z", "y", "xl", "c")


def split(x):
    hi = x.astype(bf16)
    return hi, (x - hi.astype(f32)).astype(bf16)


def dot(a, b):
    return jnp.dot(a, b, preferred_element_type=f32)


STEP = 8


def gram_kernel(parts, momentum, new_momentum, direction, gram, total):
    step = pl.program_id(0)
    piece = parts[0].astype(f32)
    for i in range(1, STEP):
        piece += parts[i].astype(f32)

    @pl.when(step == 0)
    def _():
        total[...] = piece

    @pl.when(step > 0)
    def _():
        total[...] += piece

    @pl.when(step == N_DP // STEP - 1)
    def _():
        grad = total[...]
        moved = beta_rate * momentum[...] + grad
        new_momentum[...] = moved
        direct = grad + beta_rate * moved
        direction[...] = direct
        hi, lo = split(direct)
        left = jnp.concatenate([hi, lo, hi, lo], axis=0).T
        right = jnp.concatenate([hi, hi, lo, lo], axis=0)
        place = 0
        for i in range(H // BLOCK):
            wide = dot(left[i * BLOCK : (i + 1) * BLOCK], right[:, i * BLOCK :])
            for j in range((H // BLOCK - i) * BLOCK // 128):
                gram[pl.ds(place, BLOCK), :] = wide[:, j * 128 : (j + 1) * 128]
                place += BLOCK


def sum_and_gram(parts, momentum):
    row = pl.BlockSpec((ROWS, H), lambda i: (0, 0))
    return pl.pallas_call(
        gram_kernel,
        grid=(N_DP // STEP,),
        in_specs=[pl.BlockSpec((STEP, ROWS, H), lambda i: (i, 0, 0)), row],
        out_specs=[row, row, pl.BlockSpec((PACKED, 128), lambda i: (0, 0))],
        out_shape=[
            jax.ShapeDtypeStruct((ROWS, H), f32),
            jax.ShapeDtypeStruct((ROWS, H), f32),
            jax.ShapeDtypeStruct((PACKED, 128), f32),
        ],
        scratch_shapes=[pltpu.VMEM((ROWS, H), f32)],
        compiler_params=pltpu.CompilerParams(vmem_limit_bytes=40 * 2**20),
        name="sum_and_gram",
    )(parts, momentum)


def newton_kernel(packed, direction, master, update, new_master, weights, gram, g_hi, g_lo, p_hi, p_lo):
    n = H // BLOCK
    place = 0
    for i in range(n):
        for j in range(i, n):
            tile = jnp.concatenate(
                [packed[pl.ds(place, BLOCK), :], packed[pl.ds(place + BLOCK, BLOCK), :]], axis=1
            )
            place += 2 * BLOCK
            gram[i * BLOCK : (i + 1) * BLOCK, j * BLOCK : (j + 1) * BLOCK] = tile
            if j > i:
                gram[j * BLOCK : (j + 1) * BLOCK, i * BLOCK : (i + 1) * BLOCK] = tile.T
    rows = lax.broadcasted_iota(jnp.int32, (BLOCK, BLOCK), 0)
    cols = lax.broadcasted_iota(jnp.int32, (BLOCK, BLOCK), 1)
    on = rows == cols
    trace = jnp.zeros((), f32)
    for i in range(n):
        span = slice(i * BLOCK, (i + 1) * BLOCK)
        trace += jnp.sum(jnp.where(on, gram[span, span], 0.0))
    inverse = 1.0 / (jnp.sqrt(jnp.full((1, 1), trace, f32)) + small_eps)

    def full(a_hi, a_lo, b_hi, b_lo, span):
        b = b_hi[...]
        return dot(a_hi[span, :], b) + dot(a_lo[span, :], b) + dot(a_hi[span, :], b_lo[...])

    def thin(x, b_hi, b_lo):
        hi, lo = split(x)
        both = dot(jnp.concatenate([hi, lo], axis=0), b_hi[...])
        return both[:ROWS] + both[ROWS:] + dot(hi, b_lo[...])

    spans = [slice(i * BLOCK, (i + 1) * BLOCK) for i in range(n)]
    wide_rows = lax.broadcasted_iota(jnp.int32, (BLOCK, H), 0)
    wide_cols = lax.broadcasted_iota(jnp.int32, (BLOCK, H), 1)

    def store(value, hi_ref, lo_ref, span):
        hi, lo = split(value)
        hi_ref[span, :] = hi
        lo_ref[span, :] = lo

    for span in spans:
        value = gram[span, :] * inverse * inverse
        gram[span, :] = value
        store(value, g_hi, g_lo, span)
    scaled = direction[...] * inverse
    for step in range(ITERS):
        if step == ITERS - 1:
            first = thin(scaled, g_hi, g_lo)
            second = thin(first, g_hi, g_lo)
            scaled = coef_first * scaled + coef_second * first + coef_third * second
            break
        for i, span in enumerate(spans):
            square = full(g_hi, g_lo, g_hi, g_lo, span)
            poly = coef_second * gram[span, :] + coef_third * square
            poly += jnp.where(wide_rows + i * BLOCK == wide_cols, coef_first, 0.0)
            store(poly, p_hi, p_lo, span)
        scaled = thin(scaled, p_hi, p_lo)
        for span in spans:
            gram[span, :] = full(g_hi, g_lo, p_hi, p_lo, span)
        for span in spans:
            store(gram[span, :], g_hi, g_lo, span)
        for span in spans:
            gram[span, :] = full(g_hi, g_lo, p_hi, p_lo, span)
        for span in spans:
            store(gram[span, :], g_hi, g_lo, span)
    result = (0.2 * max(D, H) ** 0.5) * scaled
    update[...] = result
    moved = master[...] * (1.0 - learn_rate * decay_rate) - learn_rate * result
    new_master[...] = moved
    weights[...] = moved.astype(bf16)


def newton(packed, direction, master):
    whole = pl.BlockSpec(memory_space=pltpu.VMEM)
    return pl.pallas_call(
        newton_kernel,
        in_specs=[whole] * 3,
        out_specs=[whole] * 3,
        out_shape=[
            jax.ShapeDtypeStruct((ROWS, H), f32),
            jax.ShapeDtypeStruct((ROWS, H), f32),
            jax.ShapeDtypeStruct((ROWS, H), bf16),
        ],
        scratch_shapes=[pltpu.VMEM((H, H), f32)] + [pltpu.VMEM((H, H), bf16)] * 4,
        compiler_params=pltpu.CompilerParams(vmem_limit_bytes=56 * 2**20),
        name="newton",
    )(packed, direction, master)


def exchange(x, axes):
    return lax.all_to_all(x, axes, 0, 0, tiled=True)


def swap(x, axis):
    return lax.ppermute(x, axis, [(0, 1), (1, 0)])


def repeat(x, n):
    return jnp.broadcast_to(x[None], (n,) + x.shape)


def summed_gram(gram):
    core = lax.axis_index("c")
    half = PACKED // 2
    given = lax.dynamic_slice(gram, ((1 - core) * half, 0), (half, 128))
    kept = lax.dynamic_slice(gram, (core * half, 0), (half, 128))
    part = kept + swap(given, "c")
    piece = exchange(part.reshape(64, half // 64, 128), CHIPS).sum(0)
    mine = exchange(repeat(piece, 64), CHIPS).reshape(half, 128)
    other = swap(mine, "c")
    return jnp.concatenate([jnp.where(core == 0, mine, other), jnp.where(core == 0, other, mine)], 0)


def gathered(rows):
    core = lax.axis_index("c")
    low = lax.axis_index("xl") == 0
    other = swap(rows, "xl")
    pair = jnp.where(low, jnp.stack([rows, other]), jnp.stack([other, rows]))
    mine = exchange(repeat(pair, 16), ("z", "y"))
    other = swap(mine, "c")
    whole = jnp.where(core == 0, jnp.stack([mine, other], 2), jnp.stack([other, mine], 2))
    return whole.reshape(1, N_DP * ROWS, H)


def shards(grad_parts, master, momentum):
    parts = exchange(grad_parts.reshape(N_DP, ROWS, H), DP)
    new_momentum, direction, gram = sum_and_gram(parts, momentum.reshape(ROWS, H))
    update, new_master, weights = newton(summed_gram(gram), direction, master.reshape(ROWS, H))
    return (
        gathered(weights),
        new_momentum.reshape(momentum.shape),
        new_master.reshape(master.shape),
        update.reshape(master.shape),
    )


def solution(mesh):
    fine = Mesh(mesh.devices.reshape(4, 4, 2, 2, 2), ("z", "y", "xl", "c", "xh"))
    rows = P(None, "xh", DP, None)
    return jax.shard_map(
        shards,
        mesh=fine,
        in_specs=(P(DP, None, "xh", None), rows, rows),
        out_specs=(P(None, "xh", None), rows, rows, rows),
        check_vma=False,
    )
```

time: 1050 us -> 302 us (0.29)
  waiting for transfers between devices: 874 us -> 109 us
  matrix products: 78.6 us -> 0 us
  Pallas kernels: 0 us -> 52.6 us
  blocking collectives: 66.9 us -> 109 us
  starting transfers between devices: 0.87 us -> 16.3 us
  between operations: 14.6 us -> 0.87 us
    psum x3 -> x0, waiting for transfers between devices: 455 us -> none  [summed_gram(): return lax.psum(partial_gram, ('dp', 'mp'))]
    reduce_scatter x1 -> x0, waiting for transfers between devices: 310 us -> none  [shards(): lax.psum_scatter(local_terms, 'dp', scatter_dimension=1, tiled=True)]
    all_to_all x0 -> x3, blocking collectives: none -> 109 us  [exchange(): return lax.all_to_all(x, axes, 0, 0, tiled=True)]
    all_gather x1 -> x0, waiting for transfers between devices: 109 us -> none  [shards(): new_weights = lax.all_gather(weight_rows, 'dp', axis=1, tiled=True)]
    all_to_all x0 -> x1, waiting for transfers between devices: none -> 92.3 us  [exchange(): return lax.all_to_all(x, axes, 0, 0, tiled=True)]
    dot_general x9 -> x0, matrix products: 78.6 us -> none  [the longest x3 51.9 us: newton_step(): jnp.einsum('ehk,ekl->ehl', gram, gram, precision=lax.Precision.HIGHEST)]
    psum x1 -> x0, blocking collectives: 66.9 us -> none  [shards(): lax.psum(jnp.sum(direction * direction, axis=(1, 2)), ('dp', 'mp'))]
    pallas_call x0 -> x2, Pallas kernels: none -> 52.6 us  [the longest x1 45.4 us: newton(): pl.pallas_call(newton_kernel, in_specs=[whole] * 3, out_specs=[whole] * 3...]
where the time goes in v1:
time: 302 us; the launch traced here: 298 us
  waiting for transfers between devices  109 us (36%)
  blocking collectives  109 us (36%)
  Pallas kernels  52.6 us (17%)
  starting transfers between devices  16.3 us (5%)
  other arithmetic  7.79 us (3%)
    all_to_all x3, blocking collectives, exchange(): return lax.all_to_all(x, axes, 0, 0, tiled=True)  109 us
    all_to_all x1, waiting for transfers between devices, exchange(): return lax.all_to_all(x, axes, 0, 0, tiled=True)  92.3 us
    pallas_call x1, Pallas kernels, newton(): pl.pallas_call(newton_kernel, in_specs=[whole] * 3, out_specs=[whole] * 3...  45.4 us
    ppermute x4, waiting for transfers between devices, swap(): return lax.ppermute(x, axis, [(0, 1), (1, 0)])  16.3 us
    all_to_all x1, starting transfers between devices, exchange(): return lax.all_to_all(x, axes, 0, 0, tiled=True)  11.2 us
    pallas_call x1, Pallas kernels, sum_and_gram(): pl.pallas_call(gram_kernel, grid=(N_DP // STEP,), in_specs=[pl.BlockSpec(...  7.18 us
  transfers between devices with their start and end apart: 5, of which 5 were waited for; matrix products, arithmetic and copies ran while one was open for 0% of the time, Pallas kernels for 0%

profile of v1, /device:TPU:1, one launch (start us, length us, event | category | flops | bytes accessed | tf_op | source)
XLA Modules:
  0.0 297.9 jit_solution(5169423047798200927)
XLA Ops:
  0.6 0.0 copy-start.1
  0.6 11.2 %all-to-all-start = ((bf16[64,56,1024]{2,1,0:T(8,128)(2,1)}), bf16[64,56,1024]{2,1,0:T(8,128)(2,1)}, u32[]{:S(2)}, u32[]{:S(2)}) async-start(bf16[64,56,1024]{2,1,0:T(8,128)(2,1)} %bitcast.17), calls=%async_computation | async-start | bytes 14680064 | tf_op jit(solution)/shard_map/all_to_all | solution.py:183
  11.9 92.3 %all-to-all-done.parts = bf16[64,56,1024]{2,1,0:T(8,128)(2,1)} async-done(((bf16[64,56,1024]{2,1,0:T(8,128)(2,1)}), bf16[64,56,1024]{2,1,0:T(8,128)(2,1)}, u32[]{:S(2)}, u32[]{:S(2)}) %all-to-all-start) | async-done | bytes 7340064 | tf_op jit(solution)/shard_map/all_to_all | solution.py:183
  104.2 0.0 copy-done.1
  104.2 7.2 %sum_and_gram.1 = (f32[56,1024]{1,0:T(8,128)}, f32[56,1024]{1,0:T(8,128)S(1)}, f32[5120,128]{1,0:T(8,128)S(1)}) custom-call(bf16[64,56,1024]{2,1,0:T(8,128)(2,1)} %all-to-all-done.parts, f32[56,1024]{1,0:T(8,128)S(1)} %bitcast.15), custom_call_target="tpu_custom_call" | custom-call | tf_op jit(solution)/shard_map/sum_and_gram/pallas_call | solution.py:78
  111.4 0.0 copy-start
  111.4 0.7 copy-done
  112.1 1.1 constant_dynamic-slice_fusion
  113.2 0.0 collective-permute-start
  113.2 3.4 %collective-permute-done = f32[2560,128]{1,0:T(8,128)} collective-permute-done((f32[2560,128]{1,0:T(8,128)}, f32[2560,128]{1,0:T(8,128)}, u32[]{:S(2)}, u32[]{:S(2)}) %collective-permute-start) | collective-permute-done | bytes 1310752 | tf_op jit(solution)/shard_map/ppermute | solution.py:187
  116.6 1.4 dynamic-slice_add_fusion
  118.0 37.5 %all_to_all.20 = f32[64,40,128]{2,1,0:T(8,128)S(1)} all-to-all(f32[64,40,128]{2,1,0:T(8,128)S(1)} %bitcast.19), channel_id=1, replica_groups=mesh['z'=4,'y'=4,'xl'=2,'c'=2,'xh'=2] {'z','y','xl','xh'}, dimensions={0} | all-to-all | bytes 2621440 | tf_op jit(solution)/shard_map/all_to_all | solution.py:183
  155.5 0.1 reduce_sum.9
  155.6 0.1 broadcast_in_dim.4
  155.7 25.1 %all_to_all.21 = f32[64,40,128]{2,1,0:T(8,128)S(1)} all-to-all(f32[64,40,128]{2,1,0:T(8,128)S(1)} %broadcast_in_dim.4), channel_id=1, replica_groups=mesh['z'=4,'y'=4,'xl'=2,'c'=2,'xh'=2] {'z','y','xl','xh'}, dimensions={0} | all-to-all | bytes 2621440 | tf_op jit(solution)/shard_map/all_to_all | solution.py:183
  180.8 2.6 collective-permute-start.1
  183.4 2.7 collective-permute-done.1
  186.1 0.2 broadcast_select_fusion.1
  186.3 1.7 pad_maximum_fusion.packed
  187.9 45.4 %newton.1 = (f32[56,1024]{1,0:T(8,128)}, f32[56,1024]{1,0:T(8,128)}, bf16[56,1024]{1,0:T(8,128)(2,1)}) custom-call(f32[5120,128]{1,0:T(8,128)} %pad_maximum_fusion.packed, f32[56,1024]{1,0:T(8,128)} %copy-done, f32[56,1024]{1,0:T(8,128)} %bitcast.22), custom_call_target="tpu_custom_call" | custom-call | tf_op jit(solution)/shard_map/newton/pallas_call | solution.py:167
  233.4 0.3 collective-permute-start.2
  233.7 4.3 %collective-permute-done.2 = bf16[56,1024]{1,0:T(8,128)(2,1)S(1)} collective-permute-done((bf16[56,1024]{1,0:T(8,128)(2,1)}, bf16[56,1024]{1,0:T(8,128)(2,1)S(1)}, u32[]{:S(2)}, u32[]{:S(2)}) %collective-permute-start.2) | collective-permute-done | bytes 114720 | tf_op jit(solution)/shard_map/ppermute | solution.py:187
  237.9 1.0 maximum_select_fusion.1
  238.9 0.5 broadcast_in_dim.5
  239.4 46.8 %all_to_all.22 = bf16[16,2,56,1024]{3,2,1,0:T(8,128)(2,1)S(1)} all-to-all(bf16[16,2,56,1024]{3,2,1,0:T(8,128)(2,1)S(1)} %broadcast_in_dim.5), channel_id=1, replica_groups=mesh['z'=4,'y'=4,'xl'=2,'c'=2,'xh'=2] {'z','y'}, dimensions={0} | all-to-all | bytes 7340032 | tf_op jit(solution)/shard_map/all_to_all | solution.py:183
  286.2 2.1 collective-permute-start.3
  288.3 6.0 %collective-permute-done.3 = bf16[16,2,56,1024]{3,2,1,0:T(8,128)(2,1)S(1)} collective-permute-done((bf16[16,2,56,1024]{3,2,1,0:T(8,128)(2,1)S(1)}, bf16[16,2,56,1024]{3,2,1,0:T(8,128)(2,1)S(1)}, u32[]{:S(2)}, u32[]{:S(2)}) %collective-permute-start.3) | collective-permute-done | bytes 3670048 | tf_op jit(solution)/shard_map/ppermute | solution.py:187
  294.3 3.4 %maximum_select_fusion = bf16[16,2,2,56,1024]{4,3,2,1,0:T(8,128)(2,1)} fusion(bf16[16,2,1,56,1024]{4,3,2,1,0:T(8,128)(2,1)S(1)} %bitcast.21, bf16[16,2,1,56,1024]{4,3,2,1,0:T(8,128)(2,1)S(1)} %bitcast.16, pred[]{:T(512)S(6)} %eq.8), kind=kLoop, calls=%fused_computation | loop fusion | flops 11010048 | bytes 14680065 | tf_op jit(solution)/shard_map/jit(_where)/select_n | solution.py:213
Async XLA Ops:
  0.6 103.6 %copy-start.1 = (f32[1,1,56,1024]{3,2,1,0:T(8,128)S(1)}, f32[1,1,56,1024]{3,2,1,0:T(8,128)}, u32[]{:S(2)}) copy-start(f32[1,1,56,1024]{3,2,1,0:T(8,128)} %param.5) | copy-start | bytes 688132
  0.6 103.5 %all-to-all-start = ((bf16[64,56,1024]{2,1,0:T(8,128)(2,1)}), bf16[64,56,1024]{2,1,0:T(8,128)(2,1)}, u32[]{:S(2)}, u32[]{:S(2)}) async-start(bf16[64,56,1024]{2,1,0:T(8,128)(2,1)} %bitcast.17), calls=%async_computation | async-start | bytes 14680064 | tf_op jit(solution)/shard_map/all_to_all | solution.py:183
  111.4 0.7 copy-start
  113.2 3.4 %collective-permute-start = (f32[2560,128]{1,0:T(8,128)}, f32[2560,128]{1,0:T(8,128)}, u32[]{:S(2)}, u32[]{:S(2)}) collective-permute-start(f32[2560,128]{1,0:T(8,128)} %constant_dynamic-slice_fusion), channel_id=1, source_target_pairs={{0,2},{2,0},{1,3},{3,1},{4,6},{6,4},{5,7},{7,5},{8,10},{10,8},{9,1... | collective-permute-start | bytes 3932168 | tf_op jit(solution)/shard_map/ppermute | solution.py:187
  180.8 5.3 %collective-permute-start.1 = (f32[2560,128]{1,0:T(8,128)S(1)}, f32[2560,128]{1,0:T(8,128)S(1)}, u32[]{:S(2)}, u32[]{:S(2)}) collective-permute-start(f32[2560,128]{1,0:T(8,128)S(1)} %bitcast.20), channel_id=1, source_target_pairs={{0,2},{2,0},{1,3},{3,1},{4,6},{6,4},{5,7},{7,5},{8,10},{10,8},{9,1... | collective-permute-start | bytes 3932168 | tf_op jit(solution)/shard_map/ppermute | solution.py:187
  233.4 4.6 %collective-permute-start.2 = (bf16[56,1024]{1,0:T(8,128)(2,1)}, bf16[56,1024]{1,0:T(8,128)(2,1)S(1)}, u32[]{:S(2)}, u32[]{:S(2)}) collective-permute-start(bf16[56,1024]{1,0:T(8,128)(2,1)} %get-tuple-element.12), channel_id=1, source_target_pairs={{0,4},{4,0},{1,5},{5,1},{2,6},{6,2},{3,7},{7,3},{8,12},{12,8},{9,1... | collective-permute-start | bytes 344072 | tf_op jit(solution)/shard_map/ppermute | solution.py:187
  286.2 8.1 %collective-permute-start.3 = (bf16[16,2,56,1024]{3,2,1,0:T(8,128)(2,1)S(1)}, bf16[16,2,56,1024]{3,2,1,0:T(8,128)(2,1)S(1)}, u32[]{:S(2)}, u32[]{:S(2)}) collective-permute-start(bf16[16,2,56,1024]{3,2,1,0:T(8,128)(2,1)S(1)} %all_to_all.22), channel_id=1, source_target_pairs={{0,2},{2,0},{1,3},{3,1},{4,6},{6,4},{5,7},{7,5},{8,10},{10,8},{9,1... | collective-permute-start | bytes 11010056 | tf_op jit(solution)/shard_map/ppermute | solution.py:187

commit v2 on v0

v2 whole, which is shorter than its diff:
```python
import functools

import jax
import jax.numpy as jnp
import numpy as np
from jax import lax
from jax.experimental import pallas as pl
from jax.experimental.pallas import tpu as pltpu
from jax.sharding import Mesh, PartitionSpec as P

D = 7168
H = 1024
ITERS = 3
N_DP = 64
ROWS = 56
BLOCK = 256
UPPER = [(i, j) for i in range(H // BLOCK) for j in range(i, H // BLOCK)]
PACKED = len(UPPER) * BLOCK * BLOCK // 128

beta_rate = 0.95
learn_rate = 0.02
decay_rate = 0.1
small_eps = 1e-07
coef_first = 3.4445
coef_second = -4.775
coef_third = 2.0315

f32 = jnp.float32
bf16 = jnp.bfloat16
CHIPS = ("z", "y", "xl", "xh")
DP = ("z", "y", "xl", "c")


def split(x):
    hi = x.astype(bf16)
    return hi, (x - hi.astype(f32)).astype(bf16)


def dot(a, b):
    return jnp.dot(a, b, preferred_element_type=f32)


WIDE = H // 2


def gram_kernel(place_ref, early, late, late_other, momentum, new_momentum, direction, kept, given):
    left = early[0]
    for i in range(1, early.shape[0]):
        left += early[i]
    grad = jnp.concatenate([left, late[...] + late_other[...]], axis=1)
    moved = beta_rate * momentum[...] + grad
    new_momentum[...] = moved
    direct = grad + beta_rate * moved
    direction[...] = direct
    hi, lo = split(direct)
    tall = jnp.concatenate([hi, lo, hi, lo], axis=0).T
    deep = jnp.concatenate([hi, hi, lo, lo], axis=0)
    place = 0
    for i in range(H // BLOCK):
        wide = dot(tall[i * BLOCK : (i + 1) * BLOCK], deep[:, i * BLOCK :])
        for j in range((H // BLOCK - i) * BLOCK // 128):
            half, at = divmod(place, PACKED // 2)
            value = wide[:, j * 128 : (j + 1) * 128]

            @pl.when(place_ref[1] == half)
            def _():
                kept[pl.ds(at, BLOCK), :] = value

            @pl.when(place_ref[1] != half)
            def _():
                given[pl.ds(at, BLOCK), :] = value

            place += BLOCK


def direction_and_gram(place, early, late, late_other, momentum):
    whole = pl.BlockSpec(memory_space=pltpu.VMEM)
    row = jax.ShapeDtypeStruct((ROWS, H), f32)
    half = jax.ShapeDtypeStruct((PACKED // 2, 128), f32)
    return pl.pallas_call(
        gram_kernel,
        in_specs=[pl.BlockSpec(memory_space=pltpu.SMEM)] + [whole] * 4,
        out_specs=[whole] * 4,
        out_shape=[row, row, half, half],
        compiler_params=pltpu.CompilerParams(vmem_limit_bytes=24 * 2**20),
        name="direction_and_gram",
    )(place, early, late, late_other, momentum)


def newton_kernel(
    place_ref, mine, other, direction, direction_other, master, master_other,
    update, new_master, pairs, gram, g_hi, g_lo, p_hi, p_lo,
):
    n = H // BLOCK
    spans = [slice(i * BLOCK, (i + 1) * BLOCK) for i in range(n)]
    on = lax.broadcasted_iota(jnp.int32, (BLOCK, BLOCK), 0) == lax.broadcasted_iota(
        jnp.int32, (BLOCK, BLOCK), 1
    )
    first_core = place_ref[1] == 0

    def loaded(place):
        half, at = divmod(place, PACKED // 2)
        a, b = mine[pl.ds(at, BLOCK), :], other[pl.ds(at, BLOCK), :]
        return jnp.where(first_core, a, b) if half == 0 else jnp.where(first_core, b, a)

    def put(value, i, j, hi_ref, lo_ref):
        hi, lo = split(value)
        hi_ref[spans[i], spans[j]] = hi
        lo_ref[spans[i], spans[j]] = lo
        if j > i:
            hi_ref[spans[j], spans[i]] = hi.T
            lo_ref[spans[j], spans[i]] = lo.T

    def full(a_hi, a_lo, b_hi, b_lo, i):
        cols = slice(i * BLOCK, H)
        b = b_hi[:, cols]
        return (
            dot(a_hi[spans[i], :], b)
            + dot(a_lo[spans[i], :], b)
            + dot(a_hi[spans[i], :], b_lo[:, cols])
        )

    def thin(x, b_hi, b_lo):
        hi, lo = split(x)
        both = dot(jnp.concatenate([hi, lo], axis=0), b_hi[...])
        return both[: 2 * ROWS] + both[2 * ROWS :] + dot(hi, b_lo[...])

    def poly():
        for i in range(n):
            square = full(g_hi, g_lo, g_hi, g_lo, i)
            for j in range(i, n):
                value = coef_second * gram[spans[i], spans[j]]
                value += coef_third * square[:, (j - i) * BLOCK : (j - i + 1) * BLOCK]
                if i == j:
                    value += jnp.where(on, coef_first, 0.0)
                put(value, i, j, p_hi, p_lo)

    def times_poly():
        for i in range(n):
            gram[spans[i], i * BLOCK :] = full(g_hi, g_lo, p_hi, p_lo, i)
        for i in range(n):
            for j in range(i, n):
                put(gram[spans[i], spans[j]], i, j, g_hi, g_lo)

    place = 0
    trace = jnp.zeros((), f32)
    for i in range(n):
        for j in range(i, n):
            tile = jnp.concatenate([loaded(place), loaded(place + BLOCK)], axis=1)
            place += 2 * BLOCK
            gram[spans[i], spans[j]] = tile
            if i == j:
                trace += jnp.sum(jnp.where(on, tile, 0.0))
    inverse = 1.0 / (jnp.sqrt(jnp.full((1, 1), trace, f32)) + small_eps)
    for i in range(n):
        for j in range(i, n):
            value = gram[spans[i], spans[j]] * inverse * inverse
            gram[spans[i], spans[j]] = value
            put(value, i, j, g_hi, g_lo)

    scaled = jnp.concatenate([direction[...], direction_other[...]], axis=0) * inverse
    poly()
    scaled = thin(scaled, p_hi, p_lo)
    times_poly()
    times_poly()
    poly()
    scaled = thin(scaled, p_hi, p_lo)

    def last_gram(x):
        return thin(thin(thin(x, p_hi, p_lo), p_hi, p_lo), g_hi, g_lo)

    once = last_gram(scaled)
    twice = last_gram(once)
    scaled = coef_first * scaled + coef_second * once + coef_third * twice
    result = (0.2 * max(D, H) ** 0.5) * scaled
    update[...] = result[:ROWS]

    def stepped(old, change):
        return old * (1.0 - learn_rate * decay_rate) - learn_rate * change

    moved = stepped(master[...], result[:ROWS])
    new_master[...] = moved
    weights = moved.astype(bf16)
    weights_other = stepped(master_other[...], result[ROWS:]).astype(bf16)
    low = place_ref[0]
    for i in range(16):
        pairs[i, low] = weights
        pairs[i, 1 - low] = weights_other


def newton(place, *operands):
    whole = pl.BlockSpec(memory_space=pltpu.VMEM)
    row = jax.ShapeDtypeStruct((ROWS, H), f32)
    return pl.pallas_call(
        newton_kernel,
        in_specs=[pl.BlockSpec(memory_space=pltpu.SMEM)] + [whole] * 6,
        out_specs=[whole] * 3,
        out_shape=[row, row, jax.ShapeDtypeStruct((16, 2, ROWS, H), bf16)],
        scratch_shapes=[pltpu.VMEM((H, H), f32)] + [pltpu.VMEM((H, H), bf16)] * 4,
        compiler_params=pltpu.CompilerParams(vmem_limit_bytes=56 * 2**20),
        name="newton",
    )(place, *operands)


def exchange(x, axes):
    return lax.all_to_all(x, axes, 0, 0, tiled=True)


def swap(x, axis):
    return lax.ppermute(x, axis, [(0, 1), (1, 0)])


def repeat(x, n):
    return jnp.broadcast_to(x[None], (n,) + x.shape)


def pick(x, axis, index):
    return lax.dynamic_index_in_dim(x, index, axis, keepdims=False)


def late_kernel(given, grads, out, sems):
    copies = []
    for xl in range(2):
        for c in range(2):
            copy = pltpu.make_async_copy(
                grads.at[:, xl, c, :, pl.ds(WIDE, WIDE)], out.at[:, c, xl], sems.at[2 * xl + c]
            )
            copy.start()
            copies.append(copy)
    for copy in copies:
        copy.wait()


def late_columns(given, grads):
    return pl.pallas_call(
        late_kernel,
        in_specs=[pl.BlockSpec(memory_space=pl.ANY), pl.BlockSpec(memory_space=pltpu.HBM)],
        out_specs=pl.BlockSpec(memory_space=pltpu.VMEM),
        out_shape=jax.ShapeDtypeStruct((16, 2, 2, ROWS, WIDE), bf16),
        scratch_shapes=[pltpu.SemaphoreType.DMA((4,))],
        compiler_params=pltpu.CompilerParams(vmem_limit_bytes=16 * 2**20),
        name="late_columns",
    )(given, grads)


def summed_parts(place, grads, master):
    low, core = place[0], place[1]
    grads = grads.reshape(16, 2, 2, ROWS, H)

    def left(c):
        block = lax.dynamic_slice(grads, (0, 0, c, 0, 0), (16, 2, 1, ROWS, WIDE))
        return block.reshape(16, 2, ROWS, WIDE)

    given = left(1 - core)
    swapped = swap(given, "c")
    late = late_columns(given, grads).reshape(32, 2 * ROWS, WIDE)
    late = exchange(late, ("z", "y", "c"))
    early = left(core).astype(f32) + swapped.astype(f32)
    early = pick(early, 1, low) + swap(pick(early, 1, 1 - low), "xl")
    late = late.astype(f32).sum(0).reshape(2, ROWS, WIDE)
    late_other = swap(pick(late, 0, 1 - low), "xl")
    late_other, master = lax.optimization_barrier((late_other, master))
    master_other = swap(master, "xl")
    early, master_other = lax.optimization_barrier((exchange(early, ("z", "y")), master_other))
    return early, pick(late, 0, low), late_other, master_other


def summed_gram(kept, given, ready):
    part = kept + swap(given, "c")
    piece = exchange(part.reshape(64, -1, 128), CHIPS).sum(0)
    piece, ready = lax.optimization_barrier((piece, ready))
    mine = exchange(repeat(piece, 64), CHIPS).reshape(PACKED // 2, 128)
    return mine, swap(mine, "c"), ready


def place_kernel(which, place, piece, *refs):
    out, sem = refs[-2:]
    copy = pltpu.make_async_copy(piece, out.at[:, place[which]], sem)
    copy.start()
    copy.wait()


def placed(place, piece, which, held=None):
    rest = [] if held is None else [held]
    return pl.pallas_call(
        functools.partial(place_kernel, which),
        in_specs=[pl.BlockSpec(memory_space=pltpu.SMEM)]
        + [pl.BlockSpec(memory_space=pltpu.VMEM)]
        + [pl.BlockSpec(memory_space=pltpu.HBM)] * len(rest),
        out_specs=pl.BlockSpec(memory_space=pltpu.HBM),
        out_shape=jax.ShapeDtypeStruct((32, 2, ROWS, H), bf16),
        input_output_aliases={2: 0} if rest else {},
        scratch_shapes=[pltpu.SemaphoreType.DMA],
        compiler_params=pltpu.CompilerParams(vmem_limit_bytes=16 * 2**20),
        name="placed",
    )(place, piece, *rest)


def gathered(place, pairs):
    mine = exchange(pairs, ("z", "y")).reshape(32, ROWS, H)
    other = swap(mine, "c")
    whole = placed(place, other, 2, placed(place, mine, 1))
    return whole.reshape(1, N_DP * ROWS, H)


def shards(grad_parts, master, momentum):
    core, low = lax.axis_index("c"), lax.axis_index("xl")
    place = jnp.stack([low, core, 1 - core]).astype(jnp.int32)
    master = master.reshape(ROWS, H)
    early, late, late_other, master_other = summed_parts(place, grad_parts, master)
    new_momentum, direction, kept, given = direction_and_gram(
        place, early, late, late_other, momentum.reshape(ROWS, H)
    )
    direction_other = swap(direction, "xl")
    mine, other, direction_other = summed_gram(kept, given, direction_other)
    update, new_master, pairs = newton(
        place, mine, other, direction, direction_other, master, master_other
    )
    return (
        gathered(place, pairs),
        new_momentum.reshape(momentum.shape),
        new_master.reshape(momentum.shape),
        update.reshape(momentum.shape),
    )


def solution(mesh):
    fine = Mesh(mesh.devices.reshape(4, 4, 2, 2, 2), ("z", "y", "xl", "c", "xh"))
    rows = P(None, "xh", DP, None)
    return jax.shard_map(
        shards,
        mesh=fine,
        in_specs=(P(DP, None, "xh", None), rows, rows),
        out_specs=(P(None, "xh", None), rows, rows, rows),
        check_vma=False,
    )
```

time: 1050 us -> 258 us (0.25)
  waiting for transfers between devices: 874 us -> 89.2 us
  matrix products: 78.6 us -> 0 us
  Pallas kernels: 0 us -> 35.2 us
  starting transfers between devices: 0.87 us -> 35.1 us
  between operations: 14.6 us -> 0.97 us
    psum x3 -> x0, waiting for transfers between devices: 455 us -> none  [summed_gram(): return lax.psum(partial_gram, ('dp', 'mp'))]
    reduce_scatter x1 -> x0, waiting for transfers between devices: 310 us -> none  [shards(): lax.psum_scatter(local_terms, 'dp', scatter_dimension=1, tiled=True)]
    all_gather x1 -> x0, waiting for transfers between devices: 109 us -> none  [shards(): new_weights = lax.all_gather(weight_rows, 'dp', axis=1, tiled=True)]
    dot_general x9 -> x0, matrix products: 78.6 us -> none  [the longest x3 51.9 us: newton_step(): jnp.einsum('ehk,ekl->ehl', gram, gram, precision=lax.Precision.HIGHEST)]
    all_to_all x0 -> x2, blocking collectives: none -> 76.6 us  [exchange(): return lax.all_to_all(x, axes, 0, 0, tiled=True)]
    psum x1 -> x0, blocking collectives: 66.9 us -> none  [shards(): lax.psum(jnp.sum(direction * direction, axis=(1, 2)), ('dp', 'mp'))]
    ppermute x0 -> x8, waiting for transfers between devices: none -> 56 us  [swap(): return lax.ppermute(x, axis, [(0, 1), (1, 0)])]
    pallas_call x0 -> x5, Pallas kernels: none -> 35.2 us  [the longest x1 27.2 us: newton(): pl.pallas_call(newton_kernel, in_specs=[pl.BlockSpec(memory_space=pltpu.S...]
  transfers between devices with their start and end apart: 5 -> 11, of which waited for: 5 -> 8; matrix products, arithmetic and copies ran while one was open for 0% -> 4% of each run, Pallas kernels for 0% -> 1%
where the time goes in v2:
time: 258 us; the launch traced here: 257 us
  waiting for transfers between devices  89.2 us (35%)
  blocking collectives  76.6 us (30%)
  Pallas kernels  35.2 us (14%)
  starting transfers between devices  35.1 us (14%)
  local copies, waits for them, and re-layouts  10.2 us (4%)
  other arithmetic  9.89 us (4%)
    all_to_all x2, blocking collectives, exchange(): return lax.all_to_all(x, axes, 0, 0, tiled=True)  76.6 us
    ppermute x8, waiting for transfers between devices, swap(): return lax.ppermute(x, axis, [(0, 1), (1, 0)])  56 us
    all_to_all x3, waiting for transfers between devices, exchange(): return lax.all_to_all(x, axes, 0, 0, tiled=True)  33.2 us
    pallas_call x1, Pallas kernels, newton(): pl.pallas_call(newton_kernel, in_specs=[pl.BlockSpec(memory_space=pltpu.S...  27.2 us
    all_to_all x3, starting transfers between devices, exchange(): return lax.all_to_all(x, axes, 0, 0, tiled=True)  20.8 us
    ppermute x8, starting transfers between devices, swap(): return lax.ppermute(x, axis, [(0, 1), (1, 0)])  14.3 us
    unnamed x24, local copies, waits for them, and re-layouts  6.81 us
  transfers between devices with their start and end apart: 11, of which 8 were waited for; matrix products, arithmetic and copies ran while one was open for 4% of the time, Pallas kernels for 1%

profile of v2, /device:TPU:1, one launch (start us, length us, event | category | flops | bytes accessed | tf_op | source)
XLA Modules:
  0.0 257.2 jit_solution(4095623948375175195)
XLA Ops:
  0.6 1.7 dynamic-slice_bitcast_fusion.1.given
  2.3 1.5 collective-permute-start
  3.8 0.0 copy-start
  3.8 3.1 %copy-done = bf16[1,1,3584,1024]{3,2,1,0:T(8,128)(2,1)S(1)} copy-done((bf16[1,1,3584,1024]{3,2,1,0:T(8,128)(2,1)S(1)}, bf16[1,1,3584,1024]{3,2,1,0:T(8,128)(2,1)}, u32[]{:S(2)}) %copy-start) | copy-done | bytes 7340056
  6.9 0.5 late_columns.1
  7.4 0.0 copy-start.1
  7.4 1.8 copy-done.1
  9.3 8.3 %all-to-all-start.1 = ((bf16[32,112,512]{2,1,0:T(8,128)(2,1)}), bf16[32,112,512]{2,1,0:T(8,128)(2,1)}, u32[]{:S(2)}, u32[]{:S(2)}) async-start(bf16[32,112,512]{2,1,0:T(8,128)(2,1)} %bitcast.31), calls=%async_computation.1 | async-start | bytes 7340032 | tf_op jit(solution)/shard_map/all_to_all | solution.py:206
  17.6 0.0 collective-permute-done
  17.6 2.7 %convert_add_fusion = f32[16,2,56,512]{3,2,1,0:T(8,128)S(1)} fusion(bf16[16,2,56,512]{3,2,1,0:T(8,128)(2,1)} %collective-permute-done, bf16[16,2,2,56,1024]{4,3,2,1,0:T(8,128)(2,1)} %bitcast.29, s32[]{:T(128)S(6)} %select_n.16), kind=kLoop, calls=%fused_computation.1 | loop fusion | flops 2752512 | bytes 7340036 | tf_op jit(solution)/shard_map/add | solution.py:258
  20.3 0.0 copy-start.6
  20.3 1.6 dynamic-slice_bitcast_fusion
  21.9 0.8 copy-done.6
  22.7 1.2 collective-permute-start.1
  24.0 40.4 %collective-permute-done.1 = f32[16,56,512]{2,1,0:T(8,128)S(1)} collective-permute-done((f32[16,56,512]{2,1,0:T(8,128)}, f32[16,56,512]{2,1,0:T(8,128)S(1)}, u32[]{:S(2)}, u32[]{:S(2)}) %collective-permute-start.1) | collective-permute-done | bytes 1835040 | tf_op jit(solution)/shard_map/ppermute | solution.py:210
  64.4 3.2 %bitcast_add_fusion = f32[16,56,512]{2,1,0:T(8,128)} fusion(f32[16,56,512]{2,1,0:T(8,128)S(1)} %collective-permute-done.1, f32[16,2,56,512]{3,2,1,0:T(8,128)} %copy-done.6, s32[]{:T(128)S(6)} %select_n.18), kind=kLoop, calls=%fused_computation.2 | loop fusion | flops 458752 | bytes 5505028 | tf_op jit(solution)/shard_map/add | solution.py:259
  67.6 0.0 all-to-all-done.1
  67.6 6.5 %all-to-all-start = ((f32[16,56,512]{2,1,0:T(8,128)}), f32[16,56,512]{2,1,0:T(8,128)S(1)}, u32[]{:S(2)}, u32[]{:S(2)}) async-start(f32[16,56,512]{2,1,0:T(8,128)} %bitcast_add_fusion), calls=%async_computation | async-start | bytes 3670016 | tf_op jit(solution)/shard_map/all_to_all | solution.py:206
  74.1 0.0 copy-start.9
  74.1 0.0 copy-start.2
  74.1 2.6 %convert_reduce_fusion = f32[112,512]{1,0:T(8,128)S(1)} fusion(bf16[32,112,512]{2,1,0:T(8,128)(2,1)} %all-to-all-done.1), kind=kLoop, calls=%fused_computation | loop fusion | flops 3612672 | bytes 3899392 | tf_op jit(solution)/shard_map/reduce_sum | solution.py:260
  76.8 1.3 collective-permute-start.2
  78.1 2.7 %collective-permute-done.2.late_other = f32[56,512]{1,0:T(8,128)S(1)} collective-permute-done((f32[56,512]{1,0:T(8,128)S(1)}, f32[56,512]{1,0:T(8,128)S(1)}, u32[]{:S(2)}, u32[]{:S(2)}) %collective-permute-start.2) | collective-permute-done | bytes 114720 | tf_op jit(solution)/shard_map/ppermute | solution.py:210
  80.8 0.0 copy-done.9
  80.8 1.2 collective-permute-start.3
  82.0 0.1 pad_add_fusion.place_ref.place
  82.1 0.0 copy-start.4
  82.1 3.9 %collective-permute-done.3.master_other = f32[56,1024]{1,0:T(8,128)S(1)} collective-permute-done((f32[56,1024]{1,0:T(8,128)S(1)}, f32[56,1024]{1,0:T(8,128)S(1)}, u32[]{:S(2)}, u32[]{:S(2)}) %collective-permute-start.3) | collective-permute-done | bytes 229408 | tf_op jit(solution)/shard_map/ppermute | solution.py:210
  86.0 0.0 copy-start.10
  86.0 13.2 %all-to-all-done.early = f32[16,56,512]{2,1,0:T(8,128)S(1)} async-done(((f32[16,56,512]{2,1,0:T(8,128)}), f32[16,56,512]{2,1,0:T(8,128)S(1)}, u32[]{:S(2)}, u32[]{:S(2)}) %all-to-all-start) | async-done | bytes 1835040 | tf_op jit(solution)/shard_map/all_to_all | solution.py:206
  99.1 0.0 copy-done.2
  99.1 2.7 %direction_and_gram.1 = (f32[56,1024]{1,0:T(8,128)}, f32[56,1024]{1,0:T(8,128)S(1)}, f32[2560,128]{1,0:T(8,128)S(1)}, f32[2560,128]{1,0:T(8,128)S(1)}) custom-call(s32[3]{0:T(128)S(1)} %pad_add_fusion.place_ref.place, f32[16,56,512]{2,1,0:T(8,128)S(1)} %all-to-all-done.early, f32[56,512]{1,0:T(8,128)S(1)} %get-tuple-element.30.late, ...), custom_call_target="tpu_custom_call" | custom-call | tf_op jit(solution)/shard_map/direction_and_gram/pallas_call | solution.py:80
  101.9 0.0 copy-start.3
  101.9 3.5 %collective-permute-start.4 = (f32[2560,128]{1,0:T(8,128)S(1)}, f32[2560,128]{1,0:T(8,128)S(1)}, u32[]{:S(2)}, u32[]{:S(2)}) collective-permute-start(f32[2560,128]{1,0:T(8,128)S(1)} %get-tuple-element.21), channel_id=1, source_target_pairs={{0,2},{2,0},{1,3},{3,1},{4,6},{6,4},{5,7},{7,5},{8,10},{10,8},{9,1... | collective-permute-start | bytes 3932168 | tf_op jit(solution)/shard_map/ppermute | solution.py:210
  105.3 2.7 %collective-permute-done.4 = f32[2560,128]{1,0:T(8,128)S(1)} collective-permute-done((f32[2560,128]{1,0:T(8,128)S(1)}, f32[2560,128]{1,0:T(8,128)S(1)}, u32[]{:S(2)}, u32[]{:S(2)}) %collective-permute-start.4) | collective-permute-done | bytes 1310752 | tf_op jit(solution)/shard_map/ppermute | solution.py:210
  108.0 1.2 add.33
  109.2 0.0 copy-done.4
  109.2 0.0 copy-done.10
  109.2 5.9 %all-to-all-start.2 = ((f32[64,40,128]{2,1,0:T(8,128)}), f32[64,40,128]{2,1,0:T(8,128)S(1)}, u32[]{:S(2)}, u32[]{:S(2)}) async-start(f32[64,40,128]{2,1,0:T(8,128)} %bitcast.38), calls=%async_computation.2 | async-start | bytes 2621440 | tf_op jit(solution)/shard_map/all_to_all | solution.py:206
  115.1 0.0 copy-done.3
  115.2 1.1 collective-permute-start.5
  116.2 20.1 %all-to-all-done.2 = f32[64,40,128]{2,1,0:T(8,128)S(1)} async-done(((f32[64,40,128]{2,1,0:T(8,128)}), f32[64,40,128]{2,1,0:T(8,128)S(1)}, u32[]{:S(2)}, u32[]{:S(2)}) %all-to-all-start.2) | async-done | bytes 1310752 | tf_op jit(solution)/shard_map/all_to_all | solution.py:206
  136.3 0.1 reduce_sum.19
  136.4 0.0 collective-permute-done.5.direction_other
  136.4 0.0 copy-start.11
  136.4 0.1 broadcast_in_dim.2
  136.5 27.8 %all_to_all.25 = f32[64,40,128]{2,1,0:T(8,128)S(1)} all-to-all(f32[64,40,128]{2,1,0:T(8,128)S(1)} %broadcast_in_dim.2), channel_id=1, replica_groups=mesh['z'=4,'y'=4,'xl'=2,'c'=2,'xh'=2] {'z','y','xl','xh'}, dimensions={0} | all-to-all | bytes 2621440 | tf_op jit(solution)/shard_map/all_to_all | solution.py:206
  164.4 0.0 copy-done.11
  164.4 0.0 copy-start.7
  164.4 3.0 %collective-permute-start.6 = (f32[2560,128]{1,0:T(8,128)S(1)}, f32[2560,128]{1,0:T(8,128)S(1)}, u32[]{:S(2)}, u32[]{:S(2)}) collective-permute-start(f32[2560,128]{1,0:T(8,128)S(1)} %bitcast.36), channel_id=1, source_target_pairs={{0,2},{2,0},{1,3},{3,1},{4,6},{6,4},{5,7},{7,5},{8,10},{10,8},{9,1... | collective-permute-start | bytes 3932168 | tf_op jit(solution)/shard_map/ppermute | solution.py:210
  167.4 2.7 %collective-permute-done.6.other = f32[2560,128]{1,0:T(8,128)S(1)} collective-permute-done((f32[2560,128]{1,0:T(8,128)S(1)}, f32[2560,128]{1,0:T(8,128)S(1)}, u32[]{:S(2)}, u32[]{:S(2)}) %collective-permute-start.6) | collective-permute-done | bytes 1310752 | tf_op jit(solution)/shard_map/ppermute | solution.py:210
  170.0 0.0 copy-done.7
  170.0 0.0 copy-start.8
  170.0 1.0 copy-done.8
  171.1 27.2 %newton.1 = (f32[56,1024]{1,0:T(8,128)}, f32[56,1024]{1,0:T(8,128)}, bf16[16,2,56,1024]{3,2,1,0:T(8,128)(2,1)}) custom-call(s32[3]{0:T(128)} %copy-done.4, f32[2560,128]{1,0:T(8,128)} %bitcast.37, f32[2560,128]{1,0:T(8,128)} %copy-done.8, f32[56,1024]{1,0:T(8,128)} %copy-done.3, f32[56,1024]{1,0:T(8,128)} %copy-done.11, f32[56,1024]{1,0:T(8,128)} %bitcast.40, ...), custom_call_target="tpu_custom_call" | custom-call | tf_op jit(solution)/shard_map/newton/pallas_call | solution.py:194
  198.3 0.0 copy-start.5
  198.3 48.8 %all_to_all.26 = bf16[16,2,56,1024]{3,2,1,0:T(8,128)(2,1)S(1)} all-to-all(bf16[16,2,56,1024]{3,2,1,0:T(8,128)(2,1)} %get-tuple-element.26), channel_id=1, replica_groups=mesh['z'=4,'y'=4,'xl'=2,'c'=2,'xh'=2] {'z','y'}, dimensions={0} | all-to-all | bytes 7340032 | tf_op jit(solution)/shard_map/all_to_all | solution.py:206
  247.1 1.5 collective-permute-start.7
  248.6 0.0 copy-done.5
  248.6 2.4 placed.2.refs_0_
  251.0 3.6 %collective-permute-done.7.piece = bf16[32,56,1024]{2,1,0:T(8,128)(2,1)S(1)} collective-permute-done((bf16[32,56,1024]{2,1,0:T(8,128)(2,1)S(1)}, bf16[32,56,1024]{2,1,0:T(8,128)(2,1)S(1)}, u32[]{:S(2)}, u32[]{:S(2)}) %collective-permute-start.7) | collective-permute-done | bytes 3670048 | tf_op jit(solution)/shard_map/ppermute | solution.py:210
  254.6 2.4 placed.3
  (1 shorter events, 0.0 us)
Async XLA Ops:
  2.3 15.3 %collective-permute-start = (bf16[16,2,56,512]{3,2,1,0:T(8,128)(2,1)S(1)}, bf16[16,2,56,512]{3,2,1,0:T(8,128)(2,1)}, u32[]{:S(2)}, u32[]{:S(2)}) collective-permute-start(bf16[16,2,56,512]{3,2,1,0:T(8,128)(2,1)S(1)} %dynamic-slice_bitcast_fusion.1.given), channel_id=1, source_target_pairs={{0,2},{2,0},{1,3},{3,1},{4,6},{6,4},{5,7},{7,5},{8,10},{10,8},{9,1... | collective-permute-start | bytes 5505032 | tf_op jit(solution)/shard_map/ppermute | solution.py:210
  3.8 3.1 %copy-start = (bf16[1,1,3584,1024]{3,2,1,0:T(8,128)(2,1)S(1)}, bf16[1,1,3584,1024]{3,2,1,0:T(8,128)(2,1)}, u32[]{:S(2)}) copy-start(bf16[1,1,3584,1024]{3,2,1,0:T(8,128)(2,1)} %param.3) | copy-start | bytes 22020100
  7.4 1.8 copy-start.1
  9.3 58.3 %all-to-all-start.1 = ((bf16[32,112,512]{2,1,0:T(8,128)(2,1)}), bf16[32,112,512]{2,1,0:T(8,128)(2,1)}, u32[]{:S(2)}, u32[]{:S(2)}) async-start(bf16[32,112,512]{2,1,0:T(8,128)(2,1)} %bitcast.31), calls=%async_computation.1 | async-start | bytes 7340032 | tf_op jit(solution)/shard_map/all_to_all | solution.py:206
  20.3 2.4 copy-start.6
  22.7 41.6 %collective-permute-start.1 = (f32[16,56,512]{2,1,0:T(8,128)}, f32[16,56,512]{2,1,0:T(8,128)S(1)}, u32[]{:S(2)}, u32[]{:S(2)}) collective-permute-start(f32[16,56,512]{2,1,0:T(8,128)} %dynamic-slice_bitcast_fusion), channel_id=1, source_target_pairs={{0,4},{4,0},{1,5},{5,1},{2,6},{6,2},{3,7},{7,3},{8,12},{12,8},{9,1... | collective-permute-start | bytes 5505032 | tf_op jit(solution)/shard_map/ppermute | solution.py:210
  67.6 31.6 %all-to-all-start = ((f32[16,56,512]{2,1,0:T(8,128)}), f32[16,56,512]{2,1,0:T(8,128)S(1)}, u32[]{:S(2)}, u32[]{:S(2)}) async-start(f32[16,56,512]{2,1,0:T(8,128)} %bitcast_add_fusion), calls=%async_computation | async-start | bytes 3670016 | tf_op jit(solution)/shard_map/all_to_all | solution.py:206
  74.1 6.7 %copy-start.9 = (f32[1,1,56,1024]{3,2,1,0:T(8,128)S(1)}, f32[1,1,56,1024]{3,2,1,0:T(8,128)}, u32[]{:S(2)}) copy-start(f32[1,1,56,1024]{3,2,1,0:T(8,128)} %param.4) | copy-start | bytes 688132
  74.1 25.0 %copy-start.2 = (f32[1,1,56,1024]{3,2,1,0:T(8,128)S(1)}, f32[1,1,56,1024]{3,2,1,0:T(8,128)}, u32[]{:S(2)}) copy-start(f32[1,1,56,1024]{3,2,1,0:T(8,128)} %param.5) | copy-start | bytes 688132
  76.8 4.0 %collective-permute-start.2 = (f32[56,512]{1,0:T(8,128)S(1)}, f32[56,512]{1,0:T(8,128)S(1)}, u32[]{:S(2)}, u32[]{:S(2)}) collective-permute-start(f32[56,512]{1,0:T(8,128)S(1)} %get-tuple-element.31), channel_id=1, source_target_pairs={{0,4},{4,0},{1,5},{5,1},{2,6},{6,2},{3,7},{7,3},{8,12},{12,8},{9,1... | collective-permute-start | bytes 344072 | tf_op jit(solution)/shard_map/ppermute | solution.py:210
  80.8 5.2 %collective-permute-start.3 = (f32[56,1024]{1,0:T(8,128)S(1)}, f32[56,1024]{1,0:T(8,128)S(1)}, u32[]{:S(2)}, u32[]{:S(2)}) collective-permute-start(f32[56,1024]{1,0:T(8,128)S(1)} %bitcast.41), channel_id=1, source_target_pairs={{0,4},{4,0},{1,5},{5,1},{2,6},{6,2},{3,7},{7,3},{8,12},{12,8},{9,1... | collective-permute-start | bytes 688136 | tf_op jit(solution)/shard_map/ppermute | solution.py:210
  82.1 27.1 %copy-start.4 = (s32[3]{0:T(128)}, s32[3]{0:T(128)S(1)}, u32[]{:S(2)}) copy-start(s32[3]{0:T(128)S(1)} %pad_add_fusion.place_ref.place) | copy-start | bytes 40
  86.0 23.2 %copy-start.10 = (f32[56,1024]{1,0:T(8,128)}, f32[56,1024]{1,0:T(8,128)S(1)}, u32[]{:S(2)}) copy-start(f32[56,1024]{1,0:T(8,128)S(1)} %collective-permute-done.3.master_other) | copy-start | bytes 688132
  101.9 13.3 %copy-start.3 = (f32[56,1024]{1,0:T(8,128)}, f32[56,1024]{1,0:T(8,128)S(1)}, u32[]{:S(2)}) copy-start(f32[56,1024]{1,0:T(8,128)S(1)} %get-tuple-element.22.direction) | copy-start | bytes 688132
  101.9 6.1 %collective-permute-start.4 = (f32[2560,128]{1,0:T(8,128)S(1)}, f32[2560,128]{1,0:T(8,128)S(1)}, u32[]{:S(2)}, u32[]{:S(2)}) collective-permute-start(f32[2560,128]{1,0:T(8,128)S(1)} %get-tuple-element.21), channel_id=1, source_target_pairs={{0,2},{2,0},{1,3},{3,1},{4,6},{6,4},{5,7},{7,5},{8,10},{10,8},{9,1... | collective-permute-start | bytes 3932168 | tf_op jit(solution)/shard_map/ppermute | solution.py:210
  109.2 27.1 %all-to-all-start.2 = ((f32[64,40,128]{2,1,0:T(8,128)}), f32[64,40,128]{2,1,0:T(8,128)S(1)}, u32[]{:S(2)}, u32[]{:S(2)}) async-start(f32[64,40,128]{2,1,0:T(8,128)} %bitcast.38), calls=%async_computation.2 | async-start | bytes 2621440 | tf_op jit(solution)/shard_map/all_to_all | solution.py:206
  115.2 21.3 %collective-permute-start.5 = (f32[56,1024]{1,0:T(8,128)S(1)}, f32[56,1024]{1,0:T(8,128)S(1)}, u32[]{:S(2)}, u32[]{:S(2)}) collective-permute-start(f32[56,1024]{1,0:T(8,128)S(1)} %get-tuple-element.22.direction), channel_id=1, source_target_pairs={{0,4},{4,0},{1,5},{5,1},{2,6},{6,2},{3,7},{7,3},{8,12},{12,8},{9,1... | collective-permute-start | bytes 688136 | tf_op jit(solution)/shard_map/ppermute | solution.py:210
  136.4 28.0 %copy-start.11 = (f32[56,1024]{1,0:T(8,128)}, f32[56,1024]{1,0:T(8,128)S(1)}, u32[]{:S(2)}) copy-start(f32[56,1024]{1,0:T(8,128)S(1)} %collective-permute-done.5.direction_other) | copy-start | bytes 688132
  164.4 5.7 %copy-start.7 = (f32[64,40,128]{2,1,0:T(8,128)}, f32[64,40,128]{2,1,0:T(8,128)S(1)}, u32[]{:S(2)}) copy-start(f32[64,40,128]{2,1,0:T(8,128)S(1)} %all_to_all.25) | copy-start | bytes 3932164
  164.4 5.7 %collective-permute-start.6 = (f32[2560,128]{1,0:T(8,128)S(1)}, f32[2560,128]{1,0:T(8,128)S(1)}, u32[]{:S(2)}, u32[]{:S(2)}) collective-permute-start(f32[2560,128]{1,0:T(8,128)S(1)} %bitcast.36), channel_id=1, source_target_pairs={{0,2},{2,0},{1,3},{3,1},{4,6},{6,4},{5,7},{7,5},{8,10},{10,8},{9,1... | collective-permute-start | bytes 3932168 | tf_op jit(solution)/shard_map/ppermute | solution.py:210
  170.0 1.1 copy-start.8
  198.3 50.3 %copy-start.5 = (s32[3]{0:T(128)S(1)}, s32[3]{0:T(128)}, u32[]{:S(2)}) copy-start(s32[3]{0:T(128)} %copy-done.4) | copy-start | bytes 40
  247.1 7.5 %collective-permute-start.7 = (bf16[32,56,1024]{2,1,0:T(8,128)(2,1)S(1)}, bf16[32,56,1024]{2,1,0:T(8,128)(2,1)S(1)}, u32[]{:S(2)}, u32[]{:S(2)}) collective-permute-start(bf16[32,56,1024]{2,1,0:T(8,128)(2,1)S(1)} %bitcast.32), channel_id=1, source_target_pairs={{0,2},{2,0},{1,3},{3,1},{4,6},{6,4},{5,7},{7,5},{8,10},{10,8},{9,1... | collective-permute-start | bytes 11010056 | tf_op jit(solution)/shard_map/ppermute | solution.py:210

commit v3 on v2

--- a/solution.py
+++ b/solution.py
@@ -41,54 +41,67 @@
 
 
 WIDE = H // 2
-
-
-def gram_kernel(place_ref, early, late, late_other, momentum, new_momentum, direction, kept, given):
-    left = early[0]
-    for i in range(1, early.shape[0]):
-        left += early[i]
-    grad = jnp.concatenate([left, late[...] + late_other[...]], axis=1)
-    moved = beta_rate * momentum[...] + grad
-    new_momentum[...] = moved
-    direct = grad + beta_rate * moved
+QUARTER = PACKED // 4
+
+
+def place_of(slab):
+    return slab // 10, slab % 10 // 5, slab % 5 * BLOCK
+
+
+def gram_kernel(
+    place_ref, early, early_other, late, late_given, momentum, momentum_other,
+    new_momentum, direction, kept, given,
+):
+    low = place_ref[0]
+
+    def moved(left, right, old):
+        grad = jnp.concatenate([left[...], right], axis=1)
+        new = beta_rate * old[...] + grad
+        return new, grad + beta_rate * new
+
+    new, direct = moved(early, late[low] + late_given[low], momentum)
+    _, direct_other = moved(early_other, late[1 - low] + late_given[1 - low], momentum_other)
+    new_momentum[...] = new
+    direct = jnp.concatenate([direct, direct_other], axis=0)
     direction[...] = direct
     hi, lo = split(direct)
     tall = jnp.concatenate([hi, lo, hi, lo], axis=0).T
     deep = jnp.concatenate([hi, hi, lo, lo], axis=0)
-    place = 0
-    for i in range(H // BLOCK):
-        wide = dot(tall[i * BLOCK : (i + 1) * BLOCK], deep[:, i * BLOCK :])
-        for j in range((H // BLOCK - i) * BLOCK // 128):
-            half, at = divmod(place, PACKED // 2)
-            value = wide[:, j * 128 : (j + 1) * 128]
-
-            @pl.when(place_ref[1] == half)
-            def _():
-                kept[pl.ds(at, BLOCK), :] = value
-
-            @pl.when(place_ref[1] != half)
-            def _():
-                given[pl.ds(at, BLOCK), :] = value
-
-            place += BLOCK
-
-
-def direction_and_gram(place, early, late, late_other, momentum):
+    for b, (i, j) in enumerate(UPPER):
+
+        @pl.when(low == b // 5)
+        def _():
+            tile = dot(tall[i * BLOCK : (i + 1) * BLOCK], deep[:, j * BLOCK : (j + 1) * BLOCK])
+            for side in range(2):
+                _, core, at = place_of(2 * b + side)
+                value = tile[:, side * 128 : (side + 1) * 128]
+
+                @pl.when(place_ref[1] == core)
+                def _():
+                    kept[pl.ds(at, BLOCK), :] = value
+
+                @pl.when(place_ref[1] != core)
+                def _():
+                    given[pl.ds(at, BLOCK), :] = value
+
+
+def direction_and_gram(place, *operands):
     whole = pl.BlockSpec(memory_space=pltpu.VMEM)
     row = jax.ShapeDtypeStruct((ROWS, H), f32)
-    half = jax.ShapeDtypeStruct((PACKED // 2, 128), f32)
+    rows = jax.ShapeDtypeStruct((2 * ROWS, H), f32)
+    quarter = jax.ShapeDtypeStruct((QUARTER, 128), f32)
     return pl.pallas_call(
         gram_kernel,
-        in_specs=[pl.BlockSpec(memory_space=pltpu.SMEM)] + [whole] * 4,
+        in_specs=[pl.BlockSpec(memory_space=pltpu.SMEM)] + [whole] * 6,
         out_specs=[whole] * 4,
-        out_shape=[row, row, half, half],
+        out_shape=[row, rows, quarter, quarter],
         compiler_params=pltpu.CompilerParams(vmem_limit_bytes=24 * 2**20),
         name="direction_and_gram",
-    )(place, early, late, late_other, momentum)
+    )(place, *operands)
 
 
 def newton_kernel(
-    place_ref, mine, other, direction, direction_other, master, master_other,
+    place_ref, mine, other, direction, master, master_other,
     update, new_master, pairs, gram, g_hi, g_lo, p_hi, p_lo,
 ):
     n = H // BLOCK
@@ -99,9 +112,10 @@
     first_core = place_ref[1] == 0
 
     def loaded(place):
-        half, at = divmod(place, PACKED // 2)
+        low, core, at = place_of(place // BLOCK)
+        at += low * QUARTER
         a, b = mine[pl.ds(at, BLOCK), :], other[pl.ds(at, BLOCK), :]
-        return jnp.where(first_core, a, b) if half == 0 else jnp.where(first_core, b, a)
+        return jnp.where(first_core, a, b) if core == 0 else jnp.where(first_core, b, a)
 
     def put(value, i, j, hi_ref, lo_ref):
         hi, lo = split(value)
@@ -158,7 +172,7 @@
             gram[spans[i], spans[j]] = value
             put(value, i, j, g_hi, g_lo)
 
-    scaled = jnp.concatenate([direction[...], direction_other[...]], axis=0) * inverse
+    scaled = direction[...] * inverse
     poly()
     scaled = thin(scaled, p_hi, p_lo)
     times_poly()
@@ -193,7 +207,7 @@
     row = jax.ShapeDtypeStruct((ROWS, H), f32)
     return pl.pallas_call(
         newton_kernel,
-        in_specs=[pl.BlockSpec(memory_space=pltpu.SMEM)] + [whole] * 6,
+        in_specs=[pl.BlockSpec(memory_space=pltpu.SMEM)] + [whole] * 5,
         out_specs=[whole] * 3,
         out_shape=[row, row, jax.ShapeDtypeStruct((16, 2, ROWS, H), bf16)],
         scratch_shapes=[pltpu.VMEM((H, H), f32)] + [pltpu.VMEM((H, H), bf16)] * 4,
@@ -243,7 +257,7 @@
     )(given, grads)
 
 
-def summed_parts(place, grads, master):
+def summed_parts(place, grads, state):
     low, core = place[0], place[1]
     grads = grads.reshape(16, 2, 2, ROWS, H)
 
@@ -258,19 +272,18 @@
     early = left(core).astype(f32) + swapped.astype(f32)
     early = pick(early, 1, low) + swap(pick(early, 1, 1 - low), "xl")
     late = late.astype(f32).sum(0).reshape(2, ROWS, WIDE)
-    late_other = swap(pick(late, 0, 1 - low), "xl")
-    late_other, master = lax.optimization_barrier((late_other, master))
-    master_other = swap(master, "xl")
-    early, master_other = lax.optimization_barrier((exchange(early, ("z", "y")), master_other))
-    return early, pick(late, 0, low), late_other, master_other
-
-
-def summed_gram(kept, given, ready):
+    late_given, state = lax.optimization_barrier((swap(late, "xl"), state))
+    state_other = swap(state, "xl")
+    early, state_other = lax.optimization_barrier((exchange(early, ("z", "y")), state_other))
+    early = early.sum(0)
+    return (early, swap(early, "xl"), late, late_given), state_other
+
+
+def summed_gram(kept, given):
     part = kept + swap(given, "c")
-    piece = exchange(part.reshape(64, -1, 128), CHIPS).sum(0)
-    piece, ready = lax.optimization_barrier((piece, ready))
-    mine = exchange(repeat(piece, 64), CHIPS).reshape(PACKED // 2, 128)
-    return mine, swap(mine, "c"), ready
+    piece = exchange(part.reshape(32, -1, 128), ("z", "y", "xh")).sum(0)
+    mine = exchange(repeat(piece, 64), ("xl", "z", "y", "xh")).reshape(2 * QUARTER, 128)
+    return mine, swap(mine, "c")
 
 
 def place_kernel(which, place, piece, *refs):
@@ -306,21 +319,22 @@
 def shards(grad_parts, master, momentum):
     core, low = lax.axis_index("c"), lax.axis_index("xl")
     place = jnp.stack([low, core, 1 - core]).astype(jnp.int32)
+    shape = master.shape
     master = master.reshape(ROWS, H)
-    early, late, late_other, master_other = summed_parts(place, grad_parts, master)
+    momentum = momentum.reshape(ROWS, H)
+    sums, state_other = summed_parts(place, grad_parts, jnp.concatenate([momentum, master]))
     new_momentum, direction, kept, given = direction_and_gram(
-        place, early, late, late_other, momentum.reshape(ROWS, H)
-    )
-    direction_other = swap(direction, "xl")
-    mine, other, direction_other = summed_gram(kept, given, direction_other)
+        place, *sums, momentum, state_other[:ROWS]
+    )
+    mine, other = summed_gram(kept, given)
     update, new_master, pairs = newton(
-        place, mine, other, direction, direction_other, master, master_other
+        place, mine, other, direction, master, state_other[ROWS:]
     )
     return (
         gathered(place, pairs),
-        new_momentum.reshape(momentum.shape),
-        new_master.reshape(momentum.shape),
-        update.reshape(momentum.shape),
+        new_momentum.reshape(shape),
+        new_master.reshape(shape),
+        update.reshape(shape),
     )
 
 

time: 258 us -> 250 us (0.969)
  waiting for transfers between devices: 89.2 us -> 69.9 us
  blocking collectives: 76.6 us -> 90.8 us
  starting transfers between devices: 35.1 us -> 31.6 us
    all_to_all x3 -> x2, waiting for transfers between devices: 33.2 us -> 7.13 us  [exchange(): return lax.all_to_all(x, axes, 0, 0, tiled=True)]
    all_to_all x2 -> x3, blocking collectives: 76.6 us -> 90.8 us  [exchange(): return lax.all_to_all(x, axes, 0, 0, tiled=True)]
    ppermute x8, waiting for transfers between devices: 56 us -> 62.8 us  [swap(): return lax.ppermute(x, axis, [(0, 1), (1, 0)])]
    all_to_all x3 -> x2, starting transfers between devices: 20.8 us -> 15.1 us  [exchange(): return lax.all_to_all(x, axes, 0, 0, tiled=True)]
    unnamed x24 -> x20, local copies, waits for them, and re-layouts: 6.81 us -> 7.85 us
  transfers between devices with their start and end apart: 11 -> 10, of which waited for: 8 -> 8; matrix products, arithmetic and copies ran while one was open for 4% -> 4% of each run, Pallas kernels for 1% -> 1%
where the time goes in v3:
time: 250 us; the launch traced here: 249 us
  blocking collectives  90.8 us (36%)
  waiting for transfers between devices  69.9 us (28%)
  Pallas kernels  35.5 us (14%)
  starting transfers between devices  31.6 us (13%)
  local copies, waits for them, and re-layouts  11.8 us (5%)
  other arithmetic  8.83 us (4%)
    all_to_all x3, blocking collectives, exchange(): return lax.all_to_all(x, axes, 0, 0, tiled=True)  90.8 us
    ppermute x8, waiting for transfers between devices, swap(): return lax.ppermute(x, axis, [(0, 1), (1, 0)])  62.8 us
    pallas_call x1, Pallas kernels, newton(): pl.pallas_call(newton_kernel, in_specs=[pl.BlockSpec(memory_space=pltpu.S...  27.2 us
    ppermute x8, starting transfers between devices, swap(): return lax.ppermute(x, axis, [(0, 1), (1, 0)])  16.5 us
    all_to_all x2, starting transfers between devices, exchange(): return lax.all_to_all(x, axes, 0, 0, tiled=True)  15.1 us
    unnamed x20, local copies, waits for them, and re-layouts  7.85 us
    all_to_all x2, waiting for transfers between devices, exchange(): return lax.all_to_all(x, axes, 0, 0, tiled=True)  7.13 us
  transfers between devices with their start and end apart: 10, of which 8 were waited for; matrix products, arithmetic and copies ran while one was open for 4% of the time, Pallas kernels for 1%

profile of v3, /device:TPU:1, one launch (start us, length us, event | category | flops | bytes accessed | tf_op | source)
XLA Modules:
  0.0 249.4 jit_solution(4746518643416039887)
XLA Ops:
  0.6 1.7 dynamic-slice_bitcast_fusion.1.given
  2.3 1.5 collective-permute-start
  3.8 0.0 copy-start
  3.8 3.1 %copy-done = bf16[1,1,3584,1024]{3,2,1,0:T(8,128)(2,1)S(1)} copy-done((bf16[1,1,3584,1024]{3,2,1,0:T(8,128)(2,1)S(1)}, bf16[1,1,3584,1024]{3,2,1,0:T(8,128)(2,1)}, u32[]{:S(2)}) %copy-start) | copy-done | bytes 7340056
  6.9 0.5 late_columns.1
  7.4 0.0 copy-start.1
  7.4 1.8 copy-done.1
  9.3 8.3 %all-to-all-start.1 = ((bf16[32,112,512]{2,1,0:T(8,128)(2,1)}), bf16[32,112,512]{2,1,0:T(8,128)(2,1)}, u32[]{:S(2)}, u32[]{:S(2)}) async-start(bf16[32,112,512]{2,1,0:T(8,128)(2,1)} %bitcast.27), calls=%async_computation.1 | async-start | bytes 7340032 | tf_op jit(solution)/shard_map/all_to_all | solution.py:220
  17.6 0.0 collective-permute-done
  17.6 2.7 %convert_add_fusion = f32[16,2,56,512]{3,2,1,0:T(8,128)S(1)} fusion(bf16[16,2,56,512]{3,2,1,0:T(8,128)(2,1)} %collective-permute-done, bf16[16,2,2,56,1024]{4,3,2,1,0:T(8,128)(2,1)} %bitcast.25, s32[]{:T(128)S(6)} %select_n.13), kind=kLoop, calls=%fused_computation.1 | loop fusion | flops 2752512 | bytes 7340036 | tf_op jit(solution)/shard_map/add | solution.py:272
  20.3 0.0 copy-start.6
  20.3 1.8 copy-done.6
  22.1 1.5 dynamic-slice_bitcast_fusion
  23.6 1.2 collective-permute-start.1
  24.8 40.3 %collective-permute-done.1 = f32[16,56,512]{2,1,0:T(8,128)S(1)} collective-permute-done((f32[16,56,512]{2,1,0:T(8,128)}, f32[16,56,512]{2,1,0:T(8,128)S(1)}, u32[]{:S(2)}, u32[]{:S(2)}) %collective-permute-start.1) | collective-permute-done | bytes 1835040 | tf_op jit(solution)/shard_map/ppermute | solution.py:224
  65.2 3.2 %bitcast_add_fusion = f32[16,56,512]{2,1,0:T(8,128)} fusion(f32[16,56,512]{2,1,0:T(8,128)S(1)} %collective-permute-done.1, f32[16,2,56,512]{3,2,1,0:T(8,128)} %copy-done.6, s32[]{:T(128)S(6)} %select_n.15), kind=kLoop, calls=%fused_computation.2 | loop fusion | flops 458752 | bytes 5505028 | tf_op jit(solution)/shard_map/add | solution.py:273
  68.4 0.0 copy-start.2
  68.4 0.0 copy-start.9
  68.4 0.0 all-to-all-done.1
  68.4 6.7 %all-to-all-start = ((f32[16,56,512]{2,1,0:T(8,128)}), f32[16,56,512]{2,1,0:T(8,128)S(1)}, u32[]{:S(2)}, u32[]{:S(2)}) async-start(f32[16,56,512]{2,1,0:T(8,128)} %bitcast_add_fusion), calls=%async_computation | async-start | bytes 3670016 | tf_op jit(solution)/shard_map/all_to_all | solution.py:220
  75.1 2.6 %convert_reduce_fusion = f32[112,512]{1,0:T(8,128)S(1)} fusion(bf16[32,112,512]{2,1,0:T(8,128)(2,1)} %all-to-all-done.1), kind=kLoop, calls=%fused_computation | loop fusion | flops 3612672 | bytes 3899392 | tf_op jit(solution)/shard_map/reduce_sum | solution.py:274
  77.7 1.3 collective-permute-start.2
  79.0 0.0 copy-done.2
  79.0 0.0 copy-done.9
  79.0 4.4 %collective-permute-done.2.late_given = f32[2,56,512]{2,1,0:T(8,128)S(1)} collective-permute-done((f32[2,56,512]{2,1,0:T(8,128)S(1)}, f32[2,56,512]{2,1,0:T(8,128)S(1)}, u32[]{:S(2)}, u32[]{:S(2)}) %collective-permute-start.2) | collective-permute-done | bytes 229408 | tf_op jit(solution)/shard_map/ppermute | solution.py:224
  83.4 1.2 collective-permute-start.3
  84.6 0.1 pad_add_fusion.place_ref.place
  84.7 0.0 copy-start.4
  84.7 8.3 %collective-permute-done.3 = f32[112,1024]{1,0:T(8,128)S(1)} collective-permute-done((f32[112,1024]{1,0:T(8,128)S(1)}, f32[112,1024]{1,0:T(8,128)S(1)}, u32[]{:S(2)}, u32[]{:S(2)}) %collective-permute-start.3) | collective-permute-done | bytes 458784 | tf_op jit(solution)/shard_map/ppermute | solution.py:224
  93.0 7.1 %all-to-all-done = f32[16,56,512]{2,1,0:T(8,128)S(1)} async-done(((f32[16,56,512]{2,1,0:T(8,128)}), f32[16,56,512]{2,1,0:T(8,128)S(1)}, u32[]{:S(2)}, u32[]{:S(2)}) %all-to-all-start) | async-done | bytes 1835040 | tf_op jit(solution)/shard_map/all_to_all | solution.py:220
  100.2 0.1 reduce_sum.28.early
  100.3 1.3 collective-permute-start.4
  101.6 0.7 fusion
  102.3 1.7 collective-permute-done.4.early_other
  104.0 3.1 %direction_and_gram.1 = (f32[56,1024]{1,0:T(8,128)}, f32[112,1024]{1,0:T(8,128)S(1)}, f32[1280,128]{1,0:T(8,128)S(1)}, f32[1280,128]{1,0:T(8,128)S(1)}) custom-call(s32[3]{0:T(128)S(1)} %pad_add_fusion.place_ref.place, f32[56,512]{1,0:T(8,128)S(1)} %reduce_sum.28.early, f32[56,512]{1,0:T(8,128)S(1)} %collective-permute-done.4.early_other, ...), custom_call_target="tpu_custom_call" | custom-call | tf_op jit(solution)/shard_map/direction_and_gram/pallas_call | solution.py:93
  107.1 0.0 copy-start.3
  107.1 4.6 %collective-permute-start.5 = (f32[1280,128]{1,0:T(8,128)S(1)}, f32[1280,128]{1,0:T(8,128)S(1)}, u32[]{:S(2)}, u32[]{:S(2)}) collective-permute-start(f32[1280,128]{1,0:T(8,128)S(1)} %get-tuple-element.20), channel_id=1, source_target_pairs={{0,2},{2,0},{1,3},{3,1},{4,6},{6,4},{5,7},{7,5},{8,10},{10,8},{9,1... | collective-permute-start | bytes 1966088 | tf_op jit(solution)/shard_map/ppermute | solution.py:224
  111.7 1.7 collective-permute-done.5
  113.4 0.1 add.30
  113.5 0.0 copy-done.3
  113.5 19.7 %all_to_all.25 = f32[32,40,128]{2,1,0:T(8,128)S(1)} all-to-all(f32[32,40,128]{2,1,0:T(8,128)S(1)} %bitcast.37), channel_id=1, replica_groups=mesh['z'=4,'y'=4,'xl'=2,'c'=2,'xh'=2] {'z','y','xh'}, dimensions={0} | all-to-all | bytes 1310720 | tf_op jit(solution)/shard_map/all_to_all | solution.py:220
  133.1 0.1 reduce_sum.29
  133.2 0.0 copy-done.4
  133.2 0.1 broadcast_in_dim.2
  133.3 22.3 %all_to_all.26 = f32[64,40,128]{2,1,0:T(8,128)S(1)} all-to-all(f32[64,40,128]{2,1,0:T(8,128)S(1)} %broadcast_in_dim.2), channel_id=1, replica_groups=mesh['z'=4,'y'=4,'xl'=2,'c'=2,'xh'=2] {'xl','z','y','xh'}, dimensions={0} | all-to-all | bytes 2621440 | tf_op jit(solution)/shard_map/all_to_all | solution.py:220
  155.6 0.0 copy-start.7
  155.6 3.9 %collective-permute-start.6 = (f32[2560,128]{1,0:T(8,128)S(1)}, f32[2560,128]{1,0:T(8,128)S(1)}, u32[]{:S(2)}, u32[]{:S(2)}) collective-permute-start(f32[2560,128]{1,0:T(8,128)S(1)} %bitcast.35), channel_id=1, source_target_pairs={{0,2},{2,0},{1,3},{3,1},{4,6},{6,4},{5,7},{7,5},{8,10},{10,8},{9,1... | collective-permute-start | bytes 3932168 | tf_op jit(solution)/shard_map/ppermute | solution.py:224
  159.5 2.7 %collective-permute-done.6.other = f32[2560,128]{1,0:T(8,128)S(1)} collective-permute-done((f32[2560,128]{1,0:T(8,128)S(1)}, f32[2560,128]{1,0:T(8,128)S(1)}, u32[]{:S(2)}, u32[]{:S(2)}) %collective-permute-start.6) | collective-permute-done | bytes 1310752 | tf_op jit(solution)/shard_map/ppermute | solution.py:224
  162.2 0.0 copy-start.8
  162.2 0.0 copy-done.7
  162.2 1.1 copy-done.8
  163.3 27.2 %newton.1 = (f32[56,1024]{1,0:T(8,128)}, f32[56,1024]{1,0:T(8,128)}, bf16[16,2,56,1024]{3,2,1,0:T(8,128)(2,1)}) custom-call(s32[3]{0:T(128)} %copy-done.4, f32[2560,128]{1,0:T(8,128)} %bitcast.36, f32[2560,128]{1,0:T(8,128)} %copy-done.8, f32[112,1024]{1,0:T(8,128)} %copy-done.3, f32[56,1024]{1,0:T(8,128)} %bitcast.38, f32[56,1024]{1,0:T(8,128)} %get-tuple-element.26.master_other), custom_call_target="tpu_custom_call" | custom-call | tf_op jit(solution)/shard_map/newton/pallas_call | solution.py:208
  190.5 0.0 copy-start.5
  190.5 48.8 %all_to_all.27 = bf16[16,2,56,1024]{3,2,1,0:T(8,128)(2,1)S(1)} all-to-all(bf16[16,2,56,1024]{3,2,1,0:T(8,128)(2,1)} %get-tuple-element.22), channel_id=1, replica_groups=mesh['z'=4,'y'=4,'xl'=2,'c'=2,'xh'=2] {'z','y'}, dimensions={0} | all-to-all | bytes 7340032 | tf_op jit(solution)/shard_map/all_to_all | solution.py:220
  239.3 1.5 collective-permute-start.7
  240.8 0.0 copy-done.5
  240.8 2.4 placed.2.refs_0_
  243.2 3.6 %collective-permute-done.7.piece = bf16[32,56,1024]{2,1,0:T(8,128)(2,1)S(1)} collective-permute-done((bf16[32,56,1024]{2,1,0:T(8,128)(2,1)S(1)}, bf16[32,56,1024]{2,1,0:T(8,128)(2,1)S(1)}, u32[]{:S(2)}, u32[]{:S(2)}) %collective-permute-start.7) | collective-permute-done | bytes 3670048 | tf_op jit(solution)/shard_map/ppermute | solution.py:224
  246.8 2.4 placed.3
  (1 shorter events, 0.0 us)
Async XLA Ops:
  2.3 15.3 %collective-permute-start = (bf16[16,2,56,512]{3,2,1,0:T(8,128)(2,1)S(1)}, bf16[16,2,56,512]{3,2,1,0:T(8,128)(2,1)}, u32[]{:S(2)}, u32[]{:S(2)}) collective-permute-start(bf16[16,2,56,512]{3,2,1,0:T(8,128)(2,1)S(1)} %dynamic-slice_bitcast_fusion.1.given), channel_id=1, source_target_pairs={{0,2},{2,0},{1,3},{3,1},{4,6},{6,4},{5,7},{7,5},{8,10},{10,8},{9,1... | collective-permute-start | bytes 5505032 | tf_op jit(solution)/shard_map/ppermute | solution.py:224
  3.8 3.1 %copy-start = (bf16[1,1,3584,1024]{3,2,1,0:T(8,128)(2,1)S(1)}, bf16[1,1,3584,1024]{3,2,1,0:T(8,128)(2,1)}, u32[]{:S(2)}) copy-start(bf16[1,1,3584,1024]{3,2,1,0:T(8,128)(2,1)} %param.3) | copy-start | bytes 22020100
  7.4 1.8 copy-start.1
  9.3 59.2 %all-to-all-start.1 = ((bf16[32,112,512]{2,1,0:T(8,128)(2,1)}), bf16[32,112,512]{2,1,0:T(8,128)(2,1)}, u32[]{:S(2)}, u32[]{:S(2)}) async-start(bf16[32,112,512]{2,1,0:T(8,128)(2,1)} %bitcast.27), calls=%async_computation.1 | async-start | bytes 7340032 | tf_op jit(solution)/shard_map/all_to_all | solution.py:220
  20.3 1.8 copy-start.6
  23.6 41.6 %collective-permute-start.1 = (f32[16,56,512]{2,1,0:T(8,128)}, f32[16,56,512]{2,1,0:T(8,128)S(1)}, u32[]{:S(2)}, u32[]{:S(2)}) collective-permute-start(f32[16,56,512]{2,1,0:T(8,128)} %dynamic-slice_bitcast_fusion), channel_id=1, source_target_pairs={{0,4},{4,0},{1,5},{5,1},{2,6},{6,2},{3,7},{7,3},{8,12},{12,8},{9,1... | collective-permute-start | bytes 5505032 | tf_op jit(solution)/shard_map/ppermute | solution.py:224
  68.4 10.6 %copy-start.2 = (f32[1,1,56,1024]{3,2,1,0:T(8,128)S(1)}, f32[1,1,56,1024]{3,2,1,0:T(8,128)}, u32[]{:S(2)}) copy-start(f32[1,1,56,1024]{3,2,1,0:T(8,128)} %param.5) | copy-start | bytes 688132
  68.4 10.6 %copy-start.9 = (f32[1,1,56,1024]{3,2,1,0:T(8,128)S(1)}, f32[1,1,56,1024]{3,2,1,0:T(8,128)}, u32[]{:S(2)}) copy-start(f32[1,1,56,1024]{3,2,1,0:T(8,128)} %param.4) | copy-start | bytes 688132
  68.4 31.8 %all-to-all-start = ((f32[16,56,512]{2,1,0:T(8,128)}), f32[16,56,512]{2,1,0:T(8,128)S(1)}, u32[]{:S(2)}, u32[]{:S(2)}) async-start(f32[16,56,512]{2,1,0:T(8,128)} %bitcast_add_fusion), calls=%async_computation | async-start | bytes 3670016 | tf_op jit(solution)/shard_map/all_to_all | solution.py:220
  77.7 5.7 %collective-permute-start.2 = (f32[2,56,512]{2,1,0:T(8,128)S(1)}, f32[2,56,512]{2,1,0:T(8,128)S(1)}, u32[]{:S(2)}, u32[]{:S(2)}) collective-permute-start(f32[2,56,512]{2,1,0:T(8,128)S(1)} %bitcast.32), channel_id=1, source_target_pairs={{0,4},{4,0},{1,5},{5,1},{2,6},{6,2},{3,7},{7,3},{8,12},{12,8},{9,1... | collective-permute-start | bytes 688136 | tf_op jit(solution)/shard_map/ppermute | solution.py:224
  83.4 9.6 %collective-permute-start.3 = (f32[112,1024]{1,0:T(8,128)S(1)}, f32[112,1024]{1,0:T(8,128)S(1)}, u32[]{:S(2)}, u32[]{:S(2)}) collective-permute-start(f32[112,1024]{1,0:T(8,128)S(1)} %pad_maximum_fusion), channel_id=1, source_target_pairs={{0,4},{4,0},{1,5},{5,1},{2,6},{6,2},{3,7},{7,3},{8,12},{12,8},{9,1... | collective-permute-start | bytes 1376264 | tf_op jit(solution)/shard_map/ppermute | solution.py:224
  84.7 48.5 %copy-start.4 = (s32[3]{0:T(128)}, s32[3]{0:T(128)S(1)}, u32[]{:S(2)}) copy-start(s32[3]{0:T(128)S(1)} %pad_add_fusion.place_ref.place) | copy-start | bytes 40
  100.3 3.7 %collective-permute-start.4 = (f32[56,512]{1,0:T(8,128)S(1)}, f32[56,512]{1,0:T(8,128)S(1)}, u32[]{:S(2)}, u32[]{:S(2)}) collective-permute-start(f32[56,512]{1,0:T(8,128)S(1)} %reduce_sum.28.early), channel_id=1, source_target_pairs={{0,4},{4,0},{1,5},{5,1},{2,6},{6,2},{3,7},{7,3},{8,12},{12,8},{9,1... | collective-permute-start | bytes 344072 | tf_op jit(solution)/shard_map/ppermute | solution.py:224
  107.1 6.4 %copy-start.3 = (f32[112,1024]{1,0:T(8,128)}, f32[112,1024]{1,0:T(8,128)S(1)}, u32[]{:S(2)}) copy-start(f32[112,1024]{1,0:T(8,128)S(1)} %get-tuple-element.21.direction) | copy-start | bytes 1376260
  107.1 6.3 %collective-permute-start.5 = (f32[1280,128]{1,0:T(8,128)S(1)}, f32[1280,128]{1,0:T(8,128)S(1)}, u32[]{:S(2)}, u32[]{:S(2)}) collective-permute-start(f32[1280,128]{1,0:T(8,128)S(1)} %get-tuple-element.20), channel_id=1, source_target_pairs={{0,2},{2,0},{1,3},{3,1},{4,6},{6,4},{5,7},{7,5},{8,10},{10,8},{9,1... | collective-permute-start | bytes 1966088 | tf_op jit(solution)/shard_map/ppermute | solution.py:224
  155.6 6.6 %copy-start.7 = (f32[64,40,128]{2,1,0:T(8,128)}, f32[64,40,128]{2,1,0:T(8,128)S(1)}, u32[]{:S(2)}) copy-start(f32[64,40,128]{2,1,0:T(8,128)S(1)} %all_to_all.26) | copy-start | bytes 3932164
  155.6 6.6 %collective-permute-start.6 = (f32[2560,128]{1,0:T(8,128)S(1)}, f32[2560,128]{1,0:T(8,128)S(1)}, u32[]{:S(2)}, u32[]{:S(2)}) collective-permute-start(f32[2560,128]{1,0:T(8,128)S(1)} %bitcast.35), channel_id=1, source_target_pairs={{0,2},{2,0},{1,3},{3,1},{4,6},{6,4},{5,7},{7,5},{8,10},{10,8},{9,1... | collective-permute-start | bytes 3932168 | tf_op jit(solution)/shard_map/ppermute | solution.py:224
  162.2 1.1 copy-start.8
  190.5 50.3 %copy-start.5 = (s32[3]{0:T(128)S(1)}, s32[3]{0:T(128)}, u32[]{:S(2)}) copy-start(s32[3]{0:T(128)} %copy-done.4) | copy-start | bytes 40
  239.3 7.5 %collective-permute-start.7 = (bf16[32,56,1024]{2,1,0:T(8,128)(2,1)S(1)}, bf16[32,56,1024]{2,1,0:T(8,128)(2,1)S(1)}, u32[]{:S(2)}, u32[]{:S(2)}) collective-permute-start(bf16[32,56,1024]{2,1,0:T(8,128)(2,1)S(1)} %bitcast.28), channel_id=1, source_target_pairs={{0,2},{2,0},{1,3},{3,1},{4,6},{6,4},{5,7},{7,5},{8,10},{10,8},{9,1... | collective-permute-start | bytes 11010056 | tf_op jit(solution)/shard_map/ppermute | solution.py:224

commit v4 on v3

--- a/solution.py
+++ b/solution.py
@@ -232,33 +232,81 @@
     return lax.dynamic_index_in_dim(x, index, axis, keepdims=False)
 
 
-def late_kernel(given, grads, out, sems):
-    copies = []
-    for xl in range(2):
-        for c in range(2):
-            copy = pltpu.make_async_copy(
-                grads.at[:, xl, c, :, pl.ds(WIDE, WIDE)], out.at[:, c, xl], sems.at[2 * xl + c]
-            )
-            copy.start()
-            copies.append(copy)
+def late_kernel(given, grads, out, held, sems, out_sems):
+    parts = [(xl, c) for xl in range(2) for c in range(2)]
+    into = [
+        pltpu.make_async_copy(
+            grads.at[:, xl, c, :, pl.ds(WIDE, WIDE)], held.at[2 * xl + c], sems.at[2 * xl + c]
+        )
+        for xl, c in parts
+    ]
+    away = [
+        pltpu.make_async_copy(held.at[2 * xl + c], out.at[:, c, xl], out_sems.at[2 * xl + c])
+        for xl, c in parts
+    ]
+    for copy in into:
+        copy.start()
+    for copy, back in zip(into, away):
+        copy.wait()
+        back.start()
+    for back in away:
+        back.wait()
+
+
+def late_columns(given, grads):
+    return pl.pallas_call(
+        late_kernel,
+        in_specs=[pl.BlockSpec(memory_space=pl.ANY)] * 2,
+        out_specs=pl.BlockSpec(memory_space=pltpu.HBM),
+        out_shape=jax.ShapeDtypeStruct((16, 2, 2, ROWS, WIDE), bf16),
+        scratch_shapes=[
+            pltpu.VMEM((4, 16, ROWS, WIDE), bf16),
+            pltpu.SemaphoreType.DMA((4,)),
+            pltpu.SemaphoreType.DMA((4,)),
+        ],
+        compiler_params=pltpu.CompilerParams(vmem_limit_bytes=52 * 2**20),
+        name="late_columns",
+    )(given, grads)
+
+
+def early_kernel(place, grads, swapped, kept, given, held, sems):
+    low, core = place[0], place[1]
+    copies = [
+        pltpu.make_async_copy(
+            grads.at[:, xl, core, :, pl.ds(0, WIDE)], held.at[xl], sems.at[xl]
+        )
+        for xl in range(2)
+    ]
+    for copy in copies:
+        copy.start()
     for copy in copies:
         copy.wait()
-
-
-def late_columns(given, grads):
-    return pl.pallas_call(
-        late_kernel,
-        in_specs=[pl.BlockSpec(memory_space=pl.ANY), pl.BlockSpec(memory_space=pltpu.HBM)],
-        out_specs=pl.BlockSpec(memory_space=pltpu.VMEM),
-        out_shape=jax.ShapeDtypeStruct((16, 2, 2, ROWS, WIDE), bf16),
-        scratch_shapes=[pltpu.SemaphoreType.DMA((4,))],
-        compiler_params=pltpu.CompilerParams(vmem_limit_bytes=16 * 2**20),
-        name="late_columns",
-    )(given, grads)
+    for k in range(16):
+        given[k] = held[1 - low, k].astype(f32) + swapped[k, 1 - low].astype(f32)
+    for k in range(16):
+        kept[k] = held[low, k].astype(f32) + swapped[k, low].astype(f32)
+
+
+def early_sums(place, grads, swapped):
+    whole = pl.BlockSpec(memory_space=pltpu.VMEM)
+    half = jax.ShapeDtypeStruct((16, ROWS, WIDE), f32)
+    return pl.pallas_call(
+        early_kernel,
+        in_specs=[
+            pl.BlockSpec(memory_space=pltpu.SMEM),
+            pl.BlockSpec(memory_space=pl.ANY),
+            whole,
+        ],
+        out_specs=[whole, whole],
+        out_shape=[half, half],
+        scratch_shapes=[pltpu.VMEM((2, 16, ROWS, WIDE), bf16), pltpu.SemaphoreType.DMA((2,))],
+        compiler_params=pltpu.CompilerParams(vmem_limit_bytes=48 * 2**20),
+        name="early_sums",
+    )(place, grads, swapped)
 
 
 def summed_parts(place, grads, state):
-    low, core = place[0], place[1]
+    core = place[1]
     grads = grads.reshape(16, 2, 2, ROWS, H)
 
     def left(c):
@@ -269,8 +317,8 @@
     swapped = swap(given, "c")
     late = late_columns(given, grads).reshape(32, 2 * ROWS, WIDE)
     late = exchange(late, ("z", "y", "c"))
-    early = left(core).astype(f32) + swapped.astype(f32)
-    early = pick(early, 1, low) + swap(pick(early, 1, 1 - low), "xl")
+    kept, given = early_sums(place, grads, swapped)
+    early = kept + swap(given, "xl")
     late = late.astype(f32).sum(0).reshape(2, ROWS, WIDE)
     late_given, state = lax.optimization_barrier((swap(late, "xl"), state))
     state_other = swap(state, "xl")

time: 250 us -> 243 us (0.972)
  local copies, waits for them, and re-layouts: 11.8 us -> 3.55 us
  Pallas kernels: 35.5 us -> 41.5 us
  other arithmetic: 8.83 us -> 4.61 us
    unnamed x20 -> x14, local copies, waits for them, and re-layouts: 7.85 us -> 1.08 us
    pallas_call x1 -> x2, Pallas kernels: 0.52 us -> 6.48 us  [the longest x1 3.4 us: early_sums(): pl.pallas_call(early_kernel, in_specs=[pl.BlockSpec(memory_space=pltpu.SM...]
    add x2 -> x1, other arithmetic: 5.89 us -> 1.66 us  [summed_parts(): early = kept + swap(given, 'xl')]
  transfers between devices with their start and end apart: 10 -> 10, of which waited for: 8 -> 8; matrix products, arithmetic and copies ran while one was open for 4% -> 2% of each run, Pallas kernels for 1% -> 4%
where the time goes in v4:
time: 243 us
  blocking collectives  90.8 us (37%)
  waiting for transfers between devices  69.7 us (29%)
  Pallas kernels  41.5 us (17%)
  starting transfers between devices  31.7 us (13%)
  other arithmetic  4.61 us (2%)
  local copies, waits for them, and re-layouts  3.55 us (1%)
    all_to_all x3, blocking collectives, exchange(): return lax.all_to_all(x, axes, 0, 0, tiled=True)  90.8 us
    ppermute x8, waiting for transfers between devices, swap(): return lax.ppermute(x, axis, [(0, 1), (1, 0)])  62.6 us
    pallas_call x1, Pallas kernels, newton(): pl.pallas_call(newton_kernel, in_specs=[pl.BlockSpec(memory_space=pltpu.S...  27.2 us
    ppermute x8, starting transfers between devices, swap(): return lax.ppermute(x, axis, [(0, 1), (1, 0)])  16.6 us
    all_to_all x2, starting transfers between devices, exchange(): return lax.all_to_all(x, axes, 0, 0, tiled=True)  15.1 us
    all_to_all x2, waiting for transfers between devices, exchange(): return lax.all_to_all(x, axes, 0, 0, tiled=True)  7.12 us
  transfers between devices with their start and end apart: 10, of which 8 were waited for; matrix products, arithmetic and copies ran while one was open for 2% of the time, Pallas kernels for 4%

profile of v4, /device:TPU:1, one launch (start us, length us, event | category | flops | bytes accessed | tf_op | source)
XLA Modules:
  0.0 242.8 jit_solution(2513460543359166420)
XLA Ops:
  0.6 1.7 dynamic-slice_bitcast_fusion.given
  2.3 1.5 collective-permute-start
  3.8 3.1 %late_columns.1 = bf16[16,2,2,56,512]{4,3,2,1,0:T(8,128)(2,1)} custom-call(bf16[16,2,56,512]{3,2,1,0:T(8,128)(2,1)S(1)} %dynamic-slice_bitcast_fusion.given, bf16[16,2,2,56,1024]{4,3,2,1,0:T(8,128)(2,1)} %bitcast.24), custom_call_target="tpu_custom_call" | custom-call | tf_op jit(solution)/shard_map/late_columns/pallas_call | solution.py:257
  6.9 8.4 %all-to-all-start.1 = ((bf16[32,112,512]{2,1,0:T(8,128)(2,1)}), bf16[32,112,512]{2,1,0:T(8,128)(2,1)}, u32[]{:S(2)}, u32[]{:S(2)}) async-start(bf16[32,112,512]{2,1,0:T(8,128)(2,1)} %bitcast.27), calls=%async_computation.1 | async-start | bytes 7340032 | tf_op jit(solution)/shard_map/all_to_all | solution.py:220
  15.3 0.1 pad_add_fusion.place.place_ref
  15.3 0.0 copy-start.2
  15.3 0.0 collective-permute-done.swapped
  15.3 3.4 %early_sums.1 = (f32[16,56,512]{2,1,0:T(8,128)S(1)}, f32[16,56,512]{2,1,0:T(8,128)S(1)}) custom-call(s32[3]{0:T(128)S(1)} %pad_add_fusion.place.place_ref, bf16[16,2,2,56,1024]{4,3,2,1,0:T(8,128)(2,1)} %bitcast.25, bf16[16,2,56,512]{3,2,1,0:T(8,128)(2,1)} %collective-permute-done.swapped), custom_call_target="tpu_custom_call" | custom-call | tf_op jit(solution)/shard_map/early_sums/pallas_call | solution.py:293
  18.7 1.3 collective-permute-start.1
  20.0 40.1 %collective-permute-done.1 = f32[16,56,512]{2,1,0:T(8,128)S(1)} collective-permute-done((f32[16,56,512]{2,1,0:T(8,128)S(1)}, f32[16,56,512]{2,1,0:T(8,128)S(1)}, u32[]{:S(2)}, u32[]{:S(2)}) %collective-permute-start.1) | collective-permute-done | bytes 1835040 | tf_op jit(solution)/shard_map/ppermute | solution.py:224
  60.1 1.7 add.11
  61.8 0.0 copy-start
  61.8 0.0 copy-start.6
  61.8 0.0 all-to-all-done.1
  61.8 6.8 %all-to-all-start = ((f32[16,56,512]{2,1,0:T(8,128)}), f32[16,56,512]{2,1,0:T(8,128)S(1)}, u32[]{:S(2)}, u32[]{:S(2)}) async-start(f32[16,56,512]{2,1,0:T(8,128)} %add.11), calls=%async_computation | async-start | bytes 3670016 | tf_op jit(solution)/shard_map/all_to_all | solution.py:220
  68.6 2.6 %convert_reduce_fusion = f32[112,512]{1,0:T(8,128)S(1)} fusion(bf16[32,112,512]{2,1,0:T(8,128)(2,1)} %all-to-all-done.1), kind=kLoop, calls=%fused_computation | loop fusion | flops 3612672 | bytes 3899392 | tf_op jit(solution)/shard_map/reduce_sum | solution.py:322
  71.1 1.3 collective-permute-start.2
  72.4 0.0 copy-done
  72.4 0.0 copy-done.6
  72.5 4.4 %collective-permute-done.2.late_given = f32[2,56,512]{2,1,0:T(8,128)S(1)} collective-permute-done((f32[2,56,512]{2,1,0:T(8,128)S(1)}, f32[2,56,512]{2,1,0:T(8,128)S(1)}, u32[]{:S(2)}, u32[]{:S(2)}) %collective-permute-start.2) | collective-permute-done | bytes 229408 | tf_op jit(solution)/shard_map/ppermute | solution.py:224
  76.9 1.2 collective-permute-start.3
  78.1 8.4 %collective-permute-done.3 = f32[112,1024]{1,0:T(8,128)S(1)} collective-permute-done((f32[112,1024]{1,0:T(8,128)S(1)}, f32[112,1024]{1,0:T(8,128)S(1)}, u32[]{:S(2)}, u32[]{:S(2)}) %collective-permute-start.3) | collective-permute-done | bytes 458784 | tf_op jit(solution)/shard_map/ppermute | solution.py:224
  86.5 7.1 %all-to-all-done = f32[16,56,512]{2,1,0:T(8,128)S(1)} async-done(((f32[16,56,512]{2,1,0:T(8,128)}), f32[16,56,512]{2,1,0:T(8,128)S(1)}, u32[]{:S(2)}, u32[]{:S(2)}) %all-to-all-start) | async-done | bytes 1835040 | tf_op jit(solution)/shard_map/all_to_all | solution.py:220
  93.6 0.1 reduce_sum.28.early
  93.7 1.3 collective-permute-start.4
  95.0 0.7 fusion
  95.8 1.7 collective-permute-done.4.early_other
  97.5 0.0 copy-done.2
  97.5 3.1 %direction_and_gram.1 = (f32[56,1024]{1,0:T(8,128)}, f32[112,1024]{1,0:T(8,128)S(1)}, f32[1280,128]{1,0:T(8,128)S(1)}, f32[1280,128]{1,0:T(8,128)S(1)}) custom-call(s32[3]{0:T(128)S(1)} %pad_add_fusion.place.place_ref, f32[56,512]{1,0:T(8,128)S(1)} %reduce_sum.28.early, f32[56,512]{1,0:T(8,128)S(1)} %collective-permute-done.4.early_other, ...), custom_call_target="tpu_custom_call" | custom-call | tf_op jit(solution)/shard_map/direction_and_gram/pallas_call | solution.py:93
  100.5 0.0 copy-start.1
  100.5 4.6 %collective-permute-start.5 = (f32[1280,128]{1,0:T(8,128)S(1)}, f32[1280,128]{1,0:T(8,128)S(1)}, u32[]{:S(2)}, u32[]{:S(2)}) collective-permute-start(f32[1280,128]{1,0:T(8,128)S(1)} %get-tuple-element.24), channel_id=1, source_target_pairs={{0,2},{2,0},{1,3},{3,1},{4,6},{6,4},{5,7},{7,5},{8,10},{10,8},{9,1... | collective-permute-start | bytes 1966088 | tf_op jit(solution)/shard_map/ppermute | solution.py:224
  105.1 1.7 collective-permute-done.5
  106.8 0.1 add.12
  106.9 0.0 copy-done.1
  106.9 19.7 %all_to_all.25 = f32[32,40,128]{2,1,0:T(8,128)S(1)} all-to-all(f32[32,40,128]{2,1,0:T(8,128)S(1)} %bitcast.30), channel_id=1, replica_groups=mesh['z'=4,'y'=4,'xl'=2,'c'=2,'xh'=2] {'z','y','xh'}, dimensions={0} | all-to-all | bytes 1310720 | tf_op jit(solution)/shard_map/all_to_all | solution.py:220
  126.6 0.1 reduce_sum.29
  126.6 0.1 broadcast_in_dim.2
  126.7 22.3 %all_to_all.26 = f32[64,40,128]{2,1,0:T(8,128)S(1)} all-to-all(f32[64,40,128]{2,1,0:T(8,128)S(1)} %broadcast_in_dim.2), channel_id=1, replica_groups=mesh['z'=4,'y'=4,'xl'=2,'c'=2,'xh'=2] {'xl','z','y','xh'}, dimensions={0} | all-to-all | bytes 2621440 | tf_op jit(solution)/shard_map/all_to_all | solution.py:220
  149.1 0.0 copy-start.4
  149.1 3.9 %collective-permute-start.6 = (f32[2560,128]{1,0:T(8,128)S(1)}, f32[2560,128]{1,0:T(8,128)S(1)}, u32[]{:S(2)}, u32[]{:S(2)}) collective-permute-start(f32[2560,128]{1,0:T(8,128)S(1)} %bitcast.28), channel_id=1, source_target_pairs={{0,2},{2,0},{1,3},{3,1},{4,6},{6,4},{5,7},{7,5},{8,10},{10,8},{9,1... | collective-permute-start | bytes 3932168 | tf_op jit(solution)/shard_map/ppermute | solution.py:224
  153.0 2.7 %collective-permute-done.6.other = f32[2560,128]{1,0:T(8,128)S(1)} collective-permute-done((f32[2560,128]{1,0:T(8,128)S(1)}, f32[2560,128]{1,0:T(8,128)S(1)}, u32[]{:S(2)}, u32[]{:S(2)}) %collective-permute-start.6) | collective-permute-done | bytes 1310752 | tf_op jit(solution)/shard_map/ppermute | solution.py:224
  155.6 0.0 copy-start.5
  155.6 0.0 copy-done.4
  155.6 1.1 copy-done.5
  156.7 27.2 %newton.1 = (f32[56,1024]{1,0:T(8,128)}, f32[56,1024]{1,0:T(8,128)}, bf16[16,2,56,1024]{3,2,1,0:T(8,128)(2,1)}) custom-call(s32[3]{0:T(128)} %copy-done.2, f32[2560,128]{1,0:T(8,128)} %bitcast.29, f32[2560,128]{1,0:T(8,128)} %copy-done.5, f32[112,1024]{1,0:T(8,128)} %copy-done.1, f32[56,1024]{1,0:T(8,128)} %bitcast.31, f32[56,1024]{1,0:T(8,128)} %get-tuple-element.30.master_other), custom_call_target="tpu_custom_call" | custom-call | tf_op jit(solution)/shard_map/newton/pallas_call | solution.py:208
  183.9 0.0 copy-start.3
  183.9 48.8 %all_to_all.27 = bf16[16,2,56,1024]{3,2,1,0:T(8,128)(2,1)S(1)} all-to-all(bf16[16,2,56,1024]{3,2,1,0:T(8,128)(2,1)} %get-tuple-element.26), channel_id=1, replica_groups=mesh['z'=4,'y'=4,'xl'=2,'c'=2,'xh'=2] {'z','y'}, dimensions={0} | all-to-all | bytes 7340032 | tf_op jit(solution)/shard_map/all_to_all | solution.py:220
  232.7 1.5 collective-permute-start.7
  234.2 0.0 copy-done.3
  234.2 2.4 placed.2.refs_0_
  236.6 3.6 %collective-permute-done.7.piece = bf16[32,56,1024]{2,1,0:T(8,128)(2,1)S(1)} collective-permute-done((bf16[32,56,1024]{2,1,0:T(8,128)(2,1)S(1)}, bf16[32,56,1024]{2,1,0:T(8,128)(2,1)S(1)}, u32[]{:S(2)}, u32[]{:S(2)}) %collective-permute-start.7) | collective-permute-done | bytes 3670048 | tf_op jit(solution)/shard_map/ppermute | solution.py:224
  240.2 2.4 placed.3
  (1 shorter events, 0.0 us)
Async XLA Ops:
  2.3 13.0 %collective-permute-start = (bf16[16,2,56,512]{3,2,1,0:T(8,128)(2,1)S(1)}, bf16[16,2,56,512]{3,2,1,0:T(8,128)(2,1)}, u32[]{:S(2)}, u32[]{:S(2)}) collective-permute-start(bf16[16,2,56,512]{3,2,1,0:T(8,128)(2,1)S(1)} %dynamic-slice_bitcast_fusion.given), channel_id=1, source_target_pairs={{0,2},{2,0},{1,3},{3,1},{4,6},{6,4},{5,7},{7,5},{8,10},{10,8},{9,1... | collective-permute-start | bytes 5505032 | tf_op jit(solution)/shard_map/ppermute | solution.py:224
  6.9 54.9 %all-to-all-start.1 = ((bf16[32,112,512]{2,1,0:T(8,128)(2,1)}), bf16[32,112,512]{2,1,0:T(8,128)(2,1)}, u32[]{:S(2)}, u32[]{:S(2)}) async-start(bf16[32,112,512]{2,1,0:T(8,128)(2,1)} %bitcast.27), calls=%async_computation.1 | async-start | bytes 7340032 | tf_op jit(solution)/shard_map/all_to_all | solution.py:220
  15.3 82.1 %copy-start.2 = (s32[3]{0:T(128)}, s32[3]{0:T(128)S(1)}, u32[]{:S(2)}) copy-start(s32[3]{0:T(128)S(1)} %pad_add_fusion.place.place_ref) | copy-start | bytes 40
  18.7 41.4 %collective-permute-start.1 = (f32[16,56,512]{2,1,0:T(8,128)S(1)}, f32[16,56,512]{2,1,0:T(8,128)S(1)}, u32[]{:S(2)}, u32[]{:S(2)}) collective-permute-start(f32[16,56,512]{2,1,0:T(8,128)S(1)} %get-tuple-element.18), channel_id=1, source_target_pairs={{0,4},{4,0},{1,5},{5,1},{2,6},{6,2},{3,7},{7,3},{8,12},{12,8},{9,1... | collective-permute-start | bytes 5505032 | tf_op jit(solution)/shard_map/ppermute | solution.py:224
  61.8 10.6 %copy-start = (f32[1,1,56,1024]{3,2,1,0:T(8,128)S(1)}, f32[1,1,56,1024]{3,2,1,0:T(8,128)}, u32[]{:S(2)}) copy-start(f32[1,1,56,1024]{3,2,1,0:T(8,128)} %param.5) | copy-start | bytes 688132
  61.8 10.6 %copy-start.6 = (f32[1,1,56,1024]{3,2,1,0:T(8,128)S(1)}, f32[1,1,56,1024]{3,2,1,0:T(8,128)}, u32[]{:S(2)}) copy-start(f32[1,1,56,1024]{3,2,1,0:T(8,128)} %param.4) | copy-start | bytes 688132
  61.8 31.8 %all-to-all-start = ((f32[16,56,512]{2,1,0:T(8,128)}), f32[16,56,512]{2,1,0:T(8,128)S(1)}, u32[]{:S(2)}, u32[]{:S(2)}) async-start(f32[16,56,512]{2,1,0:T(8,128)} %add.11), calls=%async_computation | async-start | bytes 3670016 | tf_op jit(solution)/shard_map/all_to_all | solution.py:220
  71.1 5.7 %collective-permute-start.2 = (f32[2,56,512]{2,1,0:T(8,128)S(1)}, f32[2,56,512]{2,1,0:T(8,128)S(1)}, u32[]{:S(2)}, u32[]{:S(2)}) collective-permute-start(f32[2,56,512]{2,1,0:T(8,128)S(1)} %bitcast.21), channel_id=1, source_target_pairs={{0,4},{4,0},{1,5},{5,1},{2,6},{6,2},{3,7},{7,3},{8,12},{12,8},{9,1... | collective-permute-start | bytes 688136 | tf_op jit(solution)/shard_map/ppermute | solution.py:224
  76.9 9.6 %collective-permute-start.3 = (f32[112,1024]{1,0:T(8,128)S(1)}, f32[112,1024]{1,0:T(8,128)S(1)}, u32[]{:S(2)}, u32[]{:S(2)}) collective-permute-start(f32[112,1024]{1,0:T(8,128)S(1)} %pad_maximum_fusion), channel_id=1, source_target_pairs={{0,4},{4,0},{1,5},{5,1},{2,6},{6,2},{3,7},{7,3},{8,12},{12,8},{9,1... | collective-permute-start | bytes 1376264 | tf_op jit(solution)/shard_map/ppermute | solution.py:224
  93.7 3.7 %collective-permute-start.4 = (f32[56,512]{1,0:T(8,128)S(1)}, f32[56,512]{1,0:T(8,128)S(1)}, u32[]{:S(2)}, u32[]{:S(2)}) collective-permute-start(f32[56,512]{1,0:T(8,128)S(1)} %reduce_sum.28.early), channel_id=1, source_target_pairs={{0,4},{4,0},{1,5},{5,1},{2,6},{6,2},{3,7},{7,3},{8,12},{12,8},{9,1... | collective-permute-start | bytes 344072 | tf_op jit(solution)/shard_map/ppermute | solution.py:224
  100.5 6.4 %copy-start.1 = (f32[112,1024]{1,0:T(8,128)}, f32[112,1024]{1,0:T(8,128)S(1)}, u32[]{:S(2)}) copy-start(f32[112,1024]{1,0:T(8,128)S(1)} %get-tuple-element.25.direction) | copy-start | bytes 1376260
  100.5 6.3 %collective-permute-start.5 = (f32[1280,128]{1,0:T(8,128)S(1)}, f32[1280,128]{1,0:T(8,128)S(1)}, u32[]{:S(2)}, u32[]{:S(2)}) collective-permute-start(f32[1280,128]{1,0:T(8,128)S(1)} %get-tuple-element.24), channel_id=1, source_target_pairs={{0,2},{2,0},{1,3},{3,1},{4,6},{6,4},{5,7},{7,5},{8,10},{10,8},{9,1... | collective-permute-start | bytes 1966088 | tf_op jit(solution)/shard_map/ppermute | solution.py:224
  149.1 6.6 %copy-start.4 = (f32[64,40,128]{2,1,0:T(8,128)}, f32[64,40,128]{2,1,0:T(8,128)S(1)}, u32[]{:S(2)}) copy-start(f32[64,40,128]{2,1,0:T(8,128)S(1)} %all_to_all.26) | copy-start | bytes 3932164
  149.1 6.6 %collective-permute-start.6 = (f32[2560,128]{1,0:T(8,128)S(1)}, f32[2560,128]{1,0:T(8,128)S(1)}, u32[]{:S(2)}, u32[]{:S(2)}) collective-permute-start(f32[2560,128]{1,0:T(8,128)S(1)} %bitcast.28), channel_id=1, source_target_pairs={{0,2},{2,0},{1,3},{3,1},{4,6},{6,4},{5,7},{7,5},{8,10},{10,8},{9,1... | collective-permute-start | bytes 3932168 | tf_op jit(solution)/shard_map/ppermute | solution.py:224
  155.6 1.1 copy-start.5
  183.9 50.3 %copy-start.3 = (s32[3]{0:T(128)S(1)}, s32[3]{0:T(128)}, u32[]{:S(2)}) copy-start(s32[3]{0:T(128)} %copy-done.2) | copy-start | bytes 40
  232.7 7.5 %collective-permute-start.7 = (bf16[32,56,1024]{2,1,0:T(8,128)(2,1)S(1)}, bf16[32,56,1024]{2,1,0:T(8,128)(2,1)S(1)}, u32[]{:S(2)}, u32[]{:S(2)}) collective-permute-start(bf16[32,56,1024]{2,1,0:T(8,128)(2,1)S(1)} %bitcast.17), channel_id=1, source_target_pairs={{0,2},{2,0},{1,3},{3,1},{4,6},{6,4},{5,7},{7,5},{8,10},{10,8},{9,1... | collective-permute-start | bytes 11010056 | tf_op jit(solution)/shard_map/ppermute | solution.py:224

commit v5 on v4

--- a/solution.py
+++ b/solution.py
@@ -102,7 +102,7 @@
 
 def newton_kernel(
     place_ref, mine, other, direction, master, master_other,
-    update, new_master, pairs, gram, g_hi, g_lo, p_hi, p_lo,
+    update, new_master, left, right, gram, g_hi, g_lo, p_hi, p_lo,
 ):
     n = H // BLOCK
     spans = [slice(i * BLOCK, (i + 1) * BLOCK) for i in range(n)]
@@ -197,9 +197,10 @@
     weights = moved.astype(bf16)
     weights_other = stepped(master_other[...], result[ROWS:]).astype(bf16)
     low = place_ref[0]
-    for i in range(16):
-        pairs[i, low] = weights
-        pairs[i, 1 - low] = weights_other
+    for at, value in ((low, weights), (1 - low, weights_other)):
+        for i in range(4):
+            left[i, at] = value[:, :WIDE]
+        right[at] = value[:, WIDE:]
 
 
 def newton(place, *operands):
@@ -208,8 +209,13 @@
     return pl.pallas_call(
         newton_kernel,
         in_specs=[pl.BlockSpec(memory_space=pltpu.SMEM)] + [whole] * 5,
-        out_specs=[whole] * 3,
-        out_shape=[row, row, jax.ShapeDtypeStruct((16, 2, ROWS, H), bf16)],
+        out_specs=[whole] * 4,
+        out_shape=[
+            row,
+            row,
+            jax.ShapeDtypeStruct((4, 2, ROWS, WIDE), bf16),
+            jax.ShapeDtypeStruct((2, ROWS, WIDE), bf16),
+        ],
         scratch_shapes=[pltpu.VMEM((H, H), f32)] + [pltpu.VMEM((H, H), bf16)] * 4,
         compiler_params=pltpu.CompilerParams(vmem_limit_bytes=56 * 2**20),
         name="newton",
@@ -357,8 +363,56 @@
     )(place, piece, *rest)
 
 
-def gathered(place, pairs):
-    mine = exchange(pairs, ("z", "y")).reshape(32, ROWS, H)
+def terms_along(x, axis):
+    return [x] + [lax.ppermute(x, axis, [(i, (i + by) % 4) for i in range(4)]) for by in (1, 2, 3)]
+
+
+def collect_kernel(place, *refs):
+    *terms, out = refs
+    for by, term in enumerate(terms):
+        out[lax.rem(place[3] + 4 - by, 4)] = term[...]
+
+
+def collected(place, x):
+    whole = pl.BlockSpec(memory_space=pltpu.VMEM)
+    return pl.pallas_call(
+        collect_kernel,
+        in_specs=[pl.BlockSpec(memory_space=pltpu.SMEM)] + [whole] * 4,
+        out_specs=whole,
+        out_shape=jax.ShapeDtypeStruct((4,) + x.shape, x.dtype),
+        compiler_params=pltpu.CompilerParams(vmem_limit_bytes=24 * 2**20),
+        name="collected",
+    )(place, *terms_along(x, "z"))
+
+
+def join_kernel(place, left, *refs):
+    *terms, out = refs
+    for z in range(4):
+        for y in range(4):
+            out[z, y, :, :, :WIDE] = left[z, y]
+        for by, term in enumerate(terms):
+            out[z, lax.rem(place[4] + 4 - by, 4), :, :, WIDE:] = term[z]
+
+
+def joined(place, left, right):
+    whole = pl.BlockSpec(memory_space=pltpu.VMEM)
+    return pl.pallas_call(
+        join_kernel,
+        in_specs=[pl.BlockSpec(memory_space=pltpu.SMEM)] + [whole] * 5,
+        out_specs=whole,
+        out_shape=jax.ShapeDtypeStruct((4, 4, 2, ROWS, H), bf16),
+        compiler_params=pltpu.CompilerParams(vmem_limit_bytes=24 * 2**20),
+        name="joined",
+    )(place, left, *right)
+
+
+def gathered(place, left, right):
+    right = collected(place, right)
+    left = exchange(left, "y")
+    right, left = lax.optimization_barrier((right, left))
+    right = terms_along(right, "y")
+    left = exchange(repeat(left, 4), "z")
+    mine = joined(place, left, right).reshape(32, ROWS, H)
     other = swap(mine, "c")
     whole = placed(place, other, 2, placed(place, mine, 1))
     return whole.reshape(1, N_DP * ROWS, H)
@@ -366,7 +420,8 @@
 
 def shards(grad_parts, master, momentum):
     core, low = lax.axis_index("c"), lax.axis_index("xl")
-    place = jnp.stack([low, core, 1 - core]).astype(jnp.int32)
+    place = jnp.stack([low, core, 1 - core, lax.axis_index("z"), lax.axis_index("y")])
+    place = place.astype(jnp.int32)
     shape = master.shape
     master = master.reshape(ROWS, H)
     momentum = momentum.reshape(ROWS, H)
@@ -375,11 +430,11 @@
         place, *sums, momentum, state_other[:ROWS]
     )
     mine, other = summed_gram(kept, given)
-    update, new_master, pairs = newton(
+    update, new_master, left, right = newton(
         place, mine, other, direction, master, state_other[ROWS:]
     )
     return (
-        gathered(place, pairs),
+        gathered(place, left, right),
         new_momentum.reshape(shape),
         new_master.reshape(shape),
         update.reshape(shape),

time: 243 us -> 241 us (level)
  blocking collectives: 90.8 us -> 42 us
  waiting for transfers between devices: 69.7 us -> 99.2 us
  starting transfers between devices: 31.7 us -> 43.6 us
  local copies, waits for them, and re-layouts: 3.55 us -> 7.8 us
    all_to_all x3 -> x2, blocking collectives: 90.8 us -> 42 us  [exchange(): return lax.all_to_all(x, axes, 0, 0, tiled=True)]
    ppermute x0 -> x6, waiting for transfers between devices: none -> 29.5 us  [terms_along(): lax.ppermute(x, axis, [(i, (i + by) % 4) for i in range(4)])]
    all_to_all x2 -> x4, starting transfers between devices: 15.1 us -> 22 us  [exchange(): return lax.all_to_all(x, axes, 0, 0, tiled=True)]
    ppermute x0 -> x6, starting transfers between devices: none -> 5.97 us  [terms_along(): lax.ppermute(x, axis, [(i, (i + by) % 4) for i in range(4)])]
    unnamed x14 -> x20, local copies, waits for them, and re-layouts: 1.08 us -> 3.79 us
    all_to_all x2 -> x4, waiting for transfers between devices: 7.12 us -> 7.05 us  [exchange(): return lax.all_to_all(x, axes, 0, 0, tiled=True)]
  transfers between devices with their start and end apart: 10 -> 18, of which waited for: 8 -> 14; matrix products, arithmetic and copies ran while one was open for 2% -> 2% of each run, Pallas kernels for 4% -> 4%
where the time goes in v5:
time: 241 us; the launch traced here: 240 us
  waiting for transfers between devices  99.2 us (41%)
  starting transfers between devices  43.6 us (18%)
  blocking collectives  42 us (17%)
  Pallas kernels  41.7 us (17%)
  local copies, waits for them, and re-layouts  7.8 us (3%)
  other arithmetic  4.57 us (2%)
    ppermute x8, waiting for transfers between devices, swap(): return lax.ppermute(x, axis, [(0, 1), (1, 0)])  62.6 us
    all_to_all x2, blocking collectives, exchange(): return lax.all_to_all(x, axes, 0, 0, tiled=True)  42 us
    ppermute x6, waiting for transfers between devices, terms_along(): lax.ppermute(x, axis, [(i, (i + by) % 4) for i in range(4)])  29.5 us
    pallas_call x1, Pallas kernels, newton(): pl.pallas_call(newton_kernel, in_specs=[pl.BlockSpec(memory_space=pltpu.S...  26 us
    all_to_all x4, starting transfers between devices, exchange(): return lax.all_to_all(x, axes, 0, 0, tiled=True)  22 us
    ppermute x8, starting transfers between devices, swap(): return lax.ppermute(x, axis, [(0, 1), (1, 0)])  15.7 us
    all_to_all x4, waiting for transfers between devices, exchange(): return lax.all_to_all(x, axes, 0, 0, tiled=True)  7.05 us
    ppermute x6, starting transfers between devices, terms_along(): lax.ppermute(x, axis, [(i, (i + by) % 4) for i in range(4)])  5.97 us
  transfers between devices with their start and end apart: 18, of which 14 were waited for; matrix products, arithmetic and copies ran while one was open for 2% of the time, Pallas kernels for 4%

profile of v5, /device:TPU:1, one launch (start us, length us, event | category | flops | bytes accessed | tf_op | source)
XLA Modules:
  0.0 239.9 jit_solution(13631033635880862416)
XLA Ops:
  0.6 1.7 dynamic-slice_bitcast_fusion.given
  2.3 1.5 collective-permute-start
  3.8 3.1 %late_columns.1 = bf16[16,2,2,56,512]{4,3,2,1,0:T(8,128)(2,1)} custom-call(bf16[16,2,56,512]{3,2,1,0:T(8,128)(2,1)S(1)} %dynamic-slice_bitcast_fusion.given, bf16[16,2,2,56,1024]{4,3,2,1,0:T(8,128)(2,1)} %bitcast.26), custom_call_target="tpu_custom_call" | custom-call | tf_op jit(solution)/shard_map/late_columns/pallas_call | solution.py:263
  6.9 8.4 %all-to-all-start.1 = ((bf16[32,112,512]{2,1,0:T(8,128)(2,1)}), bf16[32,112,512]{2,1,0:T(8,128)(2,1)}, u32[]{:S(2)}, u32[]{:S(2)}) async-start(bf16[32,112,512]{2,1,0:T(8,128)(2,1)} %bitcast.29), calls=%async_computation.1 | async-start | bytes 7340032 | tf_op jit(solution)/shard_map/all_to_all | solution.py:226
  15.3 0.1 stack.23.place.place_ref
  15.4 0.0 collective-permute-done.swapped
  15.4 3.4 %early_sums.1 = (f32[16,56,512]{2,1,0:T(8,128)S(1)}, f32[16,56,512]{2,1,0:T(8,128)S(1)}) custom-call(s32[5]{0:T(128)S(1)} %stack.23.place.place_ref, bf16[16,2,2,56,1024]{4,3,2,1,0:T(8,128)(2,1)} %bitcast.27, bf16[16,2,56,512]{3,2,1,0:T(8,128)(2,1)} %collective-permute-done.swapped), custom_call_target="tpu_custom_call" | custom-call | tf_op jit(solution)/shard_map/early_sums/pallas_call | solution.py:299
  18.8 1.3 collective-permute-start.1
  20.0 40.1 %collective-permute-done.1 = f32[16,56,512]{2,1,0:T(8,128)S(1)} collective-permute-done((f32[16,56,512]{2,1,0:T(8,128)S(1)}, f32[16,56,512]{2,1,0:T(8,128)S(1)}, u32[]{:S(2)}, u32[]{:S(2)}) %collective-permute-start.1) | collective-permute-done | bytes 1835040 | tf_op jit(solution)/shard_map/ppermute | solution.py:230
  60.1 1.7 add.11
  61.8 0.0 all-to-all-done.1
  61.8 6.6 %all-to-all-start = ((f32[16,56,512]{2,1,0:T(8,128)}), f32[16,56,512]{2,1,0:T(8,128)S(1)}, u32[]{:S(2)}, u32[]{:S(2)}) async-start(f32[16,56,512]{2,1,0:T(8,128)} %add.11), calls=%async_computation | async-start | bytes 3670016 | tf_op jit(solution)/shard_map/all_to_all | solution.py:226
  68.4 0.0 copy-start
  68.4 0.0 copy-start.9
  68.5 2.6 %convert_reduce_fusion = f32[112,512]{1,0:T(8,128)S(1)} fusion(bf16[32,112,512]{2,1,0:T(8,128)(2,1)} %all-to-all-done.1), kind=kLoop, calls=%fused_computation | loop fusion | flops 3612672 | bytes 3899392 | tf_op jit(solution)/shard_map/reduce_sum | solution.py:328
  71.1 1.3 collective-permute-start.2
  72.4 0.0 copy-done.9
  72.4 4.4 %collective-permute-done.2.late_given = f32[2,56,512]{2,1,0:T(8,128)S(1)} collective-permute-done((f32[2,56,512]{2,1,0:T(8,128)S(1)}, f32[2,56,512]{2,1,0:T(8,128)S(1)}, u32[]{:S(2)}, u32[]{:S(2)}) %collective-permute-start.2) | collective-permute-done | bytes 229408 | tf_op jit(solution)/shard_map/ppermute | solution.py:230
  76.8 1.2 collective-permute-start.3
  78.0 8.4 %collective-permute-done.3 = f32[112,1024]{1,0:T(8,128)S(1)} collective-permute-done((f32[112,1024]{1,0:T(8,128)S(1)}, f32[112,1024]{1,0:T(8,128)S(1)}, u32[]{:S(2)}, u32[]{:S(2)}) %collective-permute-start.3) | collective-permute-done | bytes 458784 | tf_op jit(solution)/shard_map/ppermute | solution.py:230
  86.4 7.0 %all-to-all-done = f32[16,56,512]{2,1,0:T(8,128)S(1)} async-done(((f32[16,56,512]{2,1,0:T(8,128)}), f32[16,56,512]{2,1,0:T(8,128)S(1)}, u32[]{:S(2)}, u32[]{:S(2)}) %all-to-all-start) | async-done | bytes 1835040 | tf_op jit(solution)/shard_map/all_to_all | solution.py:226
  93.5 0.1 reduce_sum.28.early
  93.6 1.3 collective-permute-start.4
  94.9 0.7 fusion
  95.6 1.7 collective-permute-done.4.early_other
  97.3 0.0 copy-done.5
  97.3 3.1 %direction_and_gram.1 = (f32[56,1024]{1,0:T(8,128)}, f32[112,1024]{1,0:T(8,128)S(1)}, f32[1280,128]{1,0:T(8,128)S(1)}, f32[1280,128]{1,0:T(8,128)S(1)}) custom-call(s32[5]{0:T(128)S(1)} %stack.23.place.place_ref, f32[56,512]{1,0:T(8,128)S(1)} %reduce_sum.28.early, f32[56,512]{1,0:T(8,128)S(1)} %collective-permute-done.4.early_other, ...), custom_call_target="tpu_custom_call" | custom-call | tf_op jit(solution)/shard_map/direction_and_gram/pallas_call | solution.py:93
  100.4 4.6 %collective-permute-start.5 = (f32[1280,128]{1,0:T(8,128)S(1)}, f32[1280,128]{1,0:T(8,128)S(1)}, u32[]{:S(2)}, u32[]{:S(2)}) collective-permute-start(f32[1280,128]{1,0:T(8,128)S(1)} %get-tuple-element.27), channel_id=1, source_target_pairs={{0,2},{2,0},{1,3},{3,1},{4,6},{6,4},{5,7},{7,5},{8,10},{10,8},{9,1... | collective-permute-start | bytes 1966088 | tf_op jit(solution)/shard_map/ppermute | solution.py:230
  105.0 1.7 collective-permute-done.5
  106.7 0.1 add.12
  106.8 19.7 %all_to_all.30 = f32[32,40,128]{2,1,0:T(8,128)S(1)} all-to-all(f32[32,40,128]{2,1,0:T(8,128)S(1)} %bitcast.32), channel_id=1, replica_groups=mesh['z'=4,'y'=4,'xl'=2,'c'=2,'xh'=2] {'z','y','xh'}, dimensions={0} | all-to-all | bytes 1310720 | tf_op jit(solution)/shard_map/all_to_all | solution.py:226
  126.4 0.1 reduce_sum.29
  126.5 0.1 broadcast_in_dim.4
  126.6 22.3 %all_to_all.31 = f32[64,40,128]{2,1,0:T(8,128)S(1)} all-to-all(f32[64,40,128]{2,1,0:T(8,128)S(1)} %broadcast_in_dim.4), channel_id=1, replica_groups=mesh['z'=4,'y'=4,'xl'=2,'c'=2,'xh'=2] {'xl','z','y','xh'}, dimensions={0} | all-to-all | bytes 2621440 | tf_op jit(solution)/shard_map/all_to_all | solution.py:226
  148.9 3.9 %collective-permute-start.6 = (f32[2560,128]{1,0:T(8,128)S(1)}, f32[2560,128]{1,0:T(8,128)S(1)}, u32[]{:S(2)}, u32[]{:S(2)}) collective-permute-start(f32[2560,128]{1,0:T(8,128)S(1)} %bitcast.30), channel_id=1, source_target_pairs={{0,2},{2,0},{1,3},{3,1},{4,6},{6,4},{5,7},{7,5},{8,10},{10,8},{9,1... | collective-permute-start | bytes 3932168 | tf_op jit(solution)/shard_map/ppermute | solution.py:230
  152.8 2.7 %collective-permute-done.6.other = f32[2560,128]{1,0:T(8,128)S(1)} collective-permute-done((f32[2560,128]{1,0:T(8,128)S(1)}, f32[2560,128]{1,0:T(8,128)S(1)}, u32[]{:S(2)}, u32[]{:S(2)}) %collective-permute-start.6) | collective-permute-done | bytes 1310752 | tf_op jit(solution)/shard_map/ppermute | solution.py:230
  155.5 1.1 copy-done.8
  156.6 26.0 %newton.1 = (f32[56,1024]{1,0:T(8,128)}, f32[56,1024]{1,0:T(8,128)}, bf16[4,2,56,512]{3,2,1,0:T(8,128)(2,1)}, bf16[2,56,512]{2,1,0:T(8,128)(2,1)}) custom-call(s32[5]{0:T(128)} %copy-done.5, f32[2560,128]{1,0:T(8,128)} %bitcast.31, f32[2560,128]{1,0:T(8,128)} %copy-done.8, f32[112,1024]{1,0:T(8,128)} %copy-done.3, f32[56,1024]{1,0:T(8,128)} %bitcast.33, ...), custom_call_target="tpu_custom_call" | custom-call | tf_op jit(solution)/shard_map/newton/pallas_call | solution.py:209
  182.6 3.5 %all-to-all-start.4 = ((bf16[4,2,56,512]{3,2,1,0:T(8,128)(2,1)}), bf16[4,2,56,512]{3,2,1,0:T(8,128)(2,1)S(1)}, u32[]{:S(2)}, u32[]{:S(2)}) async-start(bf16[4,2,56,512]{3,2,1,0:T(8,128)(2,1)} %get-tuple-element.30), calls=%async_computation.4 | async-start | bytes 917504 | tf_op jit(solution)/shard_map/all_to_all | solution.py:226
  186.1 0.5 collective-permute-start.9
  186.6 1.6 collective-permute-start.8
  188.1 0.3 collective-permute-start.7
  188.4 2.3 collective-permute-done.9.refs_3_
  190.7 1.6 collective-permute-done.8.refs_2_
  192.3 3.0 %collective-permute-done.7.refs_1_ = bf16[2,56,512]{2,1,0:T(8,128)(2,1)S(1)} collective-permute-done((bf16[2,56,512]{2,1,0:T(8,128)(2,1)}, bf16[2,56,512]{2,1,0:T(8,128)(2,1)S(1)}, u32[]{:S(2)}, u32[]{:S(2)}) %collective-permute-start.7) | collective-permute-done | bytes 114720 | tf_op jit(solution)/shard_map/ppermute | solution.py:367
  195.3 0.9 copy-done.4
  196.2 0.6 collected.1.refs_0_
  196.8 0.0 all-to-all-done.4
  196.8 1.4 broadcast_in_dim.5
  198.2 3.6 %all-to-all-start.5 = ((bf16[4,4,2,56,512]{4,3,2,1,0:T(8,128)(2,1)}), bf16[4,4,2,56,512]{4,3,2,1,0:T(8,128)(2,1)S(1)}, u32[]{:S(2)}, u32[]{:S(2)}) async-start(bf16[4,4,2,56,512]{4,3,2,1,0:T(8,128)(2,1)} %broadcast_in_dim.5), calls=%async_computation.5 | async-start | bytes 3670016 | tf_op jit(solution)/shard_map/all_to_all | solution.py:226
  201.8 2.5 %collective-permute-start.12 = (bf16[4,2,56,512]{3,2,1,0:T(8,128)(2,1)S(1)}, bf16[4,2,56,512]{3,2,1,0:T(8,128)(2,1)S(1)}, u32[]{:S(2)}, u32[]{:S(2)}) collective-permute-start(bf16[4,2,56,512]{3,2,1,0:T(8,128)(2,1)S(1)} %collected.1.refs_0_), channel_id=1, source_target_pairs={{0,24},{8,0},{16,8},{24,16},{1,25},{9,1},{17,9},{25,17},{2,26},{10... | collective-permute-start | bytes 1376264 | tf_op jit(solution)/shard_map/ppermute | solution.py:367
  204.3 0.6 collective-permute-start.11
  204.9 0.6 collective-permute-start.10
  205.5 7.9 %collective-permute-done.12.refs_3_ = bf16[4,2,56,512]{3,2,1,0:T(8,128)(2,1)S(1)} collective-permute-done((bf16[4,2,56,512]{3,2,1,0:T(8,128)(2,1)S(1)}, bf16[4,2,56,512]{3,2,1,0:T(8,128)(2,1)S(1)}, u32[]{:S(2)}, u32[]{:S(2)}) %collective-permute-start.12) | collective-permute-done | bytes 458784 | tf_op jit(solution)/shard_map/ppermute | solution.py:367
  213.4 3.0 %collective-permute-done.11.refs_2_ = bf16[4,2,56,512]{3,2,1,0:T(8,128)(2,1)S(1)} collective-permute-done((bf16[4,2,56,512]{3,2,1,0:T(8,128)(2,1)S(1)}, bf16[4,2,56,512]{3,2,1,0:T(8,128)(2,1)S(1)}, u32[]{:S(2)}, u32[]{:S(2)}) %collective-permute-start.11) | collective-permute-done | bytes 458784 | tf_op jit(solution)/shard_map/ppermute | solution.py:367
  216.4 11.7 %collective-permute-done.10.refs_1_ = bf16[4,2,56,512]{3,2,1,0:T(8,128)(2,1)S(1)} collective-permute-done((bf16[4,2,56,512]{3,2,1,0:T(8,128)(2,1)S(1)}, bf16[4,2,56,512]{3,2,1,0:T(8,128)(2,1)S(1)}, u32[]{:S(2)}, u32[]{:S(2)}) %collective-permute-start.10) | collective-permute-done | bytes 458784 | tf_op jit(solution)/shard_map/ppermute | solution.py:367
  228.1 0.8 copy-done.1
  228.9 0.0 all-to-all-done.5.left
  228.9 1.0 copy-done.2
  229.9 0.8 joined.1
  230.7 0.6 collective-permute-start.13
  231.3 2.4 placed.2.refs_0_
  233.7 3.6 %collective-permute-done.13.piece = bf16[32,56,1024]{2,1,0:T(8,128)(2,1)S(1)} collective-permute-done((bf16[32,56,1024]{2,1,0:T(8,128)(2,1)S(1)}, bf16[32,56,1024]{2,1,0:T(8,128)(2,1)S(1)}, u32[]{:S(2)}, u32[]{:S(2)}) %collective-permute-start.13) | collective-permute-done | bytes 3670048 | tf_op jit(solution)/shard_map/ppermute | solution.py:230
  237.3 2.4 placed.3
  (13 shorter events, 0.1 us)
Async XLA Ops:
  2.3 13.1 %collective-permute-start = (bf16[16,2,56,512]{3,2,1,0:T(8,128)(2,1)S(1)}, bf16[16,2,56,512]{3,2,1,0:T(8,128)(2,1)}, u32[]{:S(2)}, u32[]{:S(2)}) collective-permute-start(bf16[16,2,56,512]{3,2,1,0:T(8,128)(2,1)S(1)} %dynamic-slice_bitcast_fusion.given), channel_id=1, source_target_pairs={{0,2},{2,0},{1,3},{3,1},{4,6},{6,4},{5,7},{7,5},{8,10},{10,8},{9,1... | collective-permute-start | bytes 5505032 | tf_op jit(solution)/shard_map/ppermute | solution.py:230
  6.9 54.9 %all-to-all-start.1 = ((bf16[32,112,512]{2,1,0:T(8,128)(2,1)}), bf16[32,112,512]{2,1,0:T(8,128)(2,1)}, u32[]{:S(2)}, u32[]{:S(2)}) async-start(bf16[32,112,512]{2,1,0:T(8,128)(2,1)} %bitcast.29), calls=%async_computation.1 | async-start | bytes 7340032 | tf_op jit(solution)/shard_map/all_to_all | solution.py:226
  15.3 82.0 %copy-start.5 = (s32[5]{0:T(128)}, s32[5]{0:T(128)S(1)}, u32[]{:S(2)}) copy-start(s32[5]{0:T(128)S(1)} %stack.23.place.place_ref) | copy-start | bytes 64
  18.8 41.4 %collective-permute-start.1 = (f32[16,56,512]{2,1,0:T(8,128)S(1)}, f32[16,56,512]{2,1,0:T(8,128)S(1)}, u32[]{:S(2)}, u32[]{:S(2)}) collective-permute-start(f32[16,56,512]{2,1,0:T(8,128)S(1)} %get-tuple-element.21), channel_id=1, source_target_pairs={{0,4},{4,0},{1,5},{5,1},{2,6},{6,2},{3,7},{7,3},{8,12},{12,8},{9,1... | collective-permute-start | bytes 5505032 | tf_op jit(solution)/shard_map/ppermute | solution.py:230
  61.8 31.7 %all-to-all-start = ((f32[16,56,512]{2,1,0:T(8,128)}), f32[16,56,512]{2,1,0:T(8,128)S(1)}, u32[]{:S(2)}, u32[]{:S(2)}) async-start(f32[16,56,512]{2,1,0:T(8,128)} %add.11), calls=%async_computation | async-start | bytes 3670016 | tf_op jit(solution)/shard_map/all_to_all | solution.py:226
  68.4 3.9 %copy-start = (f32[1,1,56,1024]{3,2,1,0:T(8,128)S(1)}, f32[1,1,56,1024]{3,2,1,0:T(8,128)}, u32[]{:S(2)}) copy-start(f32[1,1,56,1024]{3,2,1,0:T(8,128)} %param.5) | copy-start | bytes 688132
  68.4 3.9 %copy-start.9 = (f32[1,1,56,1024]{3,2,1,0:T(8,128)S(1)}, f32[1,1,56,1024]{3,2,1,0:T(8,128)}, u32[]{:S(2)}) copy-start(f32[1,1,56,1024]{3,2,1,0:T(8,128)} %param.4) | copy-start | bytes 688132
  71.1 5.7 %collective-permute-start.2 = (f32[2,56,512]{2,1,0:T(8,128)S(1)}, f32[2,56,512]{2,1,0:T(8,128)S(1)}, u32[]{:S(2)}, u32[]{:S(2)}) collective-permute-start(f32[2,56,512]{2,1,0:T(8,128)S(1)} %bitcast.23), channel_id=1, source_target_pairs={{0,4},{4,0},{1,5},{5,1},{2,6},{6,2},{3,7},{7,3},{8,12},{12,8},{9,1... | collective-permute-start | bytes 688136 | tf_op jit(solution)/shard_map/ppermute | solution.py:230
  76.8 9.6 %collective-permute-start.3 = (f32[112,1024]{1,0:T(8,128)S(1)}, f32[112,1024]{1,0:T(8,128)S(1)}, u32[]{:S(2)}, u32[]{:S(2)}) collective-permute-start(f32[112,1024]{1,0:T(8,128)S(1)} %pad_maximum_fusion), channel_id=1, source_target_pairs={{0,4},{4,0},{1,5},{5,1},{2,6},{6,2},{3,7},{7,3},{8,12},{12,8},{9,1... | collective-permute-start | bytes 1376264 | tf_op jit(solution)/shard_map/ppermute | solution.py:230
  93.6 3.7 %collective-permute-start.4 = (f32[56,512]{1,0:T(8,128)S(1)}, f32[56,512]{1,0:T(8,128)S(1)}, u32[]{:S(2)}, u32[]{:S(2)}) collective-permute-start(f32[56,512]{1,0:T(8,128)S(1)} %reduce_sum.28.early), channel_id=1, source_target_pairs={{0,4},{4,0},{1,5},{5,1},{2,6},{6,2},{3,7},{7,3},{8,12},{12,8},{9,1... | collective-permute-start | bytes 344072 | tf_op jit(solution)/shard_map/ppermute | solution.py:230
  100.4 6.4 %copy-start.3 = (f32[112,1024]{1,0:T(8,128)}, f32[112,1024]{1,0:T(8,128)S(1)}, u32[]{:S(2)}) copy-start(f32[112,1024]{1,0:T(8,128)S(1)} %get-tuple-element.28.direction) | copy-start | bytes 1376260
  100.4 6.3 %collective-permute-start.5 = (f32[1280,128]{1,0:T(8,128)S(1)}, f32[1280,128]{1,0:T(8,128)S(1)}, u32[]{:S(2)}, u32[]{:S(2)}) collective-permute-start(f32[1280,128]{1,0:T(8,128)S(1)} %get-tuple-element.27), channel_id=1, source_target_pairs={{0,2},{2,0},{1,3},{3,1},{4,6},{6,4},{5,7},{7,5},{8,10},{10,8},{9,1... | collective-permute-start | bytes 1966088 | tf_op jit(solution)/shard_map/ppermute | solution.py:230
  148.9 6.6 %copy-start.7 = (f32[64,40,128]{2,1,0:T(8,128)}, f32[64,40,128]{2,1,0:T(8,128)S(1)}, u32[]{:S(2)}) copy-start(f32[64,40,128]{2,1,0:T(8,128)S(1)} %all_to_all.31) | copy-start | bytes 3932164
  148.9 6.6 %collective-permute-start.6 = (f32[2560,128]{1,0:T(8,128)S(1)}, f32[2560,128]{1,0:T(8,128)S(1)}, u32[]{:S(2)}, u32[]{:S(2)}) collective-permute-start(f32[2560,128]{1,0:T(8,128)S(1)} %bitcast.30), channel_id=1, source_target_pairs={{0,2},{2,0},{1,3},{3,1},{4,6},{6,4},{5,7},{7,5},{8,10},{10,8},{9,1... | collective-permute-start | bytes 3932168 | tf_op jit(solution)/shard_map/ppermute | solution.py:230
  155.5 1.1 copy-start.8
  156.6 38.7 %copy-start.6 = (s32[5]{0:T(128)S(1)}, s32[5]{0:T(128)}, u32[]{:S(2)}) copy-start(s32[5]{0:T(128)} %copy-done.5) | copy-start | bytes 64
  182.6 14.2 %all-to-all-start.4 = ((bf16[4,2,56,512]{3,2,1,0:T(8,128)(2,1)}), bf16[4,2,56,512]{3,2,1,0:T(8,128)(2,1)S(1)}, u32[]{:S(2)}, u32[]{:S(2)}) async-start(bf16[4,2,56,512]{3,2,1,0:T(8,128)(2,1)} %get-tuple-element.30), calls=%async_computation.4 | async-start | bytes 917504 | tf_op jit(solution)/shard_map/all_to_all | solution.py:226
  186.1 4.6 %collective-permute-start.9 = (bf16[2,56,512]{2,1,0:T(8,128)(2,1)}, bf16[2,56,512]{2,1,0:T(8,128)(2,1)S(1)}, u32[]{:S(2)}, u32[]{:S(2)}) collective-permute-start(bf16[2,56,512]{2,1,0:T(8,128)(2,1)} %get-tuple-element.29.refs_0_), channel_id=1, source_target_pairs={{0,96},{32,0},{64,32},{96,64},{1,97},{33,1},{65,33},{97,65},{2,98}... | collective-permute-start | bytes 344072 | tf_op jit(solution)/shard_map/ppermute | solution.py:367
  186.6 5.8 %collective-permute-start.8 = (bf16[2,56,512]{2,1,0:T(8,128)(2,1)}, bf16[2,56,512]{2,1,0:T(8,128)(2,1)S(1)}, u32[]{:S(2)}, u32[]{:S(2)}) collective-permute-start(bf16[2,56,512]{2,1,0:T(8,128)(2,1)} %get-tuple-element.29.refs_0_), channel_id=1, source_target_pairs={{0,64},{32,96},{64,0},{96,32},{1,65},{33,97},{65,1},{97,33},{2,66}... | collective-permute-start | bytes 344072 | tf_op jit(solution)/shard_map/ppermute | solution.py:367
  188.1 7.1 %collective-permute-start.7 = (bf16[2,56,512]{2,1,0:T(8,128)(2,1)}, bf16[2,56,512]{2,1,0:T(8,128)(2,1)S(1)}, u32[]{:S(2)}, u32[]{:S(2)}) collective-permute-start(bf16[2,56,512]{2,1,0:T(8,128)(2,1)} %get-tuple-element.29.refs_0_), channel_id=1, source_target_pairs={{0,32},{32,64},{64,96},{96,0},{1,33},{33,65},{65,97},{97,1},{2,34}... | collective-permute-start | bytes 344072 | tf_op jit(solution)/shard_map/ppermute | solution.py:367
  195.3 0.9 copy-start.4
  198.2 30.6 %all-to-all-start.5 = ((bf16[4,4,2,56,512]{4,3,2,1,0:T(8,128)(2,1)}), bf16[4,4,2,56,512]{4,3,2,1,0:T(8,128)(2,1)S(1)}, u32[]{:S(2)}, u32[]{:S(2)}) async-start(bf16[4,4,2,56,512]{4,3,2,1,0:T(8,128)(2,1)} %broadcast_in_dim.5), calls=%async_computation.5 | async-start | bytes 3670016 | tf_op jit(solution)/shard_map/all_to_all | solution.py:226
  201.8 11.6 %collective-permute-start.12 = (bf16[4,2,56,512]{3,2,1,0:T(8,128)(2,1)S(1)}, bf16[4,2,56,512]{3,2,1,0:T(8,128)(2,1)S(1)}, u32[]{:S(2)}, u32[]{:S(2)}) collective-permute-start(bf16[4,2,56,512]{3,2,1,0:T(8,128)(2,1)S(1)} %collected.1.refs_0_), channel_id=1, source_target_pairs={{0,24},{8,0},{16,8},{24,16},{1,25},{9,1},{17,9},{25,17},{2,26},{10... | collective-permute-start | bytes 1376264 | tf_op jit(solution)/shard_map/ppermute | solution.py:367
  204.3 12.1 %collective-permute-start.11 = (bf16[4,2,56,512]{3,2,1,0:T(8,128)(2,1)S(1)}, bf16[4,2,56,512]{3,2,1,0:T(8,128)(2,1)S(1)}, u32[]{:S(2)}, u32[]{:S(2)}) collective-permute-start(bf16[4,2,56,512]{3,2,1,0:T(8,128)(2,1)S(1)} %collected.1.refs_0_), channel_id=1, source_target_pairs={{0,16},{8,24},{16,0},{24,8},{1,17},{9,25},{17,1},{25,9},{2,18},{10... | collective-permute-start | bytes 1376264 | tf_op jit(solution)/shard_map/ppermute | solution.py:367
  204.9 23.2 %collective-permute-start.10 = (bf16[4,2,56,512]{3,2,1,0:T(8,128)(2,1)S(1)}, bf16[4,2,56,512]{3,2,1,0:T(8,128)(2,1)S(1)}, u32[]{:S(2)}, u32[]{:S(2)}) collective-permute-start(bf16[4,2,56,512]{3,2,1,0:T(8,128)(2,1)S(1)} %collected.1.refs_0_), channel_id=1, source_target_pairs={{0,8},{8,16},{16,24},{24,0},{1,9},{9,17},{17,25},{25,1},{2,10},{10... | collective-permute-start | bytes 1376264 | tf_op jit(solution)/shard_map/ppermute | solution.py:367
  228.1 0.8 copy-start.1
  228.9 1.0 copy-start.2
  230.7 6.6 %collective-permute-start.13 = (bf16[32,56,1024]{2,1,0:T(8,128)(2,1)S(1)}, bf16[32,56,1024]{2,1,0:T(8,128)(2,1)S(1)}, u32[]{:S(2)}, u32[]{:S(2)}) collective-permute-start(bf16[32,56,1024]{2,1,0:T(8,128)(2,1)S(1)} %bitcast.19), channel_id=1, source_target_pairs={{0,2},{2,0},{1,3},{3,1},{4,6},{6,4},{5,7},{7,5},{8,10},{10,8},{9,1... | collective-permute-start | bytes 11010056 | tf_op jit(solution)/shard_map/ppermute | solution.py:230

commit v6 on v5

--- a/solution.py
+++ b/solution.py
@@ -275,40 +275,33 @@
     )(given, grads)
 
 
-def early_kernel(place, grads, swapped, kept, given, held, sems):
-    low, core = place[0], place[1]
-    copies = [
-        pltpu.make_async_copy(
-            grads.at[:, xl, core, :, pl.ds(0, WIDE)], held.at[xl], sems.at[xl]
-        )
-        for xl in range(2)
-    ]
-    for copy in copies:
-        copy.start()
-    for copy in copies:
-        copy.wait()
+def early_kernel(there, place, after, grads, swapped, out, held, sem):
+    xl = 1 - place[0] if there else place[0]
+    copy = pltpu.make_async_copy(
+        grads.at[:, xl, place[1], :, pl.ds(0, WIDE)], held, sem
+    )
+    copy.start()
+    copy.wait()
     for k in range(16):
-        given[k] = held[1 - low, k].astype(f32) + swapped[k, 1 - low].astype(f32)
-    for k in range(16):
-        kept[k] = held[low, k].astype(f32) + swapped[k, low].astype(f32)
-
-
-def early_sums(place, grads, swapped):
+        out[k] = held[k].astype(f32) + swapped[k, xl].astype(f32)
+
+
+def early_sums(there, place, after, grads, swapped):
     whole = pl.BlockSpec(memory_space=pltpu.VMEM)
-    half = jax.ShapeDtypeStruct((16, ROWS, WIDE), f32)
-    return pl.pallas_call(
-        early_kernel,
+    return pl.pallas_call(
+        functools.partial(early_kernel, there),
         in_specs=[
             pl.BlockSpec(memory_space=pltpu.SMEM),
             pl.BlockSpec(memory_space=pl.ANY),
+            pl.BlockSpec(memory_space=pl.ANY),
             whole,
         ],
-        out_specs=[whole, whole],
-        out_shape=[half, half],
-        scratch_shapes=[pltpu.VMEM((2, 16, ROWS, WIDE), bf16), pltpu.SemaphoreType.DMA((2,))],
-        compiler_params=pltpu.CompilerParams(vmem_limit_bytes=48 * 2**20),
+        out_specs=whole,
+        out_shape=jax.ShapeDtypeStruct((16, ROWS, WIDE), f32),
+        scratch_shapes=[pltpu.VMEM((16, ROWS, WIDE), bf16), pltpu.SemaphoreType.DMA],
+        compiler_params=pltpu.CompilerParams(vmem_limit_bytes=16 * 2**20),
         name="early_sums",
-    )(place, grads, swapped)
+    )(place, after, grads, swapped)
 
 
 def summed_parts(place, grads, state):
@@ -323,7 +316,8 @@
     swapped = swap(given, "c")
     late = late_columns(given, grads).reshape(32, 2 * ROWS, WIDE)
     late = exchange(late, ("z", "y", "c"))
-    kept, given = early_sums(place, grads, swapped)
+    given = early_sums(True, place, swapped, grads, swapped)
+    kept = early_sums(False, place, given, grads, swapped)
     early = kept + swap(given, "xl")
     late = late.astype(f32).sum(0).reshape(2, ROWS, WIDE)
     late_given, state = lax.optimization_barrier((swap(late, "xl"), state))

time: 241 us -> 242 us (level)
  local copies, waits for them, and re-layouts: 7.8 us -> 12.1 us
    unnamed x20 -> x22, local copies, waits for them, and re-layouts: 3.79 us -> 6.88 us
  transfers between devices with their start and end apart: 18 -> 18, of which waited for: 14 -> 14; matrix products, arithmetic and copies ran while one was open for 2% -> 2% of each run, Pallas kernels for 4% -> 3%
where the time goes in v6:
time: 242 us
  waiting for transfers between devices  98.3 us (41%)
  starting transfers between devices  43.6 us (18%)
  blocking collectives  42 us (17%)
  Pallas kernels  40.1 us (17%)
  local copies, waits for them, and re-layouts  12.1 us (5%)
  other arithmetic  4.57 us (2%)
    ppermute x8, waiting for transfers between devices, swap(): return lax.ppermute(x, axis, [(0, 1), (1, 0)])  61.7 us
    all_to_all x2, blocking collectives, exchange(): return lax.all_to_all(x, axes, 0, 0, tiled=True)  42 us
    ppermute x6, waiting for transfers between devices, terms_along(): lax.ppermute(x, axis, [(i, (i + by) % 4) for i in range(4)])  29.5 us
    pallas_call x1, Pallas kernels, newton(): pl.pallas_call(newton_kernel, in_specs=[pl.BlockSpec(memory_space=pltpu.S...  26 us
    all_to_all x4, starting transfers between devices, exchange(): return lax.all_to_all(x, axes, 0, 0, tiled=True)  21.9 us
    ppermute x8, starting transfers between devices, swap(): return lax.ppermute(x, axis, [(0, 1), (1, 0)])  15.7 us
    all_to_all x4, waiting for transfers between devices, exchange(): return lax.all_to_all(x, axes, 0, 0, tiled=True)  7.05 us
    unnamed x22, local copies, waits for them, and re-layouts  6.88 us
  transfers between devices with their start and end apart: 18, of which 14 were waited for; matrix products, arithmetic and copies ran while one was open for 2% of the time, Pallas kernels for 3%

profile of v6, /device:TPU:1, one launch (start us, length us, event | category | flops | bytes accessed | tf_op | source)
XLA Modules:
  0.0 241.6 jit_solution(10085591987281122954)
XLA Ops:
  0.6 2.9 %dynamic-slice_bitcast_fusion.given = bf16[16,2,56,512]{3,2,1,0:T(8,128)(2,1)} fusion(bf16[16,2,2,56,1024]{4,3,2,1,0:T(8,128)(2,1)} %bitcast.19, s32[]{:T(128)S(6)} %select_n.3), kind=kLoop, calls=%fused_computation.1 | loop fusion | bytes 3670020 | tf_op jit(solution)/shard_map/reshape | solution.py:313
  3.5 1.4 collective-permute-start
  5.0 3.1 %late_columns.1 = bf16[16,2,2,56,512]{4,3,2,1,0:T(8,128)(2,1)} custom-call(bf16[16,2,56,512]{3,2,1,0:T(8,128)(2,1)} %dynamic-slice_bitcast_fusion.given, bf16[16,2,2,56,1024]{4,3,2,1,0:T(8,128)(2,1)} %bitcast.20), custom_call_target="tpu_custom_call" | custom-call | tf_op jit(solution)/shard_map/late_columns/pallas_call | solution.py:263
  8.1 8.4 %all-to-all-start.1 = ((bf16[32,112,512]{2,1,0:T(8,128)(2,1)}), bf16[32,112,512]{2,1,0:T(8,128)(2,1)}, u32[]{:S(2)}, u32[]{:S(2)}) async-start(bf16[32,112,512]{2,1,0:T(8,128)(2,1)} %bitcast.30), calls=%async_computation.1 | async-start | bytes 7340032 | tf_op jit(solution)/shard_map/all_to_all | solution.py:226
  16.4 0.1 stack.23.place.place_ref
  16.5 0.0 collective-permute-done.after.swapped
  16.5 3.1 %copy-done = bf16[1,1,3584,1024]{3,2,1,0:T(8,128)(2,1)S(1)} copy-done((bf16[1,1,3584,1024]{3,2,1,0:T(8,128)(2,1)S(1)}, bf16[1,1,3584,1024]{3,2,1,0:T(8,128)(2,1)}, u32[]{:S(2)}) %copy-start) | copy-done | bytes 7340056
  19.6 0.9 early_sums.2.after
  20.5 1.3 collective-permute-start.1
  21.8 0.9 early_sums.3
  22.7 39.3 %collective-permute-done.1 = f32[16,56,512]{2,1,0:T(8,128)S(1)} collective-permute-done((f32[16,56,512]{2,1,0:T(8,128)S(1)}, f32[16,56,512]{2,1,0:T(8,128)S(1)}, u32[]{:S(2)}, u32[]{:S(2)}) %collective-permute-start.1) | collective-permute-done | bytes 1835040 | tf_op jit(solution)/shard_map/ppermute | solution.py:230
  62.0 1.7 add.11
  63.6 0.0 all-to-all-done.1
  63.6 6.5 %all-to-all-start = ((f32[16,56,512]{2,1,0:T(8,128)}), f32[16,56,512]{2,1,0:T(8,128)S(1)}, u32[]{:S(2)}, u32[]{:S(2)}) async-start(f32[16,56,512]{2,1,0:T(8,128)} %add.11), calls=%async_computation | async-start | bytes 3670016 | tf_op jit(solution)/shard_map/all_to_all | solution.py:226
  70.2 0.0 copy-start.1
  70.2 0.0 copy-start.10
  70.2 2.6 %convert_reduce_fusion = f32[112,512]{1,0:T(8,128)S(1)} fusion(bf16[32,112,512]{2,1,0:T(8,128)(2,1)} %all-to-all-done.1), kind=kLoop, calls=%fused_computation | loop fusion | flops 3612672 | bytes 3899392 | tf_op jit(solution)/shard_map/reduce_sum | solution.py:322
  72.8 1.3 collective-permute-start.2
  74.2 4.3 %collective-permute-done.2.late_given = f32[2,56,512]{2,1,0:T(8,128)S(1)} collective-permute-done((f32[2,56,512]{2,1,0:T(8,128)S(1)}, f32[2,56,512]{2,1,0:T(8,128)S(1)}, u32[]{:S(2)}, u32[]{:S(2)}) %collective-permute-start.2) | collective-permute-done | bytes 229408 | tf_op jit(solution)/shard_map/ppermute | solution.py:230
  78.5 1.2 collective-permute-start.3
  79.8 8.4 %collective-permute-done.3 = f32[112,1024]{1,0:T(8,128)S(1)} collective-permute-done((f32[112,1024]{1,0:T(8,128)S(1)}, f32[112,1024]{1,0:T(8,128)S(1)}, u32[]{:S(2)}, u32[]{:S(2)}) %collective-permute-start.3) | collective-permute-done | bytes 458784 | tf_op jit(solution)/shard_map/ppermute | solution.py:230
  88.1 7.0 %all-to-all-done = f32[16,56,512]{2,1,0:T(8,128)S(1)} async-done(((f32[16,56,512]{2,1,0:T(8,128)}), f32[16,56,512]{2,1,0:T(8,128)S(1)}, u32[]{:S(2)}, u32[]{:S(2)}) %all-to-all-start) | async-done | bytes 1835040 | tf_op jit(solution)/shard_map/all_to_all | solution.py:226
  95.2 0.1 reduce_sum.28.early
  95.3 1.3 collective-permute-start.4
  96.6 0.7 fusion
  97.4 1.7 collective-permute-done.4.early_other
  99.0 3.1 %direction_and_gram.1 = (f32[56,1024]{1,0:T(8,128)}, f32[112,1024]{1,0:T(8,128)S(1)}, f32[1280,128]{1,0:T(8,128)S(1)}, f32[1280,128]{1,0:T(8,128)S(1)}) custom-call(s32[5]{0:T(128)S(1)} %stack.23.place.place_ref, f32[56,512]{1,0:T(8,128)S(1)} %reduce_sum.28.early, f32[56,512]{1,0:T(8,128)S(1)} %collective-permute-done.4.early_other, ...), custom_call_target="tpu_custom_call" | custom-call | tf_op jit(solution)/shard_map/direction_and_gram/pallas_call | solution.py:93
  102.1 4.6 %collective-permute-start.5 = (f32[1280,128]{1,0:T(8,128)S(1)}, f32[1280,128]{1,0:T(8,128)S(1)}, u32[]{:S(2)}, u32[]{:S(2)}) collective-permute-start(f32[1280,128]{1,0:T(8,128)S(1)} %get-tuple-element.23), channel_id=1, source_target_pairs={{0,2},{2,0},{1,3},{3,1},{4,6},{6,4},{5,7},{7,5},{8,10},{10,8},{9,1... | collective-permute-start | bytes 1966088 | tf_op jit(solution)/shard_map/ppermute | solution.py:230
  106.7 1.7 collective-permute-done.5
  108.4 0.1 add.12
  108.5 19.7 %all_to_all.30 = f32[32,40,128]{2,1,0:T(8,128)S(1)} all-to-all(f32[32,40,128]{2,1,0:T(8,128)S(1)} %bitcast.33), channel_id=1, replica_groups=mesh['z'=4,'y'=4,'xl'=2,'c'=2,'xh'=2] {'z','y','xh'}, dimensions={0} | all-to-all | bytes 1310720 | tf_op jit(solution)/shard_map/all_to_all | solution.py:226
  128.2 0.1 reduce_sum.29
  128.2 0.1 broadcast_in_dim.4
  128.3 22.3 %all_to_all.31 = f32[64,40,128]{2,1,0:T(8,128)S(1)} all-to-all(f32[64,40,128]{2,1,0:T(8,128)S(1)} %broadcast_in_dim.4), channel_id=1, replica_groups=mesh['z'=4,'y'=4,'xl'=2,'c'=2,'xh'=2] {'xl','z','y','xh'}, dimensions={0} | all-to-all | bytes 2621440 | tf_op jit(solution)/shard_map/all_to_all | solution.py:226
  150.7 3.9 %collective-permute-start.6 = (f32[2560,128]{1,0:T(8,128)S(1)}, f32[2560,128]{1,0:T(8,128)S(1)}, u32[]{:S(2)}, u32[]{:S(2)}) collective-permute-start(f32[2560,128]{1,0:T(8,128)S(1)} %bitcast.31), channel_id=1, source_target_pairs={{0,2},{2,0},{1,3},{3,1},{4,6},{6,4},{5,7},{7,5},{8,10},{10,8},{9,1... | collective-permute-start | bytes 3932168 | tf_op jit(solution)/shard_map/ppermute | solution.py:230
  154.6 2.7 %collective-permute-done.6.other = f32[2560,128]{1,0:T(8,128)S(1)} collective-permute-done((f32[2560,128]{1,0:T(8,128)S(1)}, f32[2560,128]{1,0:T(8,128)S(1)}, u32[]{:S(2)}, u32[]{:S(2)}) %collective-permute-start.6) | collective-permute-done | bytes 1310752 | tf_op jit(solution)/shard_map/ppermute | solution.py:230
  157.2 1.1 copy-done.9
  158.3 26.0 %newton.1 = (f32[56,1024]{1,0:T(8,128)}, f32[56,1024]{1,0:T(8,128)}, bf16[4,2,56,512]{3,2,1,0:T(8,128)(2,1)}, bf16[2,56,512]{2,1,0:T(8,128)(2,1)}) custom-call(s32[5]{0:T(128)} %copy-done.6, f32[2560,128]{1,0:T(8,128)} %bitcast.32, f32[2560,128]{1,0:T(8,128)} %copy-done.9, f32[112,1024]{1,0:T(8,128)} %copy-done.4, f32[56,1024]{1,0:T(8,128)} %bitcast.34, ...), custom_call_target="tpu_custom_call" | custom-call | tf_op jit(solution)/shard_map/newton/pallas_call | solution.py:209
  184.3 3.5 %all-to-all-start.4 = ((bf16[4,2,56,512]{3,2,1,0:T(8,128)(2,1)}), bf16[4,2,56,512]{3,2,1,0:T(8,128)(2,1)S(1)}, u32[]{:S(2)}, u32[]{:S(2)}) async-start(bf16[4,2,56,512]{3,2,1,0:T(8,128)(2,1)} %get-tuple-element.26), calls=%async_computation.4 | async-start | bytes 917504 | tf_op jit(solution)/shard_map/all_to_all | solution.py:226
  187.8 0.5 collective-permute-start.9
  188.3 1.6 collective-permute-start.8
  189.9 0.3 collective-permute-start.7
  190.1 2.3 collective-permute-done.9.refs_3_
  192.4 1.6 collective-permute-done.8.refs_2_
  194.0 3.0 %collective-permute-done.7.refs_1_ = bf16[2,56,512]{2,1,0:T(8,128)(2,1)S(1)} collective-permute-done((bf16[2,56,512]{2,1,0:T(8,128)(2,1)}, bf16[2,56,512]{2,1,0:T(8,128)(2,1)S(1)}, u32[]{:S(2)}, u32[]{:S(2)}) %collective-permute-start.7) | collective-permute-done | bytes 114720 | tf_op jit(solution)/shard_map/ppermute | solution.py:361
  197.0 0.9 copy-done.5
  197.9 0.6 collected.1.refs_0_
  198.5 0.0 all-to-all-done.4
  198.5 1.4 broadcast_in_dim.5
  199.9 3.6 %all-to-all-start.5 = ((bf16[4,4,2,56,512]{4,3,2,1,0:T(8,128)(2,1)}), bf16[4,4,2,56,512]{4,3,2,1,0:T(8,128)(2,1)S(1)}, u32[]{:S(2)}, u32[]{:S(2)}) async-start(bf16[4,4,2,56,512]{4,3,2,1,0:T(8,128)(2,1)} %broadcast_in_dim.5), calls=%async_computation.5 | async-start | bytes 3670016 | tf_op jit(solution)/shard_map/all_to_all | solution.py:226
  203.5 2.5 %collective-permute-start.12 = (bf16[4,2,56,512]{3,2,1,0:T(8,128)(2,1)S(1)}, bf16[4,2,56,512]{3,2,1,0:T(8,128)(2,1)S(1)}, u32[]{:S(2)}, u32[]{:S(2)}) collective-permute-start(bf16[4,2,56,512]{3,2,1,0:T(8,128)(2,1)S(1)} %collected.1.refs_0_), channel_id=1, source_target_pairs={{0,24},{8,0},{16,8},{24,16},{1,25},{9,1},{17,9},{25,17},{2,26},{10... | collective-permute-start | bytes 1376264 | tf_op jit(solution)/shard_map/ppermute | solution.py:361
  206.0 0.6 collective-permute-start.11
  206.6 0.6 collective-permute-start.10
  207.2 7.9 %collective-permute-done.12.refs_3_ = bf16[4,2,56,512]{3,2,1,0:T(8,128)(2,1)S(1)} collective-permute-done((bf16[4,2,56,512]{3,2,1,0:T(8,128)(2,1)S(1)}, bf16[4,2,56,512]{3,2,1,0:T(8,128)(2,1)S(1)}, u32[]{:S(2)}, u32[]{:S(2)}) %collective-permute-start.12) | collective-permute-done | bytes 458784 | tf_op jit(solution)/shard_map/ppermute | solution.py:361
  215.1 3.0 %collective-permute-done.11.refs_2_ = bf16[4,2,56,512]{3,2,1,0:T(8,128)(2,1)S(1)} collective-permute-done((bf16[4,2,56,512]{3,2,1,0:T(8,128)(2,1)S(1)}, bf16[4,2,56,512]{3,2,1,0:T(8,128)(2,1)S(1)}, u32[]{:S(2)}, u32[]{:S(2)}) %collective-permute-start.11) | collective-permute-done | bytes 458784 | tf_op jit(solution)/shard_map/ppermute | solution.py:361
  218.1 11.7 %collective-permute-done.10.refs_1_ = bf16[4,2,56,512]{3,2,1,0:T(8,128)(2,1)S(1)} collective-permute-done((bf16[4,2,56,512]{3,2,1,0:T(8,128)(2,1)S(1)}, bf16[4,2,56,512]{3,2,1,0:T(8,128)(2,1)S(1)}, u32[]{:S(2)}, u32[]{:S(2)}) %collective-permute-start.10) | collective-permute-done | bytes 458784 | tf_op jit(solution)/shard_map/ppermute | solution.py:361
  229.8 0.8 copy-done.2
  230.6 0.0 all-to-all-done.5.left
  230.6 1.0 copy-done.3
  231.6 0.8 joined.1
  232.4 0.6 collective-permute-start.13
  233.0 2.4 placed.2.refs_0_
  235.4 3.6 %collective-permute-done.13.piece = bf16[32,56,1024]{2,1,0:T(8,128)(2,1)S(1)} collective-permute-done((bf16[32,56,1024]{2,1,0:T(8,128)(2,1)S(1)}, bf16[32,56,1024]{2,1,0:T(8,128)(2,1)S(1)}, u32[]{:S(2)}, u32[]{:S(2)}) %collective-permute-start.13) | collective-permute-done | bytes 3670048 | tf_op jit(solution)/shard_map/ppermute | solution.py:230
  239.1 2.4 placed.3
  (16 shorter events, 0.1 us)
Async XLA Ops:
  3.5 13.0 %collective-permute-start = (bf16[16,2,56,512]{3,2,1,0:T(8,128)(2,1)}, bf16[16,2,56,512]{3,2,1,0:T(8,128)(2,1)S(1)}, u32[]{:S(2)}, u32[]{:S(2)}) collective-permute-start(bf16[16,2,56,512]{3,2,1,0:T(8,128)(2,1)} %dynamic-slice_bitcast_fusion.given), channel_id=1, source_target_pairs={{0,2},{2,0},{1,3},{3,1},{4,6},{6,4},{5,7},{7,5},{8,10},{10,8},{9,1... | collective-permute-start | bytes 5505032 | tf_op jit(solution)/shard_map/ppermute | solution.py:230
  8.1 55.6 %all-to-all-start.1 = ((bf16[32,112,512]{2,1,0:T(8,128)(2,1)}), bf16[32,112,512]{2,1,0:T(8,128)(2,1)}, u32[]{:S(2)}, u32[]{:S(2)}) async-start(bf16[32,112,512]{2,1,0:T(8,128)(2,1)} %bitcast.30), calls=%async_computation.1 | async-start | bytes 7340032 | tf_op jit(solution)/shard_map/all_to_all | solution.py:226
  16.5 82.5 %copy-start.6 = (s32[5]{0:T(128)}, s32[5]{0:T(128)S(1)}, u32[]{:S(2)}) copy-start(s32[5]{0:T(128)S(1)} %stack.23.place.place_ref) | copy-start | bytes 64
  16.5 3.1 %copy-start = (bf16[1,1,3584,1024]{3,2,1,0:T(8,128)(2,1)S(1)}, bf16[1,1,3584,1024]{3,2,1,0:T(8,128)(2,1)}, u32[]{:S(2)}) copy-start(bf16[1,1,3584,1024]{3,2,1,0:T(8,128)(2,1)} %param.3) | copy-start | bytes 22020100
  20.5 41.5 %collective-permute-start.1 = (f32[16,56,512]{2,1,0:T(8,128)S(1)}, f32[16,56,512]{2,1,0:T(8,128)S(1)}, u32[]{:S(2)}, u32[]{:S(2)}) collective-permute-start(f32[16,56,512]{2,1,0:T(8,128)S(1)} %early_sums.2.after), channel_id=1, source_target_pairs={{0,4},{4,0},{1,5},{5,1},{2,6},{6,2},{3,7},{7,3},{8,12},{12,8},{9,1... | collective-permute-start | bytes 5505032 | tf_op jit(solution)/shard_map/ppermute | solution.py:230
  63.6 31.6 %all-to-all-start = ((f32[16,56,512]{2,1,0:T(8,128)}), f32[16,56,512]{2,1,0:T(8,128)S(1)}, u32[]{:S(2)}, u32[]{:S(2)}) async-start(f32[16,56,512]{2,1,0:T(8,128)} %add.11), calls=%async_computation | async-start | bytes 3670016 | tf_op jit(solution)/shard_map/all_to_all | solution.py:226
  70.2 4.0 %copy-start.1 = (f32[1,1,56,1024]{3,2,1,0:T(8,128)S(1)}, f32[1,1,56,1024]{3,2,1,0:T(8,128)}, u32[]{:S(2)}) copy-start(f32[1,1,56,1024]{3,2,1,0:T(8,128)} %param.5) | copy-start | bytes 688132
  70.2 4.0 %copy-start.10 = (f32[1,1,56,1024]{3,2,1,0:T(8,128)S(1)}, f32[1,1,56,1024]{3,2,1,0:T(8,128)}, u32[]{:S(2)}) copy-start(f32[1,1,56,1024]{3,2,1,0:T(8,128)} %param.4) | copy-start | bytes 688132
  72.8 5.7 %collective-permute-start.2 = (f32[2,56,512]{2,1,0:T(8,128)S(1)}, f32[2,56,512]{2,1,0:T(8,128)S(1)}, u32[]{:S(2)}, u32[]{:S(2)}) collective-permute-start(f32[2,56,512]{2,1,0:T(8,128)S(1)} %bitcast.27), channel_id=1, source_target_pairs={{0,4},{4,0},{1,5},{5,1},{2,6},{6,2},{3,7},{7,3},{8,12},{12,8},{9,1... | collective-permute-start | bytes 688136 | tf_op jit(solution)/shard_map/ppermute | solution.py:230
  78.5 9.6 %collective-permute-start.3 = (f32[112,1024]{1,0:T(8,128)S(1)}, f32[112,1024]{1,0:T(8,128)S(1)}, u32[]{:S(2)}, u32[]{:S(2)}) collective-permute-start(f32[112,1024]{1,0:T(8,128)S(1)} %pad_maximum_fusion), channel_id=1, source_target_pairs={{0,4},{4,0},{1,5},{5,1},{2,6},{6,2},{3,7},{7,3},{8,12},{12,8},{9,1... | collective-permute-start | bytes 1376264 | tf_op jit(solution)/shard_map/ppermute | solution.py:230
  95.3 3.7 %collective-permute-start.4 = (f32[56,512]{1,0:T(8,128)S(1)}, f32[56,512]{1,0:T(8,128)S(1)}, u32[]{:S(2)}, u32[]{:S(2)}) collective-permute-start(f32[56,512]{1,0:T(8,128)S(1)} %reduce_sum.28.early), channel_id=1, source_target_pairs={{0,4},{4,0},{1,5},{5,1},{2,6},{6,2},{3,7},{7,3},{8,12},{12,8},{9,1... | collective-permute-start | bytes 344072 | tf_op jit(solution)/shard_map/ppermute | solution.py:230
  102.1 6.4 %copy-start.4 = (f32[112,1024]{1,0:T(8,128)}, f32[112,1024]{1,0:T(8,128)S(1)}, u32[]{:S(2)}) copy-start(f32[112,1024]{1,0:T(8,128)S(1)} %get-tuple-element.24.direction) | copy-start | bytes 1376260
  102.1 6.3 %collective-permute-start.5 = (f32[1280,128]{1,0:T(8,128)S(1)}, f32[1280,128]{1,0:T(8,128)S(1)}, u32[]{:S(2)}, u32[]{:S(2)}) collective-permute-start(f32[1280,128]{1,0:T(8,128)S(1)} %get-tuple-element.23), channel_id=1, source_target_pairs={{0,2},{2,0},{1,3},{3,1},{4,6},{6,4},{5,7},{7,5},{8,10},{10,8},{9,1... | collective-permute-start | bytes 1966088 | tf_op jit(solution)/shard_map/ppermute | solution.py:230
  150.7 6.6 %copy-start.8 = (f32[64,40,128]{2,1,0:T(8,128)}, f32[64,40,128]{2,1,0:T(8,128)S(1)}, u32[]{:S(2)}) copy-start(f32[64,40,128]{2,1,0:T(8,128)S(1)} %all_to_all.31) | copy-start | bytes 3932164
  150.7 6.6 %collective-permute-start.6 = (f32[2560,128]{1,0:T(8,128)S(1)}, f32[2560,128]{1,0:T(8,128)S(1)}, u32[]{:S(2)}, u32[]{:S(2)}) collective-permute-start(f32[2560,128]{1,0:T(8,128)S(1)} %bitcast.31), channel_id=1, source_target_pairs={{0,2},{2,0},{1,3},{3,1},{4,6},{6,4},{5,7},{7,5},{8,10},{10,8},{9,1... | collective-permute-start | bytes 3932168 | tf_op jit(solution)/shard_map/ppermute | solution.py:230
  157.2 1.1 copy-start.9
  158.3 38.7 %copy-start.7 = (s32[5]{0:T(128)S(1)}, s32[5]{0:T(128)}, u32[]{:S(2)}) copy-start(s32[5]{0:T(128)} %copy-done.6) | copy-start | bytes 64
  184.3 14.2 %all-to-all-start.4 = ((bf16[4,2,56,512]{3,2,1,0:T(8,128)(2,1)}), bf16[4,2,56,512]{3,2,1,0:T(8,128)(2,1)S(1)}, u32[]{:S(2)}, u32[]{:S(2)}) async-start(bf16[4,2,56,512]{3,2,1,0:T(8,128)(2,1)} %get-tuple-element.26), calls=%async_computation.4 | async-start | bytes 917504 | tf_op jit(solution)/shard_map/all_to_all | solution.py:226
  187.8 4.6 %collective-permute-start.9 = (bf16[2,56,512]{2,1,0:T(8,128)(2,1)}, bf16[2,56,512]{2,1,0:T(8,128)(2,1)S(1)}, u32[]{:S(2)}, u32[]{:S(2)}) collective-permute-start(bf16[2,56,512]{2,1,0:T(8,128)(2,1)} %get-tuple-element.25.refs_0_), channel_id=1, source_target_pairs={{0,96},{32,0},{64,32},{96,64},{1,97},{33,1},{65,33},{97,65},{2,98}... | collective-permute-start | bytes 344072 | tf_op jit(solution)/shard_map/ppermute | solution.py:361
  188.3 5.8 %collective-permute-start.8 = (bf16[2,56,512]{2,1,0:T(8,128)(2,1)}, bf16[2,56,512]{2,1,0:T(8,128)(2,1)S(1)}, u32[]{:S(2)}, u32[]{:S(2)}) collective-permute-start(bf16[2,56,512]{2,1,0:T(8,128)(2,1)} %get-tuple-element.25.refs_0_), channel_id=1, source_target_pairs={{0,64},{32,96},{64,0},{96,32},{1,65},{33,97},{65,1},{97,33},{2,66}... | collective-permute-start | bytes 344072 | tf_op jit(solution)/shard_map/ppermute | solution.py:361
  189.9 7.1 %collective-permute-start.7 = (bf16[2,56,512]{2,1,0:T(8,128)(2,1)}, bf16[2,56,512]{2,1,0:T(8,128)(2,1)S(1)}, u32[]{:S(2)}, u32[]{:S(2)}) collective-permute-start(bf16[2,56,512]{2,1,0:T(8,128)(2,1)} %get-tuple-element.25.refs_0_), channel_id=1, source_target_pairs={{0,32},{32,64},{64,96},{96,0},{1,33},{33,65},{65,97},{97,1},{2,34}... | collective-permute-start | bytes 344072 | tf_op jit(solution)/shard_map/ppermute | solution.py:361
  197.0 0.9 copy-start.5
  199.9 30.6 %all-to-all-start.5 = ((bf16[4,4,2,56,512]{4,3,2,1,0:T(8,128)(2,1)}), bf16[4,4,2,56,512]{4,3,2,1,0:T(8,128)(2,1)S(1)}, u32[]{:S(2)}, u32[]{:S(2)}) async-start(bf16[4,4,2,56,512]{4,3,2,1,0:T(8,128)(2,1)} %broadcast_in_dim.5), calls=%async_computation.5 | async-start | bytes 3670016 | tf_op jit(solution)/shard_map/all_to_all | solution.py:226
  203.5 11.6 %collective-permute-start.12 = (bf16[4,2,56,512]{3,2,1,0:T(8,128)(2,1)S(1)}, bf16[4,2,56,512]{3,2,1,0:T(8,128)(2,1)S(1)}, u32[]{:S(2)}, u32[]{:S(2)}) collective-permute-start(bf16[4,2,56,512]{3,2,1,0:T(8,128)(2,1)S(1)} %collected.1.refs_0_), channel_id=1, source_target_pairs={{0,24},{8,0},{16,8},{24,16},{1,25},{9,1},{17,9},{25,17},{2,26},{10... | collective-permute-start | bytes 1376264 | tf_op jit(solution)/shard_map/ppermute | solution.py:361
  206.0 12.1 %collective-permute-start.11 = (bf16[4,2,56,512]{3,2,1,0:T(8,128)(2,1)S(1)}, bf16[4,2,56,512]{3,2,1,0:T(8,128)(2,1)S(1)}, u32[]{:S(2)}, u32[]{:S(2)}) collective-permute-start(bf16[4,2,56,512]{3,2,1,0:T(8,128)(2,1)S(1)} %collected.1.refs_0_), channel_id=1, source_target_pairs={{0,16},{8,24},{16,0},{24,8},{1,17},{9,25},{17,1},{25,9},{2,18},{10... | collective-permute-start | bytes 1376264 | tf_op jit(solution)/shard_map/ppermute | solution.py:361
  206.6 23.2 %collective-permute-start.10 = (bf16[4,2,56,512]{3,2,1,0:T(8,128)(2,1)S(1)}, bf16[4,2,56,512]{3,2,1,0:T(8,128)(2,1)S(1)}, u32[]{:S(2)}, u32[]{:S(2)}) collective-permute-start(bf16[4,2,56,512]{3,2,1,0:T(8,128)(2,1)S(1)} %collected.1.refs_0_), channel_id=1, source_target_pairs={{0,8},{8,16},{16,24},{24,0},{1,9},{9,17},{17,25},{25,1},{2,10},{10... | collective-permute-start | bytes 1376264 | tf_op jit(solution)/shard_map/ppermute | solution.py:361
  229.8 0.8 copy-start.2
  230.6 1.0 copy-start.3
  232.4 6.6 %collective-permute-start.13 = (bf16[32,56,1024]{2,1,0:T(8,128)(2,1)S(1)}, bf16[32,56,1024]{2,1,0:T(8,128)(2,1)S(1)}, u32[]{:S(2)}, u32[]{:S(2)}) collective-permute-start(bf16[32,56,1024]{2,1,0:T(8,128)(2,1)S(1)} %bitcast.23), channel_id=1, source_target_pairs={{0,2},{2,0},{1,3},{3,1},{4,6},{6,4},{5,7},{7,5},{8,10},{10,8},{9,1... | collective-permute-start | bytes 11010056 | tf_op jit(solution)/shard_map/ppermute | solution.py:230
